TPU v7x, 1024 devices: a whole 4x4x32 slice. The times are simulated.
1024 devices in a mesh: row: 32 (over z), col: 32 (over y, x, core).
Axes of the slice: x: 4, y: 4, z: 32, core: 2. Of those that a mesh axis runs over, the one named last changes fastest.
Arguments:
- density: bfloat16 [32768, 32768], P('row', 'col'), as said below
- occupancy: int32 [256, 256], P('row', 'col'), may hold values from 0 to 1, as said below
- product_keep: int32 [4, 256], replicated, may hold values 0 or 1
Outputs:
- purified: bfloat16 [512, 32768], P('row', 'col')
Inputs may be any that keep to these rules, and one draw needn't show every extreme that they name: density is symmetric. occupancy is symmetric and every diagonal block is stored.
All inputs are finite; a program needn't handle non-finite values.
Results may differ from a plain program's by a relative error of at most 0.015.
Values may be sent and summed in bfloat16 or wider, within the bound.
No kernel may reach another device: no remote copies, remote signals or barrier semaphores. Data moves between devices by JAX's collectives and lax.ppermute only.
A program may use at most 32 MiB of HBM per device.

v0:
```python
import jax
import jax.numpy as jnp
from jax import lax
from jax.sharding import PartitionSpec as P

BS = 128


def broadcast(block, axis, source):
    block = jnp.where(lax.axis_index(axis) == source, block, jnp.zeros_like(block))
    return lax.psum(block, axis)


def body(density, occupancy, product_keep):
    rows_here, cols_here = density.shape
    row_index = lax.axis_index("row")
    col_index = lax.axis_index("col")
    row_count = lax.axis_size("row")
    window_len = product_keep.shape[0] * BS
    occupied = jnp.repeat(jnp.repeat(occupancy, BS, axis=0), BS, axis=1).astype(jnp.bfloat16)
    dense_block = density * occupied
    window_panel = broadcast(dense_block[:window_len], "row", 0)
    keep_rows = jnp.repeat(product_keep, BS, axis=0)
    blocks_down = rows_here // BS
    blocks_across = cols_here // BS
    keep_square = lax.dynamic_slice_in_dim(keep_rows, row_index * blocks_down, blocks_down, 1)
    lefts = window_panel
    summed = lax.psum(
        lax.dot_general(
            lefts, dense_block, (((1,), (1,)), ((), ())), preferred_element_type=jnp.float32
        ).astype(jnp.bfloat16),
        "col",
    ).astype(jnp.float32)
    square_mask = jnp.repeat(keep_square, BS, axis=1).astype(jnp.float32)
    square = (summed * square_mask).astype(jnp.bfloat16)
    offset = col_index * cols_here - row_index * rows_here
    source = jnp.arange(cols_here, dtype=jnp.int32) + offset
    inside = ((source >= 0) & (source < rows_here)).astype(jnp.float32)
    picked = jnp.clip(source, 0, rows_here - 1)
    out_rows = window_len // row_count
    lefts = square
    product = jnp.dot(lefts, dense_block, preferred_element_type=jnp.float32)
    diagonal_part = jnp.take(lefts, picked, axis=1).astype(jnp.float32) * inside[None, :]
    result = lax.psum_scatter(
        3.0 * diagonal_part - 2.0 * product, "row", scatter_dimension=0, tiled=True
    )
    keep_out = lax.dynamic_slice_in_dim(keep_rows, row_index * out_rows, out_rows, 0)
    keep_out = lax.dynamic_slice_in_dim(keep_out, col_index * blocks_across, blocks_across, 1)
    out_mask = jnp.repeat(keep_out, BS, axis=1).astype(jnp.float32)
    return (result * out_mask).astype(jnp.bfloat16)


def solution(mesh):
    return jax.shard_map(
        body,
        mesh=mesh,
        in_specs=(P("row", "col"), P("row", "col"), P()),
        out_specs=P("row", "col"),
        check_vma=False,
    )
```

profile of v0, /device:TPU:6, one launch (start us, length us, event | category | flops | bytes accessed | tf_op | source)
XLA Modules:
  0.0 617.7 jit_solution(8071955343175203365)
XLA Ops:
  6.5 0.0 all-reduce.3.cloned.1.call-start
  6.5 0.7 convert_element_type.47
  7.2 0.0 copy-start.1
  7.3 2.9 broadcast_in_dim.31
  10.2 0.0 copy-done.1
  10.2 0.3 bitcast_multiply_fusion.1
  10.5 1.0 slice_select_fusion
  11.6 0.0 all-reduce.3.cloned.1.call-update
  11.6 0.0 all-reduce.5.cloned.1.call-start
  11.6 0.0 copy-start.4
  11.7 273.5 %all-reduce.3.cloned.1.call-done = bf16[512,1024]{1,0:T(8,128)(2,1)} async-done(((bf16[512,1024]{1,0:T(8,128)(2,1)}), bf16[512,1024]{1,0:T(8,128)(2,1)}) %all-reduce.3.cloned.1.call-update) | async-done | bytes 1048592 | tf_op jit(solution)/shard_map/psum | solution.py:11
  285.1 3.5 convolution_convert_fusion
  288.6 0.0 all-reduce.5.cloned.1.call-update
  288.6 0.0 reduce-scatter.2.cloned.1.call-start
  288.7 0.0 copy-done.4
  288.8 0.0 copy-start.2
  288.8 0.8 copy-done.2
  289.6 0.1 dynamic-slice_convert_fusion
  289.7 168.2 %all-reduce.5.cloned.1.call-done = bf16[512,1024]{1,0:T(8,128)(2,1)} async-done(((bf16[512,1024]{1,0:T(8,128)(2,1)}), bf16[512,1024]{1,0:T(8,128)(2,1)}) %all-reduce.5.cloned.1.call-update) | async-done | bytes 1048592 | tf_op jit(solution)/shard_map/psum | solution.py:28
  457.9 0.0 copy-start.3
  457.9 0.6 broadcast_in_dim.34
  458.5 0.6 copy-done.3
  459.1 1.5 fusion
  460.7 1.5 copy.6
  462.2 5.1 gather_fusion
  467.3 0.0 copy-start
  467.3 2.4 copy.7
  469.6 0.0 copy-done
  469.6 3.9 bitcast_subtract_fusion
  473.5 0.0 reduce-scatter.2.cloned.1.call-update
  473.6 0.8 dynamic-slice_convert_fusion.1
  474.4 135.2 %reduce-scatter.2.cloned.1.call-done = f32[16,1024]{1,0:T(8,128)} async-done(((f32[512,1024]{1,0:T(8,128)}), f32[16,1024]{1,0:T(8,128)}) %reduce-scatter.2.cloned.1.call-update) | async-done | bytes 65552 | tf_op jit(solution)/shard_map/reduce_scatter | solution.py:44
  609.6 0.1 broadcast_in_dim.36
  609.7 1.5 fusion.1
  (5 shorter events, 0.1 us)
Async XLA Ops:
  6.5 278.6 %all-reduce.3.cloned.1.call-start = ((), (), s32[]{:S(2)}) async-start(), calls=%async_computation.1 | async-start | bytes 2097152 | tf_op jit(solution)/shard_map/psum | solution.py:11
  7.2 3.0 copy-start.1
  11.6 446.3 %all-reduce.5.cloned.1.call-start = ((), (), s32[]{:S(2)}) async-start(), calls=%async_computation.2 | async-start | bytes 2097152 | tf_op jit(solution)/shard_map/psum | solution.py:28
  11.6 277.1 %copy-start.4 = (s32[4,256]{1,0:T(4,128)S(1)}, s32[4,256]{1,0:T(4,128)}, u32[]{:S(2)}) copy-start(s32[4,256]{1,0:T(4,128)} %param.5) | copy-start | bytes 12292
  288.6 321.0 %reduce-scatter.2.cloned.1.call-start = ((), (), s32[]{:S(2)}) async-start(), calls=%async_computation.3 | async-start | bytes 2162688 | tf_op jit(solution)/shard_map/reduce_scatter | solution.py:44
  288.8 0.8 copy-start.2
  457.9 1.2 copy-start.3
  467.3 2.4 copy-start
Sparse Core Ops, SparseCore 0:
  11.7 273.3 all-reduce.2
  288.7 169.1 all-reduce.4
  473.7 135.9 reduce-scatter.1
where the time goes:
time: 618 us
  waiting for transfers between devices  577 us (93%)
  local copies, waits for them, and re-layouts  14.1 us (2%)
  between operations  13.2 us (2%)
  matrix products  7.37 us (1%)
    psum x1, waiting for transfers between devices, broadcast(): return lax.psum(block, axis)  273 us
    psum x1, waiting for transfers between devices, body(): lax.psum(lax.dot_general(lefts, dense_block, (((1,), (1,)), ((), ())), pr...  168 us
    reduce_scatter x1, waiting for transfers between devices, body(): lax.psum_scatter(3.0 * diagonal_part - 2.0 * product, 'row', scatter_dime...  135 us
  transfers between devices with their start and end apart: 3, of which 3 were waited for; matrix products, arithmetic and copies ran while one was open for 0% of the time, Pallas kernels for 0%

commit v1 on v0

v1 whole, which is shorter than its diff:
```python
import functools

import jax
import jax.numpy as jnp
from jax import lax
from jax.experimental import pallas as pl
from jax.experimental.pallas import tpu as pltpu
from jax.sharding import PartitionSpec as P

BS = 128
BF16 = jnp.bfloat16
F32 = jnp.float32
VMEM = pl.BlockSpec(memory_space=pltpu.VMEM)
SMEM = pl.BlockSpec(memory_space=pltpu.SMEM)
BOTH = ("row", "col")


def call(kernel, outs, cost, scratch=()):
    return functools.partial(
        pl.pallas_call,
        kernel,
        out_shape=outs,
        out_specs=jax.tree.map(lambda _: VMEM, outs),
        scratch_shapes=list(scratch),
        compiler_params=pltpu.CompilerParams(vmem_limit_bytes=24 * 2**20),
        cost_estimate=pl.CostEstimate(flops=cost, bytes_accessed=4 * 2**20, transcendentals=0),
    )


def mask_kernel(where_ref, occ_ref, density_ref, sparse_ref, panel_ref):
    down, across = occ_ref.shape
    window = panel_ref.shape[0] // BS
    first = where_ref[0] == 0
    for i in range(down):
        for j in range(across):
            spot = (pl.ds(i * BS, BS), pl.ds(j * BS, BS))
            kept = density_ref[spot] * occ_ref[i, j].astype(F32).astype(BF16)
            sparse_ref[spot] = kept
            if i < window:
                panel_ref[spot] = jnp.where(first, kept, jnp.zeros_like(kept))


def square_kernel(where_ref, low_ref, high_ref, sparse_ref, kept_ref, sent_ref):
    core = where_ref[1] % 2
    tile = min(256, sparse_ref.shape[0])
    for n in range(0, sparse_ref.shape[0], tile):
        right = sparse_ref[pl.ds(n, tile), :]

        def product(left):
            return lax.dot_general(left, right, (((1,), (1,)), ((), ())), preferred_element_type=F32)

        low, high = product(low_ref[...]), product(high_ref[...])
        kept_ref[:, pl.ds(n, tile)] = jnp.where(core == 0, low, high)
        sent_ref[:, pl.ds(n, tile)] = jnp.where(core == 0, high, low).astype(BF16)


def cube_kernel(rows, where_ref, mine_ref, other_ref, sparse_ref, kept_ref, sent_ref, left_ref):
    row, col = where_ref[0], where_ref[1]
    core = col % 2
    sign = 1 - 2 * core
    piece = left_ref.shape[0] // rows
    half = rows // 2
    order = [t for start in (0, 2, 1, 3) for t in range(start, rows, 4)]
    for place, t in enumerate(order):
        target = (row + sign * t + rows) % rows
        source = pl.ds(pl.multiple_of((target % half) * piece, piece), piece)
        spot = pl.ds(place * piece, piece)

        @pl.when(target // half == core)
        def _():
            left_ref[spot, :] = mine_ref[source, :]

        @pl.when(target // half != core)
        def _():
            left_ref[spot, :] = other_ref[source, :]

    three = jnp.where(row == col, 3.0, 0.0).astype(F32)
    tile = min(256, sparse_ref.shape[1])
    middle = left_ref.shape[0] // 2
    for n in range(0, sparse_ref.shape[1], tile):
        spot = pl.ds(n, tile)
        product = jnp.dot(left_ref[...], sparse_ref[:, spot], preferred_element_type=F32)
        total = three * left_ref[:, spot].astype(F32) - 2.0 * product
        kept_ref[:, spot] = total[:middle]
        sent_ref[:, spot] = total[middle:].astype(BF16)


def order_kernel(groups, where_ref, kept_ref, got_ref, out_ref):
    row, col = where_ref[0], where_ref[1]
    sign = 1 - 2 * (col % 2)
    piece = out_ref.shape[0] // groups
    for u in range(groups):
        place = (row // 4 + sign * u + groups) % groups
        source = pl.ds(u * piece, piece)
        total = kept_ref[source, :] + got_ref[source, :].astype(F32)
        out_ref[pl.ds(pl.multiple_of(place * piece, piece), piece), :] = total.astype(BF16)


def body(rows, cols, density, occupancy, product_keep):
    rows_here, cols_here = density.shape
    window = product_keep.shape[0] * BS
    row, col = lax.axis_index("row"), lax.axis_index("col")
    where = jnp.stack([row, col]).astype(jnp.int32)
    half = window // 2
    piece = window // rows
    chips = cols // 2
    tall = jax.ShapeDtypeStruct

    def pairs(step, every):
        return [
            (z * cols + c, ((z + (step if c % 2 == 0 else -step)) % rows) * cols + c)
            for z in range(0, rows, every)
            for c in range(cols)
        ]

    swap = [(c, c ^ 1) for c in range(cols)]
    same_core = [[2 * i + k for i in range(chips)] for k in range(2)]
    groups = rows // 4
    strided = [[4 * i + o for i in range(groups)] for o in range(4)]

    def mask(across, down_first, across_first):
        kept = lax.dynamic_slice(product_keep, (down_first, across_first), (1, across))
        return jnp.repeat(kept, BS, axis=1).astype(F32)

    sparse, panel = call(
        mask_kernel, (tall(density.shape, BF16), tall((window, cols_here), BF16)), 10**6
    )(in_specs=[SMEM, SMEM, VMEM])(where, occupancy, density)

    halves = [panel[:half], panel[half:]]
    step = rows // 2
    while step:
        halves = [h + lax.ppermute(h, BOTH, pairs(step, 2 * step)) for h in halves]
        step //= 2

    kept, sent = call(
        square_kernel, (tall((half, rows_here), F32), tall((half, rows_here), BF16)), 2 * window * rows_here * cols_here
    )(in_specs=[SMEM, VMEM, VMEM, VMEM])(where, *halves, sparse)
    kept = (kept + lax.ppermute(sent, "col", swap).astype(F32)).astype(BF16)
    parts = lax.all_to_all(kept.reshape(chips, piece, rows_here), "col", 0, 0, axis_index_groups=same_core, tiled=True)
    first = (col % 2) * half + (col // 2) * piece
    square = parts.astype(F32).sum(0) * mask(rows_here // BS, first // BS, row * (rows_here // BS))
    square = jnp.broadcast_to(square.astype(BF16), (chips, piece, rows_here))
    mine = lax.all_to_all(square, "col", 0, 0, axis_index_groups=same_core, tiled=True).reshape(half, rows_here)
    other = lax.ppermute(mine, "col", swap)

    kept, sent = call(
        functools.partial(cube_kernel, rows),
        (tall((half, cols_here), F32), tall((half, cols_here), BF16)),
        2 * window * rows_here * cols_here,
        [pltpu.VMEM((window, rows_here), BF16)],
    )(in_specs=[SMEM, VMEM, VMEM, VMEM])(where, mine, other, sparse)
    kept = kept + lax.ppermute(sent, BOTH, pairs(1, 1)).astype(F32)
    quarter = half // 2
    got = lax.ppermute(kept[quarter:].astype(BF16), BOTH, pairs(2, 1))
    ready = call(functools.partial(order_kernel, groups), tall((quarter, cols_here), BF16), 10**6)(
        in_specs=[SMEM, VMEM, VMEM]
    )(where, kept[:quarter], got)
    parts = lax.all_to_all(ready.reshape(groups, piece, cols_here), "row", 0, 0, axis_index_groups=strided, tiled=True)
    result = parts.astype(F32).sum(0)
    result = result * mask(cols_here // BS, row * piece // BS, col * (cols_here // BS))
    return result.astype(BF16)


def solution(mesh):
    rows, cols = mesh.shape["row"], mesh.shape["col"]
    return jax.shard_map(
        functools.partial(body, rows, cols),
        mesh=mesh,
        in_specs=(P("row", "col"), P("row", "col"), P()),
        out_specs=P("row", "col"),
        check_vma=False,
    )
```

time: 618 us -> 235 us (0.38)
  waiting for transfers between devices: 577 us -> 128 us
  starting transfers between devices: 0.09 us -> 77.6 us
  blocking collectives: 0 us -> 14 us
  between operations: 13.2 us -> 0.27 us
  local copies, waits for them, and re-layouts: 14.1 us -> 2.61 us
  matrix products: 7.37 us -> 0 us
  Pallas kernels: 0 us -> 7.06 us
    psum x2 -> x0, waiting for transfers between devices: 442 us -> none  [the longest x1 273 us: broadcast(): return lax.psum(block, axis)]
    reduce_scatter x1 -> x0, waiting for transfers between devices: 135 us -> none  [body(): lax.psum_scatter(3.0 * diagonal_part - 2.0 * product, 'row', scatter_dime...]
    ppermute x0 -> x14, waiting for transfers between devices: none -> 80.9 us  [the longest x10 56.3 us: body(): halves = [h + lax.ppermute(h, BOTH, pairs(step, 2 * step)) for h in halves]]
    ppermute x0 -> x14, starting transfers between devices: none -> 59.6 us  [the longest x10 40.9 us: body(): halves = [h + lax.ppermute(h, BOTH, pairs(step, 2 * step)) for h in halves]]
    all_to_all x0 -> x2, waiting for transfers between devices: none -> 46.7 us  [the longest x1 38.4 us: body(): lax.all_to_all(ready.reshape(groups, piece, cols_here), 'row', 0, 0, axis...]
    all_to_all x0 -> x2, starting transfers between devices: none -> 18 us  [the longest x1 10.6 us: body(): lax.all_to_all(ready.reshape(groups, piece, cols_here), 'row', 0, 0, axis...]
    all_to_all x0 -> x1, blocking collectives: none -> 14 us  [body(): lax.all_to_all(square, 'col', 0, 0, axis_index_groups=same_core, tiled=True)]
    gather x2 -> x0, local copies, waits for them, and re-layouts: 7.47 us -> none  [body(): jnp.take(lefts, picked, axis=1).astype(jnp.float32) * inside[None, :]]
  transfers between devices with their start and end apart: 3 -> 16, of which waited for: 3 -> 16; matrix products, arithmetic and copies ran while one was open for 0% -> 1% of each run, Pallas kernels for 0% -> 0%
where the time goes in v1:
time: 235 us; the launch traced here: 234 us
  waiting for transfers between devices  128 us (54%)
  starting transfers between devices  77.6 us (33%)
  blocking collectives  14 us (6%)
  Pallas kernels  7.06 us (3%)
  other arithmetic  4.47 us (2%)
  local copies, waits for them, and re-layouts  2.61 us (1%)
    ppermute x10, waiting for transfers between devices, body(): halves = [h + lax.ppermute(h, BOTH, pairs(step, 2 * step)) for h in halves]  56.3 us
    ppermute x10, starting transfers between devices, body(): halves = [h + lax.ppermute(h, BOTH, pairs(step, 2 * step)) for h in halves]  40.9 us
    all_to_all x1, waiting for transfers between devices, body(): lax.all_to_all(ready.reshape(groups, piece, cols_here), 'row', 0, 0, axis...  38.4 us
    all_to_all x1, blocking collectives, body(): lax.all_to_all(square, 'col', 0, 0, axis_index_groups=same_core, tiled=True)  14 us
    ppermute x1, starting transfers between devices, body(): kept = kept + lax.ppermute(sent, BOTH, pairs(1, 1)).astype(F32)  13 us
    ppermute x1, waiting for transfers between devices, body(): kept = kept + lax.ppermute(sent, BOTH, pairs(1, 1)).astype(F32)  11.8 us
    all_to_all x1, starting transfers between devices, body(): lax.all_to_all(ready.reshape(groups, piece, cols_here), 'row', 0, 0, axis...  10.6 us
    ppermute x1, waiting for transfers between devices, body(): got = lax.ppermute(kept[quarter:].astype(BF16), BOTH, pairs(2, 1))  9.09 us
  transfers between devices with their start and end apart: 16, of which 16 were waited for; matrix products, arithmetic and copies ran while one was open for 1% of the time, Pallas kernels for 0%

profile of v1, /device:TPU:6, one launch (start us, length us, event | category | flops | bytes accessed | tf_op | source)
XLA Modules:
  0.0 233.7 jit_solution(8237059248493856914)
XLA Ops:
  0.0 0.1 pad_add_fusion.where_ref
  0.1 0.0 copy-start
  0.1 1.6 copy-done
  1.7 0.0 copy-start.1
  1.7 0.7 copy-done.1
  2.4 1.4 shard_map.37
  3.7 0.1 fusion
  3.8 29.0 %collective-permute-start = (bf16[256,1024]{1,0:T(8,128)(2,1)S(1)}, bf16[256,1024]{1,0:T(8,128)(2,1)S(1)}, u32[]{:S(2)}, u32[]{:S(2)}) collective-permute-start(bf16[256,1024]{1,0:T(8,128)(2,1)S(1)} %get-tuple-element.20), channel_id=1, source_target_pairs={{0,512},{1,513},{2,514},{3,515},{4,516},{5,517},{6,518},{7,519},{8... | collective-permute-start | bytes 1572872 | tf_op jit(solution)/shard_map/ppermute | solution.py:132
  32.8 1.3 collective-permute-start.5
  34.2 10.9 %collective-permute-done = bf16[256,1024]{1,0:T(8,128)(2,1)S(1)} collective-permute-done((bf16[256,1024]{1,0:T(8,128)(2,1)S(1)}, bf16[256,1024]{1,0:T(8,128)(2,1)S(1)}, u32[]{:S(2)}, u32[]{:S(2)}) %collective-permute-start) | collective-permute-done | bytes 524320 | tf_op jit(solution)/shard_map/ppermute | solution.py:132
  45.1 10.1 %collective-permute-done.5 = bf16[256,1024]{1,0:T(8,128)(2,1)S(1)} collective-permute-done((bf16[256,1024]{1,0:T(8,128)(2,1)S(1)}, bf16[256,1024]{1,0:T(8,128)(2,1)S(1)}, u32[]{:S(2)}, u32[]{:S(2)}) %collective-permute-start.5) | collective-permute-done | bytes 524320 | tf_op jit(solution)/shard_map/ppermute | solution.py:132
  55.2 0.2 slice_add_fusion
  55.4 1.3 collective-permute-start.6
  56.7 1.3 collective-permute-start.1
  58.0 5.3 %collective-permute-done.6 = bf16[256,1024]{1,0:T(8,128)(2,1)S(1)} collective-permute-done((bf16[256,1024]{1,0:T(8,128)(2,1)S(1)}, bf16[256,1024]{1,0:T(8,128)(2,1)S(1)}, u32[]{:S(2)}, u32[]{:S(2)}) %collective-permute-start.6) | collective-permute-done | bytes 524320 | tf_op jit(solution)/shard_map/ppermute | solution.py:132
  63.3 0.2 add.64
  63.5 1.3 collective-permute-start.7
  64.9 4.1 %collective-permute-done.1 = bf16[256,1024]{1,0:T(8,128)(2,1)S(1)} collective-permute-done((bf16[256,1024]{1,0:T(8,128)(2,1)S(1)}, bf16[256,1024]{1,0:T(8,128)(2,1)S(1)}, u32[]{:S(2)}, u32[]{:S(2)}) %collective-permute-start.1) | collective-permute-done | bytes 524320 | tf_op jit(solution)/shard_map/ppermute | solution.py:132
  69.0 0.2 add.59
  69.2 1.3 collective-permute-start.2
  70.5 4.1 %collective-permute-done.7 = bf16[256,1024]{1,0:T(8,128)(2,1)S(1)} collective-permute-done((bf16[256,1024]{1,0:T(8,128)(2,1)S(1)}, bf16[256,1024]{1,0:T(8,128)(2,1)S(1)}, u32[]{:S(2)}, u32[]{:S(2)}) %collective-permute-start.7) | collective-permute-done | bytes 524320 | tf_op jit(solution)/shard_map/ppermute | solution.py:132
  74.6 0.2 add.65
  74.8 1.3 collective-permute-start.8
  76.1 4.1 %collective-permute-done.2 = bf16[256,1024]{1,0:T(8,128)(2,1)S(1)} collective-permute-done((bf16[256,1024]{1,0:T(8,128)(2,1)S(1)}, bf16[256,1024]{1,0:T(8,128)(2,1)S(1)}, u32[]{:S(2)}, u32[]{:S(2)}) %collective-permute-start.2) | collective-permute-done | bytes 524320 | tf_op jit(solution)/shard_map/ppermute | solution.py:132
  80.2 0.2 add.60
  80.4 1.3 collective-permute-start.3
  81.7 4.1 %collective-permute-done.8 = bf16[256,1024]{1,0:T(8,128)(2,1)S(1)} collective-permute-done((bf16[256,1024]{1,0:T(8,128)(2,1)S(1)}, bf16[256,1024]{1,0:T(8,128)(2,1)S(1)}, u32[]{:S(2)}, u32[]{:S(2)}) %collective-permute-start.8) | collective-permute-done | bytes 524320 | tf_op jit(solution)/shard_map/ppermute | solution.py:132
  85.8 0.2 add.66
  86.0 1.3 collective-permute-start.9
  87.3 4.1 %collective-permute-done.3 = bf16[256,1024]{1,0:T(8,128)(2,1)S(1)} collective-permute-done((bf16[256,1024]{1,0:T(8,128)(2,1)S(1)}, bf16[256,1024]{1,0:T(8,128)(2,1)S(1)}, u32[]{:S(2)}, u32[]{:S(2)}) %collective-permute-start.3) | collective-permute-done | bytes 524320 | tf_op jit(solution)/shard_map/ppermute | solution.py:132
  91.4 0.2 add.61
  91.6 1.3 collective-permute-start.4
  92.9 4.1 %collective-permute-done.9 = bf16[256,1024]{1,0:T(8,128)(2,1)S(1)} collective-permute-done((bf16[256,1024]{1,0:T(8,128)(2,1)S(1)}, bf16[256,1024]{1,0:T(8,128)(2,1)S(1)}, u32[]{:S(2)}, u32[]{:S(2)}) %collective-permute-start.9) | collective-permute-done | bytes 524320 | tf_op jit(solution)/shard_map/ppermute | solution.py:132
  97.0 0.2 add.67.high_ref
  97.2 5.4 %collective-permute-done.4 = bf16[256,1024]{1,0:T(8,128)(2,1)S(1)} collective-permute-done((bf16[256,1024]{1,0:T(8,128)(2,1)S(1)}, bf16[256,1024]{1,0:T(8,128)(2,1)S(1)}, u32[]{:S(2)}, u32[]{:S(2)}) %collective-permute-start.4) | collective-permute-done | bytes 524320 | tf_op jit(solution)/shard_map/ppermute | solution.py:132
  102.7 0.2 add.62.low_ref
  102.9 1.8 shard_map.38
  104.7 1.9 collective-permute-start.10
  106.6 1.9 collective-permute-done.10
  108.5 1.0 add_convert_fusion
  109.5 7.4 %all-to-all-start = ((bf16[16,16,1024]{2,1,0:T(8,128)(2,1)}), bf16[16,16,1024]{2,1,0:T(8,128)(2,1)S(1)}, u32[]{:S(2)}, u32[]{:S(2)}) async-start(bf16[16,16,1024]{2,1,0:T(8,128)(2,1)} %bitcast.2), calls=%async_computation | async-start | bytes 1048576 | tf_op jit(solution)/shard_map/all_to_all | solution.py:139
  116.9 0.8 convert_bitcast_fusion
  117.7 0.1 broadcast_bitcast_fusion.1
  117.8 8.3 %all-to-all-done = bf16[16,16,1024]{2,1,0:T(8,128)(2,1)S(1)} async-done(((bf16[16,16,1024]{2,1,0:T(8,128)(2,1)}), bf16[16,16,1024]{2,1,0:T(8,128)(2,1)S(1)}, u32[]{:S(2)}, u32[]{:S(2)}) %all-to-all-start) | async-done | bytes 524320 | tf_op jit(solution)/shard_map/all_to_all | solution.py:139
  126.1 0.1 convert_reduce_fusion
  126.2 0.1 broadcast_in_dim.10
  126.2 14.0 %all_to_all.15 = bf16[16,16,1024]{2,1,0:T(8,128)(2,1)S(1)} all-to-all(bf16[16,16,1024]{2,1,0:T(8,128)(2,1)S(1)} %broadcast_in_dim.10), channel_id=1, replica_groups={{0,2,4,6,8,10,12,14,16,18,20,22,24,26,28,30},{1,3,5,7,9,11,13,15,17,19,..., dimensions={0} | all-to-all | bytes 1048576 | tf_op jit(solution)/shard_map/all_to_all | solution.py:143
  140.2 1.9 collective-permute-start.11
  142.1 1.9 collective-permute-done.11.other_ref
  144.0 2.6 %shard_map.39 = (f32[256,1024]{1,0:T(8,128)S(1)}, bf16[256,1024]{1,0:T(8,128)(2,1)S(1)}) custom-call(s32[2]{0:T(128)S(1)} %pad_add_fusion.where_ref, bf16[256,1024]{1,0:T(8,128)(2,1)S(1)} %bitcast.14, bf16[256,1024]{1,0:T(8,128)(2,1)S(1)} %collective-permute-done.11.other_ref, bf16[1024,1024]{1,0:T(8,128)(2,1)S(1)} %get-tuple-element.12.sparse_ref), custom_call_target="tpu_custom_call" | custom-call | flops 1073741824 | bytes 4194304 | tf_op jit(solution)/shard_map/pallas_call | solution.py:146
  146.6 13.0 %collective-permute-start.12 = (bf16[256,1024]{1,0:T(8,128)(2,1)S(1)}, bf16[256,1024]{1,0:T(8,128)(2,1)S(1)}, u32[]{:S(2)}, u32[]{:S(2)}) collective-permute-start(bf16[256,1024]{1,0:T(8,128)(2,1)S(1)} %get-tuple-element.16), channel_id=1, source_target_pairs={{0,32},{1,993},{2,34},{3,995},{4,36},{5,997},{6,38},{7,999},{8,40}... | collective-permute-start | bytes 1572872 | tf_op jit(solution)/shard_map/ppermute | solution.py:152
  159.6 11.8 %collective-permute-done.12 = bf16[256,1024]{1,0:T(8,128)(2,1)S(1)} collective-permute-done((bf16[256,1024]{1,0:T(8,128)(2,1)S(1)}, bf16[256,1024]{1,0:T(8,128)(2,1)S(1)}, u32[]{:S(2)}, u32[]{:S(2)}) %collective-permute-start.12) | collective-permute-done | bytes 524320 | tf_op jit(solution)/shard_map/ppermute | solution.py:152
  171.4 0.2 convert_add_fusion
  171.6 1.9 collective-permute-start.13
  173.6 9.1 %collective-permute-done.13.got_ref = bf16[128,1024]{1,0:T(8,128)(2,1)S(1)} collective-permute-done((bf16[128,1024]{1,0:T(8,128)(2,1)S(1)}, bf16[128,1024]{1,0:T(8,128)(2,1)S(1)}, u32[]{:S(2)}, u32[]{:S(2)}) %collective-permute-start.13) | collective-permute-done | bytes 262176 | tf_op jit(solution)/shard_map/ppermute | solution.py:154
  182.7 1.3 shard_map.40
  184.0 10.6 %all-to-all-start.2 = ((bf16[8,16,1024]{2,1,0:T(8,128)(2,1)}), bf16[8,16,1024]{2,1,0:T(8,128)(2,1)S(1)}, u32[]{:S(2)}, u32[]{:S(2)}) async-start(bf16[8,16,1024]{2,1,0:T(8,128)(2,1)} %bitcast.6), calls=%async_computation.2 | async-start | bytes 524288 | tf_op jit(solution)/shard_map/all_to_all | solution.py:158
  194.5 0.1 broadcast_bitcast_fusion
  194.6 38.4 %all-to-all-done.2 = bf16[8,16,1024]{2,1,0:T(8,128)(2,1)S(1)} async-done(((bf16[8,16,1024]{2,1,0:T(8,128)(2,1)}), bf16[8,16,1024]{2,1,0:T(8,128)(2,1)S(1)}, u32[]{:S(2)}, u32[]{:S(2)}) %all-to-all-start.2) | async-done | bytes 262176 | tf_op jit(solution)/shard_map/all_to_all | solution.py:158
  233.1 0.6 multiply_convert_fusion
  (4 shorter events, 0.1 us)
Async XLA Ops:
  0.1 1.6 copy-start
  1.7 0.7 copy-start.1
  3.8 41.3 %collective-permute-start = (bf16[256,1024]{1,0:T(8,128)(2,1)S(1)}, bf16[256,1024]{1,0:T(8,128)(2,1)S(1)}, u32[]{:S(2)}, u32[]{:S(2)}) collective-permute-start(bf16[256,1024]{1,0:T(8,128)(2,1)S(1)} %get-tuple-element.20), channel_id=1, source_target_pairs={{0,512},{1,513},{2,514},{3,515},{4,516},{5,517},{6,518},{7,519},{8... | collective-permute-start | bytes 1572872 | tf_op jit(solution)/shard_map/ppermute | solution.py:132
  32.8 22.4 %collective-permute-start.5 = (bf16[256,1024]{1,0:T(8,128)(2,1)S(1)}, bf16[256,1024]{1,0:T(8,128)(2,1)S(1)}, u32[]{:S(2)}, u32[]{:S(2)}) collective-permute-start(bf16[256,1024]{1,0:T(8,128)(2,1)S(1)} %get-tuple-element.19), channel_id=1, source_target_pairs={{0,512},{1,513},{2,514},{3,515},{4,516},{5,517},{6,518},{7,519},{8... | collective-permute-start | bytes 1572872 | tf_op jit(solution)/shard_map/ppermute | solution.py:132
  55.4 8.0 %collective-permute-start.6 = (bf16[256,1024]{1,0:T(8,128)(2,1)S(1)}, bf16[256,1024]{1,0:T(8,128)(2,1)S(1)}, u32[]{:S(2)}, u32[]{:S(2)}) collective-permute-start(bf16[256,1024]{1,0:T(8,128)(2,1)S(1)} %get-tuple-element.17), channel_id=1, source_target_pairs={{0,256},{1,769},{2,258},{3,771},{4,260},{5,773},{6,262},{7,775},{8... | collective-permute-start | bytes 1572872 | tf_op jit(solution)/shard_map/ppermute | solution.py:132
  56.7 12.3 %collective-permute-start.1 = (bf16[256,1024]{1,0:T(8,128)(2,1)S(1)}, bf16[256,1024]{1,0:T(8,128)(2,1)S(1)}, u32[]{:S(2)}, u32[]{:S(2)}) collective-permute-start(bf16[256,1024]{1,0:T(8,128)(2,1)S(1)} %get-tuple-element.18), channel_id=1, source_target_pairs={{0,256},{1,769},{2,258},{3,771},{4,260},{5,773},{6,262},{7,775},{8... | collective-permute-start | bytes 1572872 | tf_op jit(solution)/shard_map/ppermute | solution.py:132
  63.5 11.0 %collective-permute-start.7 = (bf16[256,1024]{1,0:T(8,128)(2,1)S(1)}, bf16[256,1024]{1,0:T(8,128)(2,1)S(1)}, u32[]{:S(2)}, u32[]{:S(2)}) collective-permute-start(bf16[256,1024]{1,0:T(8,128)(2,1)S(1)} %add.64), channel_id=1, source_target_pairs={{0,128},{1,897},{2,130},{3,899},{4,132},{5,901},{6,134},{7,903},{8... | collective-permute-start | bytes 1572872 | tf_op jit(solution)/shard_map/ppermute | solution.py:132
  69.2 11.0 %collective-permute-start.2 = (bf16[256,1024]{1,0:T(8,128)(2,1)S(1)}, bf16[256,1024]{1,0:T(8,128)(2,1)S(1)}, u32[]{:S(2)}, u32[]{:S(2)}) collective-permute-start(bf16[256,1024]{1,0:T(8,128)(2,1)S(1)} %add.59), channel_id=1, source_target_pairs={{0,128},{1,897},{2,130},{3,899},{4,132},{5,901},{6,134},{7,903},{8... | collective-permute-start | bytes 1572872 | tf_op jit(solution)/shard_map/ppermute | solution.py:132
  74.8 11.0 %collective-permute-start.8 = (bf16[256,1024]{1,0:T(8,128)(2,1)S(1)}, bf16[256,1024]{1,0:T(8,128)(2,1)S(1)}, u32[]{:S(2)}, u32[]{:S(2)}) collective-permute-start(bf16[256,1024]{1,0:T(8,128)(2,1)S(1)} %add.65), channel_id=1, source_target_pairs={{0,64},{1,961},{2,66},{3,963},{4,68},{5,965},{6,70},{7,967},{8,72}... | collective-permute-start | bytes 1572872 | tf_op jit(solution)/shard_map/ppermute | solution.py:132
  80.4 11.0 %collective-permute-start.3 = (bf16[256,1024]{1,0:T(8,128)(2,1)S(1)}, bf16[256,1024]{1,0:T(8,128)(2,1)S(1)}, u32[]{:S(2)}, u32[]{:S(2)}) collective-permute-start(bf16[256,1024]{1,0:T(8,128)(2,1)S(1)} %add.60), channel_id=1, source_target_pairs={{0,64},{1,961},{2,66},{3,963},{4,68},{5,965},{6,70},{7,967},{8,72}... | collective-permute-start | bytes 1572872 | tf_op jit(solution)/shard_map/ppermute | solution.py:132
  86.0 11.0 %collective-permute-start.9 = (bf16[256,1024]{1,0:T(8,128)(2,1)S(1)}, bf16[256,1024]{1,0:T(8,128)(2,1)S(1)}, u32[]{:S(2)}, u32[]{:S(2)}) collective-permute-start(bf16[256,1024]{1,0:T(8,128)(2,1)S(1)} %add.66), channel_id=1, source_target_pairs={{0,32},{1,993},{2,34},{3,995},{4,36},{5,997},{6,38},{7,999},{8,40}... | collective-permute-start | bytes 1572872 | tf_op jit(solution)/shard_map/ppermute | solution.py:132
  91.6 11.0 %collective-permute-start.4 = (bf16[256,1024]{1,0:T(8,128)(2,1)S(1)}, bf16[256,1024]{1,0:T(8,128)(2,1)S(1)}, u32[]{:S(2)}, u32[]{:S(2)}) collective-permute-start(bf16[256,1024]{1,0:T(8,128)(2,1)S(1)} %add.61), channel_id=1, source_target_pairs={{0,32},{1,993},{2,34},{3,995},{4,36},{5,997},{6,38},{7,999},{8,40}... | collective-permute-start | bytes 1572872 | tf_op jit(solution)/shard_map/ppermute | solution.py:132
  104.7 3.8 %collective-permute-start.10 = (bf16[256,1024]{1,0:T(8,128)(2,1)S(1)}, bf16[256,1024]{1,0:T(8,128)(2,1)S(1)}, u32[]{:S(2)}, u32[]{:S(2)}) collective-permute-start(bf16[256,1024]{1,0:T(8,128)(2,1)S(1)} %get-tuple-element.14), channel_id=1, source_target_pairs={{0,1},{1,0},{2,3},{3,2},{4,5},{5,4},{6,7},{7,6},{8,9},{9,8},{10,11... | collective-permute-start | bytes 1572872 | tf_op jit(solution)/shard_map/ppermute | solution.py:138
  109.5 16.6 %all-to-all-start = ((bf16[16,16,1024]{2,1,0:T(8,128)(2,1)}), bf16[16,16,1024]{2,1,0:T(8,128)(2,1)S(1)}, u32[]{:S(2)}, u32[]{:S(2)}) async-start(bf16[16,16,1024]{2,1,0:T(8,128)(2,1)} %bitcast.2), calls=%async_computation | async-start | bytes 1048576 | tf_op jit(solution)/shard_map/all_to_all | solution.py:139
  140.2 3.8 %collective-permute-start.11 = (bf16[256,1024]{1,0:T(8,128)(2,1)S(1)}, bf16[256,1024]{1,0:T(8,128)(2,1)S(1)}, u32[]{:S(2)}, u32[]{:S(2)}) collective-permute-start(bf16[256,1024]{1,0:T(8,128)(2,1)S(1)} %bitcast.13), channel_id=1, source_target_pairs={{0,1},{1,0},{2,3},{3,2},{4,5},{5,4},{6,7},{7,6},{8,9},{9,8},{10,11... | collective-permute-start | bytes 1572872 | tf_op jit(solution)/shard_map/ppermute | solution.py:144
  146.6 24.8 %collective-permute-start.12 = (bf16[256,1024]{1,0:T(8,128)(2,1)S(1)}, bf16[256,1024]{1,0:T(8,128)(2,1)S(1)}, u32[]{:S(2)}, u32[]{:S(2)}) collective-permute-start(bf16[256,1024]{1,0:T(8,128)(2,1)S(1)} %get-tuple-element.16), channel_id=1, source_target_pairs={{0,32},{1,993},{2,34},{3,995},{4,36},{5,997},{6,38},{7,999},{8,40}... | collective-permute-start | bytes 1572872 | tf_op jit(solution)/shard_map/ppermute | solution.py:152
  171.6 11.1 %collective-permute-start.13 = (bf16[128,1024]{1,0:T(8,128)(2,1)S(1)}, bf16[128,1024]{1,0:T(8,128)(2,1)S(1)}, u32[]{:S(2)}, u32[]{:S(2)}) collective-permute-start(bf16[128,1024]{1,0:T(8,128)(2,1)S(1)} %slice.22), channel_id=1, source_target_pairs={{0,64},{1,961},{2,66},{3,963},{4,68},{5,965},{6,70},{7,967},{8,72}... | collective-permute-start | bytes 786440 | tf_op jit(solution)/shard_map/ppermute | solution.py:154
  184.0 49.1 %all-to-all-start.2 = ((bf16[8,16,1024]{2,1,0:T(8,128)(2,1)}), bf16[8,16,1024]{2,1,0:T(8,128)(2,1)S(1)}, u32[]{:S(2)}, u32[]{:S(2)}) async-start(bf16[8,16,1024]{2,1,0:T(8,128)(2,1)} %bitcast.6), calls=%async_computation.2 | async-start | bytes 524288 | tf_op jit(solution)/shard_map/all_to_all | solution.py:158

commit v2 on v1

v2 whole, which is shorter than its diff:
```python
import functools

import jax
import jax.numpy as jnp
from jax import lax
from jax.experimental import pallas as pl
from jax.experimental.pallas import tpu as pltpu
from jax.sharding import PartitionSpec as P

BS = 128
BF16 = jnp.bfloat16
F32 = jnp.float32
VMEM = pl.BlockSpec(memory_space=pltpu.VMEM)
SMEM = pl.BlockSpec(memory_space=pltpu.SMEM)
BOTH = ("row", "col")


def call(kernel, outs, cost, scratch=()):
    return functools.partial(
        pl.pallas_call,
        kernel,
        out_shape=outs,
        out_specs=jax.tree.map(lambda _: VMEM, outs),
        scratch_shapes=list(scratch),
        compiler_params=pltpu.CompilerParams(vmem_limit_bytes=24 * 2**20),
        cost_estimate=pl.CostEstimate(flops=cost, bytes_accessed=4 * 2**20, transcendentals=0),
    )


def panel_kernel(where_ref, occ_ref, density_ref, *half_refs):
    first = where_ref[0] == 0
    blocks = half_refs[0].shape[0] // BS
    for i in range(2 * blocks):
        for j in range(occ_ref.shape[1]):
            across = pl.ds(j * BS, BS)
            kept = density_ref[pl.ds(i * BS, BS), across] * occ_ref[i, j].astype(F32).astype(BF16)
            half_refs[i // blocks][pl.ds(i % blocks * BS, BS), across] = jnp.where(first, kept, jnp.zeros_like(kept))


def mask_kernel(occ_ref, density_ref, sparse_ref):
    for i in range(occ_ref.shape[0]):
        for j in range(occ_ref.shape[1]):
            spot = (pl.ds(i * BS, BS), pl.ds(j * BS, BS))
            sparse_ref[spot] = density_ref[spot] * occ_ref[i, j].astype(F32).astype(BF16)


def square_part(left_ref, sparse_ref, n):
    return lax.dot_general(
        left_ref[...], sparse_ref[n, :], (((1,), (1,)), ((), ())), preferred_element_type=F32
    )


def tiles(size):
    tile = min(256, size)
    return [pl.ds(n, tile) for n in range(0, size, tile)]


def sent_kernel(where_ref, low_ref, high_ref, sparse_ref, sent_ref):
    core = where_ref[1] % 2
    for mine, left_ref in ((1, low_ref), (0, high_ref)):

        @pl.when(core == mine)
        def _():
            for n in tiles(sparse_ref.shape[0]):
                sent_ref[:, n] = square_part(left_ref, sparse_ref, n).astype(BF16)


def kept_kernel(where_ref, low_ref, high_ref, sparse_ref, got_ref, kept_ref):
    core = where_ref[1] % 2
    for mine, left_ref in ((0, low_ref), (1, high_ref)):

        @pl.when(core == mine)
        def _():
            for n in tiles(sparse_ref.shape[0]):
                total = square_part(left_ref, sparse_ref, n) + got_ref[:, n].astype(F32)
                kept_ref[:, n] = total.astype(BF16)


def cube_part(where_ref, left_ref, sparse_ref, first, kept_ref, sent_ref):
    three = jnp.where(where_ref[0] == where_ref[1], 3.0, 0.0).astype(F32)
    middle = left_ref.shape[0] // 2
    for n in tiles(kept_ref.shape[1]):
        there = pl.ds(first + n.start, n.size)
        product = jnp.dot(left_ref[...], sparse_ref[:, there], preferred_element_type=F32)
        total = three * left_ref[:, there].astype(F32) - 2.0 * product
        kept_ref[:, n] = total[:middle]
        sent_ref[:, n] = total[middle:].astype(BF16)


def first_kernel(rows, where_ref, mine_ref, other_ref, sparse_ref, left_ref, kept_ref, sent_ref):
    row, core = where_ref[0], where_ref[1] % 2
    sign = 1 - 2 * core
    piece = left_ref.shape[0] // rows
    half = rows // 2
    order = [t for start in (0, 2, 1, 3) for t in range(start, rows, 4)]
    for place, t in enumerate(order):
        target = (row + sign * t + rows) % rows
        source = pl.ds(pl.multiple_of((target % half) * piece, piece), piece)
        spot = pl.ds(place * piece, piece)
        left_ref[spot, :] = jnp.where(target // half == core, mine_ref[source, :], other_ref[source, :])
    cube_part(where_ref, left_ref, sparse_ref, 0, kept_ref, sent_ref)


def second_kernel(where_ref, left_ref, sparse_ref, kept_ref, sent_ref):
    cube_part(where_ref, left_ref, sparse_ref, kept_ref.shape[1], kept_ref, sent_ref)


def order_kernel(groups, where_ref, *refs):
    out_ref = refs[-1]
    row, col = where_ref[0], where_ref[1]
    sign = 1 - 2 * (col % 2)
    piece = out_ref.shape[0] // groups
    wide = out_ref.shape[1] // 2
    for u in range(groups):
        place = (row // 4 + sign * u + groups) % groups
        source = pl.ds(u * piece, piece)
        spot = pl.ds(pl.multiple_of(place * piece, piece), piece)
        for side in range(2):
            kept_ref, got_ref = refs[2 * side : 2 * side + 2]
            total = kept_ref[source, :] + got_ref[source, :].astype(F32)
            out_ref[spot, pl.ds(side * wide, wide)] = total.astype(BF16)


def body(rows, cols, density, occupancy, product_keep):
    rows_here, cols_here = density.shape
    window = product_keep.shape[0] * BS
    row, col = lax.axis_index("row"), lax.axis_index("col")
    where = jnp.stack([row, col]).astype(jnp.int32)
    half = window // 2
    quarter = window // 4
    piece = window // rows
    chips = cols // 2
    wide = cols_here // 2
    tall = jax.ShapeDtypeStruct
    work = window * rows_here * cols_here

    def pairs(moves):
        return [
            (z * sign % rows * cols + c, (z + step) * sign % rows * cols + c)
            for z, step in moves
            for c in range(cols)
            for sign in [1 - 2 * (c % 2)]
        ]

    swap = [(c, c ^ 1) for c in range(cols)]
    same_core = [[2 * i + k for i in range(chips)] for k in range(2)]
    groups = rows // 4
    strided = [[4 * i + o for i in range(groups)] for o in range(4)]

    def mask(across, down_first, across_first):
        kept = lax.dynamic_slice(product_keep, (down_first, across_first), (1, across))
        return jnp.repeat(kept, BS, axis=1).astype(F32)

    halves = call(panel_kernel, [tall((half, cols_here), BF16)] * 2, 10**6)(in_specs=[SMEM, SMEM, VMEM])(
        where, occupancy, density[:window]
    )
    sparse = call(mask_kernel, tall(density.shape, BF16), 10**6)(in_specs=[SMEM, VMEM])(occupancy, density)

    have, gap, stages = [0], rows, []
    while gap > 2:
        gap //= 4
        stages.append([(z, gap) for z in have])
        stages.append([(z, -gap) for z in have] + [(z + gap, gap) for z in have])
        have = [z + step * gap for z in have for step in (-1, 0, 1, 2)]
    stages.append([(z, 1) for z in have])
    for moves in stages:
        halves = [h + lax.ppermute(h, BOTH, pairs(moves)) for h in halves]

    sent = call(sent_kernel, tall((half, rows_here), BF16), work)(in_specs=[SMEM, VMEM, VMEM, VMEM])(
        where, *halves, sparse
    )
    got = lax.ppermute(sent, "col", swap)
    kept = call(kept_kernel, tall((half, rows_here), BF16), work)(in_specs=[SMEM, VMEM, VMEM, VMEM, VMEM])(
        where, *halves, sparse, got
    )
    parts = lax.all_to_all(kept.reshape(chips, piece, rows_here), "col", 0, 0, axis_index_groups=same_core, tiled=True)
    first = (col % 2) * half + (col // 2) * piece
    square = parts.astype(F32).sum(0) * mask(rows_here // BS, first // BS, row * (rows_here // BS))
    square = jnp.broadcast_to(square.astype(BF16), (chips, piece, rows_here))
    mine = lax.all_to_all(square, "col", 0, 0, axis_index_groups=same_core, tiled=True).reshape(half, rows_here)
    other = lax.ppermute(mine, "col", swap)

    pair = (tall((half, wide), F32), tall((half, wide), BF16))
    left, *first_side = call(
        functools.partial(first_kernel, rows), (tall((window, rows_here), BF16), *pair), work
    )(in_specs=[SMEM, VMEM, VMEM, VMEM])(where, mine, other, sparse)
    second_side = call(second_kernel, pair, work)(in_specs=[SMEM, VMEM, VMEM])(where, left, sparse)
    terms = []
    for kept, sent in (first_side, second_side):
        kept = kept + lax.ppermute(sent, BOTH, pairs([(z, 1) for z in range(rows)])).astype(F32)
        got = lax.ppermute(kept[quarter:].astype(BF16), BOTH, pairs([(z, 2) for z in range(rows)]))
        terms += [kept, got]
    ready = call(functools.partial(order_kernel, groups), tall((quarter, cols_here), BF16), 10**6)(
        in_specs=[SMEM] + [VMEM] * 4
    )(where, *terms)
    parts = lax.all_to_all(ready.reshape(groups, piece, cols_here), "row", 0, 0, axis_index_groups=strided, tiled=True)
    result = parts.astype(F32).sum(0)
    result = result * mask(cols_here // BS, row * piece // BS, col * (cols_here // BS))
    return result.astype(BF16)


def solution(mesh):
    rows, cols = mesh.shape["row"], mesh.shape["col"]
    return jax.shard_map(
        functools.partial(body, rows, cols),
        mesh=mesh,
        in_specs=(P("row", "col"), P("row", "col"), P()),
        out_specs=P("row", "col"),
        check_vma=False,
    )
```

time: 235 us -> 221 us (0.940)
  waiting for transfers between devices: 128 us -> 105 us
  starting transfers between devices: 77.6 us -> 85.8 us
  Pallas kernels: 7.06 us -> 9.48 us
    ppermute x13 -> x15, waiting for transfers between devices: 79.1 us -> 56.6 us  [the longest x10 48.4 us: body(): halves = [h + lax.ppermute(h, BOTH, pairs(moves)) for h in halves]]
    all_to_all x1, starting transfers between devices: 10.6 us -> 22.9 us  [body(): lax.all_to_all(ready.reshape(groups, piece, cols_here), 'row', 0, 0, axis...]
    ppermute x13 -> x15, starting transfers between devices: 57.7 us -> 53.5 us  [the longest x10 28.5 us: body(): halves = [h + lax.ppermute(h, BOTH, pairs(moves)) for h in halves]]
    pallas_call x3 -> x6, Pallas kernels: 5.77 us -> 8.19 us  [the longest x1 2.11 us: body(): call(kept_kernel, tall((half, rows_here), BF16), work)]
  transfers between devices with their start and end apart: 16 -> 18, of which waited for: 16 -> 15; matrix products, arithmetic and copies ran while one was open for 1% -> 1% of each run, Pallas kernels for 0% -> 1%
where the time goes in v2:
time: 221 us; the launch traced here: 219 us
  waiting for transfers between devices  105 us (48%)
  starting transfers between devices  85.8 us (39%)
  blocking collectives  14 us (6%)
  Pallas kernels  9.48 us (4%)
  other arithmetic  3.69 us (2%)
    ppermute x10, waiting for transfers between devices, body(): halves = [h + lax.ppermute(h, BOTH, pairs(moves)) for h in halves]  48.4 us
    all_to_all x1, waiting for transfers between devices, body(): lax.all_to_all(ready.reshape(groups, piece, cols_here), 'row', 0, 0, axis...  37.6 us
    ppermute x10, starting transfers between devices, body(): halves = [h + lax.ppermute(h, BOTH, pairs(moves)) for h in halves]  28.5 us
    all_to_all x1, starting transfers between devices, body(): lax.all_to_all(ready.reshape(groups, piece, cols_here), 'row', 0, 0, axis...  22.9 us
    all_to_all x1, blocking collectives, body(): lax.all_to_all(square, 'col', 0, 0, axis_index_groups=same_core, tiled=True)  14 us
    ppermute x2, starting transfers between devices, body(): lax.ppermute(kept[quarter:].astype(BF16), BOTH, pairs([(z, 2) for z in ra...  10.2 us
    all_to_all x1, waiting for transfers between devices, body(): lax.all_to_all(kept.reshape(chips, piece, rows_here), 'col', 0, 0, axis_i...  8.54 us
    ppermute x2, starting transfers between devices, body(): lax.ppermute(sent, BOTH, pairs([(z, 1) for z in range(rows)])).astype(F32)  7.64 us
  transfers between devices with their start and end apart: 18, of which 15 were waited for; matrix products, arithmetic and copies ran while one was open for 1% of the time, Pallas kernels for 1%

profile of v2, /device:TPU:6, one launch (start us, length us, event | category | flops | bytes accessed | tf_op | source)
XLA Modules:
  0.0 219.4 jit_solution(9325604480312201998)
XLA Ops:
  0.0 1.3 slice.11.density_ref
  1.3 0.1 pad_add_fusion.where_ref
  1.4 0.9 shard_map.37
  2.3 15.8 %collective-permute-start.5 = (bf16[256,1024]{1,0:T(8,128)(2,1)S(1)}, bf16[256,1024]{1,0:T(8,128)(2,1)S(1)}, u32[]{:S(2)}, u32[]{:S(2)}) collective-permute-start(bf16[256,1024]{1,0:T(8,128)(2,1)S(1)} %get-tuple-element.13), channel_id=1, source_target_pairs={{0,256},{1,769},{2,258},{3,771},{4,260},{5,773},{6,262},{7,775},{8... | collective-permute-start | bytes 1572872 | tf_op jit(solution)/shard_map/ppermute | solution.py:167
  18.1 1.3 collective-permute-start
  19.4 5.3 %collective-permute-done.5 = bf16[256,1024]{1,0:T(8,128)(2,1)S(1)} collective-permute-done((bf16[256,1024]{1,0:T(8,128)(2,1)S(1)}, bf16[256,1024]{1,0:T(8,128)(2,1)S(1)}, u32[]{:S(2)}, u32[]{:S(2)}) %collective-permute-start.5) | collective-permute-done | bytes 524320 | tf_op jit(solution)/shard_map/ppermute | solution.py:167
  24.7 0.2 add.63
  24.9 2.0 collective-permute-start.6
  27.0 3.4 %collective-permute-done = bf16[256,1024]{1,0:T(8,128)(2,1)S(1)} collective-permute-done((bf16[256,1024]{1,0:T(8,128)(2,1)S(1)}, bf16[256,1024]{1,0:T(8,128)(2,1)S(1)}, u32[]{:S(2)}, u32[]{:S(2)}) %collective-permute-start) | collective-permute-done | bytes 524320 | tf_op jit(solution)/shard_map/ppermute | solution.py:167
  30.3 0.2 add.58
  30.5 1.3 collective-permute-start.1
  31.9 7.4 %collective-permute-done.6 = bf16[256,1024]{1,0:T(8,128)(2,1)S(1)} collective-permute-done((bf16[256,1024]{1,0:T(8,128)(2,1)S(1)}, bf16[256,1024]{1,0:T(8,128)(2,1)S(1)}, u32[]{:S(2)}, u32[]{:S(2)}) %collective-permute-start.6) | collective-permute-done | bytes 524320 | tf_op jit(solution)/shard_map/ppermute | solution.py:167
  39.3 0.2 add.64
  39.5 1.3 collective-permute-start.7
  40.8 6.9 %collective-permute-done.1 = bf16[256,1024]{1,0:T(8,128)(2,1)S(1)} collective-permute-done((bf16[256,1024]{1,0:T(8,128)(2,1)S(1)}, bf16[256,1024]{1,0:T(8,128)(2,1)S(1)}, u32[]{:S(2)}, u32[]{:S(2)}) %collective-permute-start.1) | collective-permute-done | bytes 524320 | tf_op jit(solution)/shard_map/ppermute | solution.py:167
  47.7 0.2 add.59
  47.9 1.3 collective-permute-start.2
  49.2 0.0 collective-permute-done.7
  49.3 0.2 add.65
  49.5 0.0 copy-start
  49.5 1.5 collective-permute-start.8
  50.9 7.8 %collective-permute-done.2 = bf16[256,1024]{1,0:T(8,128)(2,1)S(1)} collective-permute-done((bf16[256,1024]{1,0:T(8,128)(2,1)S(1)}, bf16[256,1024]{1,0:T(8,128)(2,1)S(1)}, u32[]{:S(2)}, u32[]{:S(2)}) %collective-permute-start.2) | collective-permute-done | bytes 524320 | tf_op jit(solution)/shard_map/ppermute | solution.py:167
  58.7 0.2 add.60
  58.9 1.3 collective-permute-start.3
  60.2 1.2 collective-permute-done.8
  61.4 0.2 add.66
  61.6 1.3 collective-permute-start.9
  63.0 7.9 %collective-permute-done.3 = bf16[256,1024]{1,0:T(8,128)(2,1)S(1)} collective-permute-done((bf16[256,1024]{1,0:T(8,128)(2,1)S(1)}, bf16[256,1024]{1,0:T(8,128)(2,1)S(1)}, u32[]{:S(2)}, u32[]{:S(2)}) %collective-permute-start.3) | collective-permute-done | bytes 524320 | tf_op jit(solution)/shard_map/ppermute | solution.py:167
  70.9 0.2 add.61
  71.1 1.3 collective-permute-start.4
  72.4 1.2 shard_map.38.sparse_ref
  73.6 0.2 add.67.high_ref
  73.8 8.5 %collective-permute-done.4 = bf16[256,1024]{1,0:T(8,128)(2,1)S(1)} collective-permute-done((bf16[256,1024]{1,0:T(8,128)(2,1)S(1)}, bf16[256,1024]{1,0:T(8,128)(2,1)S(1)}, u32[]{:S(2)}, u32[]{:S(2)}) %collective-permute-start.4) | collective-permute-done | bytes 524320 | tf_op jit(solution)/shard_map/ppermute | solution.py:167
  82.3 0.2 add.62.low_ref
  82.5 1.3 shard_map.39
  83.8 7.2 %collective-permute-start.10 = (bf16[256,1024]{1,0:T(8,128)(2,1)S(1)}, bf16[256,1024]{1,0:T(8,128)(2,1)S(1)}, u32[]{:S(2)}, u32[]{:S(2)}) collective-permute-start(bf16[256,1024]{1,0:T(8,128)(2,1)S(1)} %shard_map.39), channel_id=1, source_target_pairs={{0,1},{1,0},{2,3},{3,2},{4,5},{5,4},{6,7},{7,6},{8,9},{9,8},{10,11... | collective-permute-start | bytes 1572872 | tf_op jit(solution)/shard_map/ppermute | solution.py:172
  91.0 1.5 collective-permute-done.10.got_ref
  92.6 2.1 shard_map.40
  94.7 7.4 %all-to-all-start = ((bf16[16,16,1024]{2,1,0:T(8,128)(2,1)}), bf16[16,16,1024]{2,1,0:T(8,128)(2,1)S(1)}, u32[]{:S(2)}, u32[]{:S(2)}) async-start(bf16[16,16,1024]{2,1,0:T(8,128)(2,1)} %bitcast.2), calls=%async_computation | async-start | bytes 1048576 | tf_op jit(solution)/shard_map/all_to_all | solution.py:176
  102.1 0.8 convert_bitcast_fusion
  102.9 0.1 broadcast_bitcast_fusion.1
  103.0 8.5 %all-to-all-done = bf16[16,16,1024]{2,1,0:T(8,128)(2,1)S(1)} async-done(((bf16[16,16,1024]{2,1,0:T(8,128)(2,1)}), bf16[16,16,1024]{2,1,0:T(8,128)(2,1)S(1)}, u32[]{:S(2)}, u32[]{:S(2)}) %all-to-all-start) | async-done | bytes 524320 | tf_op jit(solution)/shard_map/all_to_all | solution.py:176
  111.6 0.1 convert_reduce_fusion
  111.6 0.1 broadcast_in_dim.10
  111.7 14.0 %all_to_all.15 = bf16[16,16,1024]{2,1,0:T(8,128)(2,1)S(1)} all-to-all(bf16[16,16,1024]{2,1,0:T(8,128)(2,1)S(1)} %broadcast_in_dim.10), channel_id=1, replica_groups={{0,2,4,6,8,10,12,14,16,18,20,22,24,26,28,30},{1,3,5,7,9,11,13,15,17,19,..., dimensions={0} | all-to-all | bytes 1048576 | tf_op jit(solution)/shard_map/all_to_all | solution.py:180
  125.7 1.9 collective-permute-start.11
  127.6 1.9 collective-permute-done.11.other_ref
  129.5 1.4 shard_map.41
  130.9 1.3 shard_map.42
  132.2 5.7 %collective-permute-start.14 = (bf16[256,512]{1,0:T(8,128)(2,1)S(1)}, bf16[256,512]{1,0:T(8,128)(2,1)S(1)}, u32[]{:S(2)}, u32[]{:S(2)}) collective-permute-start(bf16[256,512]{1,0:T(8,128)(2,1)S(1)} %get-tuple-element.18), channel_id=1, source_target_pairs={{0,32},{1,993},{2,34},{3,995},{4,36},{5,997},{6,38},{7,999},{8,40}... | collective-permute-start | bytes 786440 | tf_op jit(solution)/shard_map/ppermute | solution.py:190
  137.9 1.9 collective-permute-start.12
  139.8 2.0 collective-permute-done.14
  141.8 0.1 convert_add_fusion.refs_2_
  141.9 5.1 %collective-permute-start.15 = (bf16[128,512]{1,0:T(8,128)(2,1)S(1)}, bf16[128,512]{1,0:T(8,128)(2,1)S(1)}, u32[]{:S(2)}, u32[]{:S(2)}) collective-permute-start(bf16[128,512]{1,0:T(8,128)(2,1)S(1)} %slice.18), channel_id=1, source_target_pairs={{0,64},{1,961},{2,66},{3,963},{4,68},{5,965},{6,70},{7,967},{8,72}... | collective-permute-start | bytes 393224 | tf_op jit(solution)/shard_map/ppermute | solution.py:191
  147.1 0.3 collective-permute-done.12
  147.4 0.1 convert_add_fusion.1.refs_0_
  147.5 5.1 %collective-permute-start.13 = (bf16[128,512]{1,0:T(8,128)(2,1)S(1)}, bf16[128,512]{1,0:T(8,128)(2,1)S(1)}, u32[]{:S(2)}, u32[]{:S(2)}) collective-permute-start(bf16[128,512]{1,0:T(8,128)(2,1)S(1)} %slice.19), channel_id=1, source_target_pairs={{0,64},{1,961},{2,66},{3,963},{4,68},{5,965},{6,70},{7,967},{8,72}... | collective-permute-start | bytes 393224 | tf_op jit(solution)/shard_map/ppermute | solution.py:191
  152.6 0.0 collective-permute-done.15.refs_3_
  152.6 4.3 %collective-permute-done.13.refs_1_ = bf16[128,512]{1,0:T(8,128)(2,1)S(1)} collective-permute-done((bf16[128,512]{1,0:T(8,128)(2,1)S(1)}, bf16[128,512]{1,0:T(8,128)(2,1)S(1)}, u32[]{:S(2)}, u32[]{:S(2)}) %collective-permute-start.13) | collective-permute-done | bytes 131104 | tf_op jit(solution)/shard_map/ppermute | solution.py:191
  156.8 1.3 shard_map.43
  158.1 22.9 %all-to-all-start.2 = ((bf16[8,16,1024]{2,1,0:T(8,128)(2,1)}), bf16[8,16,1024]{2,1,0:T(8,128)(2,1)S(1)}, u32[]{:S(2)}, u32[]{:S(2)}) async-start(bf16[8,16,1024]{2,1,0:T(8,128)(2,1)} %bitcast.6), calls=%async_computation.2 | async-start | bytes 524288 | tf_op jit(solution)/shard_map/all_to_all | solution.py:196
  181.1 0.1 broadcast_bitcast_fusion
  181.1 37.6 %all-to-all-done.2 = bf16[8,16,1024]{2,1,0:T(8,128)(2,1)S(1)} async-done(((bf16[8,16,1024]{2,1,0:T(8,128)(2,1)}), bf16[8,16,1024]{2,1,0:T(8,128)(2,1)S(1)}, u32[]{:S(2)}, u32[]{:S(2)}) %all-to-all-start.2) | async-done | bytes 262176 | tf_op jit(solution)/shard_map/all_to_all | solution.py:196
  218.8 0.6 multiply_convert_fusion
  (8 shorter events, 0.1 us)
Async XLA Ops:
  0.0 1.4 copy-start.1
  2.3 22.4 %collective-permute-start.5 = (bf16[256,1024]{1,0:T(8,128)(2,1)S(1)}, bf16[256,1024]{1,0:T(8,128)(2,1)S(1)}, u32[]{:S(2)}, u32[]{:S(2)}) collective-permute-start(bf16[256,1024]{1,0:T(8,128)(2,1)S(1)} %get-tuple-element.13), channel_id=1, source_target_pairs={{0,256},{1,769},{2,258},{3,771},{4,260},{5,773},{6,262},{7,775},{8... | collective-permute-start | bytes 1572872 | tf_op jit(solution)/shard_map/ppermute | solution.py:167
  18.1 12.3 %collective-permute-start = (bf16[256,1024]{1,0:T(8,128)(2,1)S(1)}, bf16[256,1024]{1,0:T(8,128)(2,1)S(1)}, u32[]{:S(2)}, u32[]{:S(2)}) collective-permute-start(bf16[256,1024]{1,0:T(8,128)(2,1)S(1)} %get-tuple-element.12), channel_id=1, source_target_pairs={{0,256},{1,769},{2,258},{3,771},{4,260},{5,773},{6,262},{7,775},{8... | collective-permute-start | bytes 1572872 | tf_op jit(solution)/shard_map/ppermute | solution.py:167
  24.9 14.4 %collective-permute-start.6 = (bf16[256,1024]{1,0:T(8,128)(2,1)S(1)}, bf16[256,1024]{1,0:T(8,128)(2,1)S(1)}, u32[]{:S(2)}, u32[]{:S(2)}) collective-permute-start(bf16[256,1024]{1,0:T(8,128)(2,1)S(1)} %add.63), channel_id=1, source_target_pairs={{0,768},{1,257},{2,770},{3,259},{4,772},{5,261},{6,774},{7,263},{8... | collective-permute-start | bytes 1572872 | tf_op jit(solution)/shard_map/ppermute | solution.py:167
  30.5 17.2 %collective-permute-start.1 = (bf16[256,1024]{1,0:T(8,128)(2,1)S(1)}, bf16[256,1024]{1,0:T(8,128)(2,1)S(1)}, u32[]{:S(2)}, u32[]{:S(2)}) collective-permute-start(bf16[256,1024]{1,0:T(8,128)(2,1)S(1)} %add.58), channel_id=1, source_target_pairs={{0,768},{1,257},{2,770},{3,259},{4,772},{5,261},{6,774},{7,263},{8... | collective-permute-start | bytes 1572872 | tf_op jit(solution)/shard_map/ppermute | solution.py:167
  39.5 9.8 %collective-permute-start.7 = (bf16[256,1024]{1,0:T(8,128)(2,1)S(1)}, bf16[256,1024]{1,0:T(8,128)(2,1)S(1)}, u32[]{:S(2)}, u32[]{:S(2)}) collective-permute-start(bf16[256,1024]{1,0:T(8,128)(2,1)S(1)} %add.64), channel_id=1, source_target_pairs={{768,832},{257,193},{770,834},{259,195},{772,836},{261,197},{774,8... | collective-permute-start | bytes 1572872 | tf_op jit(solution)/shard_map/ppermute | solution.py:167
  47.9 10.8 %collective-permute-start.2 = (bf16[256,1024]{1,0:T(8,128)(2,1)S(1)}, bf16[256,1024]{1,0:T(8,128)(2,1)S(1)}, u32[]{:S(2)}, u32[]{:S(2)}) collective-permute-start(bf16[256,1024]{1,0:T(8,128)(2,1)S(1)} %add.59), channel_id=1, source_target_pairs={{768,832},{257,193},{770,834},{259,195},{772,836},{261,197},{774,8... | collective-permute-start | bytes 1572872 | tf_op jit(solution)/shard_map/ppermute | solution.py:167
  49.5 23.0 %copy-start = (bf16[1024,1024]{1,0:T(8,128)(2,1)S(1)}, bf16[1024,1024]{1,0:T(8,128)(2,1)}, u32[]{:S(2)}) copy-start(bf16[1024,1024]{1,0:T(8,128)(2,1)} %density_ref.1) | copy-start | bytes 6291460
  49.5 12.0 %collective-permute-start.8 = (bf16[256,1024]{1,0:T(8,128)(2,1)S(1)}, bf16[256,1024]{1,0:T(8,128)(2,1)S(1)}, u32[]{:S(2)}, u32[]{:S(2)}) collective-permute-start(bf16[256,1024]{1,0:T(8,128)(2,1)S(1)} %add.65), channel_id=1, source_target_pairs={{768,704},{257,321},{770,706},{259,323},{772,708},{261,325},{774,7... | collective-permute-start | bytes 1572872 | tf_op jit(solution)/shard_map/ppermute | solution.py:167
  58.9 12.0 %collective-permute-start.3 = (bf16[256,1024]{1,0:T(8,128)(2,1)S(1)}, bf16[256,1024]{1,0:T(8,128)(2,1)S(1)}, u32[]{:S(2)}, u32[]{:S(2)}) collective-permute-start(bf16[256,1024]{1,0:T(8,128)(2,1)S(1)} %add.60), channel_id=1, source_target_pairs={{768,704},{257,321},{770,706},{259,323},{772,708},{261,325},{774,7... | collective-permute-start | bytes 1572872 | tf_op jit(solution)/shard_map/ppermute | solution.py:167
  61.6 12.0 %collective-permute-start.9 = (bf16[256,1024]{1,0:T(8,128)(2,1)S(1)}, bf16[256,1024]{1,0:T(8,128)(2,1)S(1)}, u32[]{:S(2)}, u32[]{:S(2)}) collective-permute-start(bf16[256,1024]{1,0:T(8,128)(2,1)S(1)} %add.66), channel_id=1, source_target_pairs={{704,736},{321,289},{706,738},{323,291},{708,740},{325,293},{710,7... | collective-permute-start | bytes 1572872 | tf_op jit(solution)/shard_map/ppermute | solution.py:167
  71.1 11.2 %collective-permute-start.4 = (bf16[256,1024]{1,0:T(8,128)(2,1)S(1)}, bf16[256,1024]{1,0:T(8,128)(2,1)S(1)}, u32[]{:S(2)}, u32[]{:S(2)}) collective-permute-start(bf16[256,1024]{1,0:T(8,128)(2,1)S(1)} %add.61), channel_id=1, source_target_pairs={{704,736},{321,289},{706,738},{323,291},{708,740},{325,293},{710,7... | collective-permute-start | bytes 1572872 | tf_op jit(solution)/shard_map/ppermute | solution.py:167
  83.8 8.7 %collective-permute-start.10 = (bf16[256,1024]{1,0:T(8,128)(2,1)S(1)}, bf16[256,1024]{1,0:T(8,128)(2,1)S(1)}, u32[]{:S(2)}, u32[]{:S(2)}) collective-permute-start(bf16[256,1024]{1,0:T(8,128)(2,1)S(1)} %shard_map.39), channel_id=1, source_target_pairs={{0,1},{1,0},{2,3},{3,2},{4,5},{5,4},{6,7},{7,6},{8,9},{9,8},{10,11... | collective-permute-start | bytes 1572872 | tf_op jit(solution)/shard_map/ppermute | solution.py:172
  94.7 16.9 %all-to-all-start = ((bf16[16,16,1024]{2,1,0:T(8,128)(2,1)}), bf16[16,16,1024]{2,1,0:T(8,128)(2,1)S(1)}, u32[]{:S(2)}, u32[]{:S(2)}) async-start(bf16[16,16,1024]{2,1,0:T(8,128)(2,1)} %bitcast.2), calls=%async_computation | async-start | bytes 1048576 | tf_op jit(solution)/shard_map/all_to_all | solution.py:176
  125.7 3.8 %collective-permute-start.11 = (bf16[256,1024]{1,0:T(8,128)(2,1)S(1)}, bf16[256,1024]{1,0:T(8,128)(2,1)S(1)}, u32[]{:S(2)}, u32[]{:S(2)}) collective-permute-start(bf16[256,1024]{1,0:T(8,128)(2,1)S(1)} %bitcast.13), channel_id=1, source_target_pairs={{0,1},{1,0},{2,3},{3,2},{4,5},{5,4},{6,7},{7,6},{8,9},{9,8},{10,11... | collective-permute-start | bytes 1572872 | tf_op jit(solution)/shard_map/ppermute | solution.py:181
  132.2 9.7 %collective-permute-start.14 = (bf16[256,512]{1,0:T(8,128)(2,1)S(1)}, bf16[256,512]{1,0:T(8,128)(2,1)S(1)}, u32[]{:S(2)}, u32[]{:S(2)}) collective-permute-start(bf16[256,512]{1,0:T(8,128)(2,1)S(1)} %get-tuple-element.18), channel_id=1, source_target_pairs={{0,32},{1,993},{2,34},{3,995},{4,36},{5,997},{6,38},{7,999},{8,40}... | collective-permute-start | bytes 786440 | tf_op jit(solution)/shard_map/ppermute | solution.py:190
  137.9 9.5 %collective-permute-start.12 = (bf16[256,512]{1,0:T(8,128)(2,1)S(1)}, bf16[256,512]{1,0:T(8,128)(2,1)S(1)}, u32[]{:S(2)}, u32[]{:S(2)}) collective-permute-start(bf16[256,512]{1,0:T(8,128)(2,1)S(1)} %get-tuple-element.15), channel_id=1, source_target_pairs={{0,32},{1,993},{2,34},{3,995},{4,36},{5,997},{6,38},{7,999},{8,40}... | collective-permute-start | bytes 786440 | tf_op jit(solution)/shard_map/ppermute | solution.py:190
  141.9 10.6 %collective-permute-start.15 = (bf16[128,512]{1,0:T(8,128)(2,1)S(1)}, bf16[128,512]{1,0:T(8,128)(2,1)S(1)}, u32[]{:S(2)}, u32[]{:S(2)}) collective-permute-start(bf16[128,512]{1,0:T(8,128)(2,1)S(1)} %slice.18), channel_id=1, source_target_pairs={{0,64},{1,961},{2,66},{3,963},{4,68},{5,965},{6,70},{7,967},{8,72}... | collective-permute-start | bytes 393224 | tf_op jit(solution)/shard_map/ppermute | solution.py:191
  147.5 9.4 %collective-permute-start.13 = (bf16[128,512]{1,0:T(8,128)(2,1)S(1)}, bf16[128,512]{1,0:T(8,128)(2,1)S(1)}, u32[]{:S(2)}, u32[]{:S(2)}) collective-permute-start(bf16[128,512]{1,0:T(8,128)(2,1)S(1)} %slice.19), channel_id=1, source_target_pairs={{0,64},{1,961},{2,66},{3,963},{4,68},{5,965},{6,70},{7,967},{8,72}... | collective-permute-start | bytes 393224 | tf_op jit(solution)/shard_map/ppermute | solution.py:191
  158.1 60.6 %all-to-all-start.2 = ((bf16[8,16,1024]{2,1,0:T(8,128)(2,1)}), bf16[8,16,1024]{2,1,0:T(8,128)(2,1)S(1)}, u32[]{:S(2)}, u32[]{:S(2)}) async-start(bf16[8,16,1024]{2,1,0:T(8,128)(2,1)} %bitcast.6), calls=%async_computation.2 | async-start | bytes 524288 | tf_op jit(solution)/shard_map/all_to_all | solution.py:196

commit v3 on v2

v3 whole, which is shorter than its diff:
```python
import functools

import jax
import jax.numpy as jnp
from jax import lax
from jax.experimental import pallas as pl
from jax.experimental.pallas import tpu as pltpu
from jax.sharding import PartitionSpec as P

BS = 128
BF16 = jnp.bfloat16
F32 = jnp.float32
VMEM = pl.BlockSpec(memory_space=pltpu.VMEM)
SMEM = pl.BlockSpec(memory_space=pltpu.SMEM)
BOTH = ("row", "col")
STEPS = (2, 1, -1, 0)


def call(kernel, outs, cost, scratch=()):
    return functools.partial(
        pl.pallas_call,
        kernel,
        out_shape=outs,
        out_specs=jax.tree.map(lambda _: VMEM, outs),
        scratch_shapes=list(scratch),
        compiler_params=pltpu.CompilerParams(vmem_limit_bytes=24 * 2**20),
        cost_estimate=pl.CostEstimate(flops=cost, bytes_accessed=4 * 2**20, transcendentals=0),
    )


def panel_kernel(where_ref, occ_ref, density_ref, mine_ref, sent_ref):
    first = where_ref[0] == 0
    core = where_ref[1] % 2
    blocks = mine_ref.shape[0] // BS
    for half, out_ref in ((core, mine_ref), (1 - core, sent_ref)):
        for i in range(blocks):
            down = half * blocks + i
            rows = pl.ds(pl.multiple_of(down * BS, BS), BS)
            for j in range(occ_ref.shape[1]):
                across = pl.ds(j * BS, BS)
                kept = density_ref[rows, across] * occ_ref[down, j].astype(F32).astype(BF16)
                out_ref[pl.ds(i * BS, BS), across] = jnp.where(first, kept, jnp.zeros_like(kept))


def mask_kernel(occ_ref, density_ref, sparse_ref):
    for i in range(occ_ref.shape[0]):
        for j in range(occ_ref.shape[1]):
            spot = (pl.ds(i * BS, BS), pl.ds(j * BS, BS))
            sparse_ref[spot] = density_ref[spot] * occ_ref[i, j].astype(F32).astype(BF16)


def square_part(left_ref, sparse_ref, n):
    return lax.dot_general(
        left_ref[...], sparse_ref[n, :], (((1,), (1,)), ((), ())), preferred_element_type=F32
    )


def tiles(size):
    tile = min(256, size)
    return [pl.ds(n, tile) for n in range(0, size, tile)]


def own_kernel(left_ref, sparse_ref, total_ref):
    for n in tiles(sparse_ref.shape[0]):
        total_ref[:, n] = square_part(left_ref, sparse_ref, n)


def both_kernel(left_ref, sparse_ref, total_ref, out_ref):
    for n in tiles(sparse_ref.shape[0]):
        out_ref[:, n] = (total_ref[:, n] + square_part(left_ref, sparse_ref, n)).astype(BF16)


def cube_part(where_ref, left_ref, sparse_ref, first, low_ref, high_ref):
    three = jnp.where(where_ref[0] == where_ref[1], 3.0, 0.0).astype(F32)
    size = low_ref.shape[0]
    rows = pl.ds(first, 2 * size)
    for n in tiles(low_ref.shape[1]):
        product = jnp.dot(left_ref[rows, :], sparse_ref[:, n], preferred_element_type=F32)
        total = three * left_ref[rows, n].astype(F32) - 2.0 * product
        low_ref[:, n] = total[:size].astype(low_ref.dtype)
        high_ref[:, n] = total[size:].astype(high_ref.dtype)


def first_kernel(rows, where_ref, mine_ref, other_ref, sparse_ref, left_ref, low_ref, high_ref):
    row, core = where_ref[0], where_ref[1] % 2
    sign = 1 - 2 * core
    piece = left_ref.shape[0] // rows
    half = rows // 2
    order = [(t + rows) % rows for start in STEPS for t in range(start, start + rows, 4)]
    for place, t in enumerate(order):
        target = (row + sign * t + rows) % rows
        source = pl.ds(pl.multiple_of((target % half) * piece, piece), piece)
        spot = pl.ds(place * piece, piece)
        left_ref[spot, :] = jnp.where(target // half == core, mine_ref[source, :], other_ref[source, :])
    cube_part(where_ref, left_ref, sparse_ref, 0, low_ref, high_ref)


def second_kernel(where_ref, left_ref, sparse_ref, low_ref, high_ref):
    cube_part(where_ref, left_ref, sparse_ref, 2 * low_ref.shape[0], low_ref, high_ref)


def order_kernel(groups, where_ref, kept_ref, *refs):
    *got_refs, out_ref = refs
    row, col = where_ref[0], where_ref[1]
    sign = 1 - 2 * (col % 2)
    piece = out_ref.shape[0] // groups
    for u in range(groups):
        place = (row // 4 + sign * u + groups) % groups
        source = pl.ds(u * piece, piece)
        total = kept_ref[source, :]
        for got_ref in got_refs:
            total += got_ref[source, :].astype(F32)
        out_ref[pl.ds(pl.multiple_of(place * piece, piece), piece), :] = total.astype(BF16)


def body(rows, cols, density, occupancy, product_keep):
    rows_here, cols_here = density.shape
    window = product_keep.shape[0] * BS
    row, col = lax.axis_index("row"), lax.axis_index("col")
    where = jnp.stack([row, col]).astype(jnp.int32)
    half = window // 2
    piece = window // rows
    chips = cols // 2
    tall = jax.ShapeDtypeStruct
    work = window * rows_here * cols_here

    def pairs(moves):
        return [
            (z * sign % rows * cols + c, (z + step) * sign % rows * cols + c)
            for z, step in moves
            for c in range(cols)
            for sign in [1 - 2 * (c % 2)]
        ]

    same_core = [[2 * i + k for i in range(chips)] for k in range(2)]
    groups = rows // 4
    strided = [[4 * i + o for i in range(groups)] for o in range(4)]

    def mask(across, down_first, across_first):
        kept = lax.dynamic_slice(product_keep, (down_first, across_first), (1, across))
        return jnp.repeat(kept, BS, axis=1).astype(F32)

    swap = [(c, c ^ 1) for c in range(cols)]
    mine, sent = call(panel_kernel, [tall((half, cols_here), BF16)] * 2, 10**6)(in_specs=[SMEM, SMEM, VMEM])(
        where, occupancy, density[:window]
    )
    halves = [mine, lax.ppermute(sent, BOTH, swap)]
    sparse = call(mask_kernel, tall(density.shape, BF16), 10**6)(in_specs=[SMEM, VMEM])(occupancy, density)
    sibling = lax.ppermute(sparse, "col", swap)

    have, gap, stages = [0], rows, []
    while gap > 2:
        gap //= 4
        stages.append([(z, gap) for z in have])
        stages.append([(z, -gap) for z in have] + [(z + gap, gap) for z in have])
        have = [z + step * gap for z in have for step in (-1, 0, 1, 2)]
    stages.append([(z, 1) for z in have])
    for moves in stages:
        halves = [h + lax.ppermute(h, BOTH, pairs(moves)) for h in halves]

    total = call(own_kernel, tall((half, rows_here), F32), work)(in_specs=[VMEM] * 2)(halves[0], sparse)
    kept = call(both_kernel, tall((half, rows_here), BF16), work)(in_specs=[VMEM] * 3)(halves[1], sibling, total)
    parts = lax.all_to_all(kept.reshape(chips, piece, rows_here), "col", 0, 0, axis_index_groups=same_core, tiled=True)
    first = (col % 2) * half + (col // 2) * piece
    square = parts.astype(F32).sum(0) * mask(rows_here // BS, first // BS, row * (rows_here // BS))
    square = jnp.broadcast_to(square.astype(BF16), (chips, piece, rows_here))
    mine = lax.all_to_all(square, "col", 0, 0, axis_index_groups=same_core, tiled=True).reshape(half, rows_here)
    other = lax.ppermute(mine, "col", swap)

    quarter = tall((window // 4, cols_here), BF16)
    left, *sent = call(
        functools.partial(first_kernel, rows), (tall((window, rows_here), BF16), quarter, quarter), work
    )(in_specs=[SMEM, VMEM, VMEM, VMEM])(where, mine, other, sparse)
    last, kept = call(second_kernel, (quarter, tall(quarter.shape, F32)), work)(in_specs=[SMEM, VMEM, VMEM])(
        where, left, sparse
    )
    got = [
        lax.ppermute(part, BOTH, pairs([(z, step) for z in range(rows)]))
        for part, step in zip((*sent, last), STEPS)
    ]
    ready = call(functools.partial(order_kernel, groups), quarter, 10**6)(in_specs=[SMEM] + [VMEM] * 4)(
        where, kept, *got
    )
    parts = lax.all_to_all(ready.reshape(groups, piece, cols_here), "row", 0, 0, axis_index_groups=strided, tiled=True)
    result = parts.astype(F32).sum(0)
    result = result * mask(cols_here // BS, row * piece // BS, col * (cols_here // BS))
    return result.astype(BF16)


def solution(mesh):
    rows, cols = mesh.shape["row"], mesh.shape["col"]
    return jax.shard_map(
        functools.partial(body, rows, cols),
        mesh=mesh,
        in_specs=(P("row", "col"), P("row", "col"), P()),
        out_specs=P("row", "col"),
        check_vma=False,
    )
```

time: 221 us -> 206 us (0.932)
  the two profiles are of different devices: /device:TPU:6 before, /device:TPU:33 now
where the time goes in v3:
time: 206 us; the launch traced here: 205 us
  waiting for transfers between devices  127 us (62%)
  starting transfers between devices  52.8 us (26%)
  blocking collectives  11.6 us (6%)
  Pallas kernels  8.46 us (4%)
  other arithmetic  3.57 us (2%)
    ppermute x10, waiting for transfers between devices, body(): halves = [h + lax.ppermute(h, BOTH, pairs(moves)) for h in halves]  70.7 us
    all_to_all x1, waiting for transfers between devices, body(): lax.all_to_all(ready.reshape(groups, piece, cols_here), 'row', 0, 0, axis...  38.7 us
    all_to_all x1, starting transfers between devices, body(): lax.all_to_all(ready.reshape(groups, piece, cols_here), 'row', 0, 0, axis...  15.2 us
    all_to_all x1, blocking collectives, body(): lax.all_to_all(square, 'col', 0, 0, axis_index_groups=same_core, tiled=True)  11.6 us
    ppermute x3, starting transfers between devices, body(): lax.ppermute(part, BOTH, pairs([(z, step) for z in range(rows)]))  11.5 us
    all_to_all x1, waiting for transfers between devices, body(): lax.all_to_all(kept.reshape(chips, piece, rows_here), 'col', 0, 0, axis_i...  8.31 us
    ppermute x10, starting transfers between devices, body(): halves = [h + lax.ppermute(h, BOTH, pairs(moves)) for h in halves]  8.14 us
    ppermute x1, starting transfers between devices, body(): other = lax.ppermute(mine, 'col', swap)  7.98 us
  transfers between devices with their start and end apart: 18, of which 7 were waited for; matrix products, arithmetic and copies ran while one was open for 1% of the time, Pallas kernels for 1%

profile of v3, /device:TPU:33, one launch (start us, length us, event | category | flops | bytes accessed | tf_op | source)
XLA Modules:
  0.0 205.0 jit_solution(3441756086068521745)
XLA Ops:
  0.0 1.3 slice.3.density_ref
  1.3 0.1 pad_add_fusion.where_ref
  1.4 0.0 copy-done.1
  1.4 0.9 shard_map.37
  2.3 0.7 collective-permute-start
  3.0 0.7 collective-permute-start.7
  3.7 0.0 collective-permute-done
  3.7 0.7 collective-permute-start.1
  4.4 0.0 collective-permute-done.7
  4.4 0.2 add.57
  4.6 0.7 collective-permute-start.8
  5.3 0.0 collective-permute-done.1
  5.4 0.2 add.52
  5.6 0.7 collective-permute-start.2
  6.3 0.0 copy-done
  6.3 1.2 shard_map.38.sparse_ref
  7.4 2.6 %collective-permute-start.6 = (bf16[1024,1024]{1,0:T(8,128)(2,1)S(1)}, bf16[1024,1024]{1,0:T(8,128)(2,1)S(1)}, u32[]{:S(2)}, u32[]{:S(2)}) collective-permute-start(bf16[1024,1024]{1,0:T(8,128)(2,1)S(1)} %shard_map.38.sparse_ref), channel_id=1, source_target_pairs={{0,1},{1,0},{2,3},{3,2},{4,5},{5,4},{6,7},{7,6},{8,9},{9,8},{10,11... | collective-permute-start | bytes 6291464 | tf_op jit(solution)/shard_map/ppermute | solution.py:149
  10.0 0.0 collective-permute-done.8
  10.0 0.2 add.58
  10.2 0.7 collective-permute-start.9
  10.9 0.0 collective-permute-done.2
  11.0 0.2 add.53
  11.2 0.7 collective-permute-start.3
  11.9 0.0 collective-permute-done.9
  11.9 0.2 add.59
  12.1 0.7 collective-permute-start.10
  12.8 0.0 collective-permute-done.3
  12.8 0.2 add.54
  13.0 0.7 collective-permute-start.4
  13.7 0.0 collective-permute-done.10
  13.7 0.2 add.60
  13.9 1.3 collective-permute-start.11
  15.2 0.0 collective-permute-done.4
  15.2 0.2 add.55
  15.4 1.3 collective-permute-start.5
  16.7 63.4 %collective-permute-done.11 = bf16[256,1024]{1,0:T(8,128)(2,1)S(1)} collective-permute-done((bf16[256,1024]{1,0:T(8,128)(2,1)S(1)}, bf16[256,1024]{1,0:T(8,128)(2,1)S(1)}, u32[]{:S(2)}, u32[]{:S(2)}) %collective-permute-start.11) | collective-permute-done | bytes 524320 | tf_op jit(solution)/shard_map/ppermute | solution.py:159
  80.1 0.2 add.61.left_ref
  80.3 0.7 shard_map.39.total_ref
  81.1 7.2 %collective-permute-done.5 = bf16[256,1024]{1,0:T(8,128)(2,1)S(1)} collective-permute-done((bf16[256,1024]{1,0:T(8,128)(2,1)S(1)}, bf16[256,1024]{1,0:T(8,128)(2,1)S(1)}, u32[]{:S(2)}, u32[]{:S(2)}) %collective-permute-start.5) | collective-permute-done | bytes 524320 | tf_op jit(solution)/shard_map/ppermute | solution.py:159
  88.3 0.2 add.56.left_ref
  88.5 0.0 collective-permute-done.6.sparse_ref
  88.5 1.5 shard_map.40
  90.0 6.8 %all-to-all-start = ((bf16[16,16,1024]{2,1,0:T(8,128)(2,1)}), bf16[16,16,1024]{2,1,0:T(8,128)(2,1)S(1)}, u32[]{:S(2)}, u32[]{:S(2)}) async-start(bf16[16,16,1024]{2,1,0:T(8,128)(2,1)} %bitcast.2), calls=%async_computation | async-start | bytes 1048576 | tf_op jit(solution)/shard_map/all_to_all | solution.py:163
  96.8 0.8 convert_bitcast_fusion
  97.7 0.1 broadcast_bitcast_fusion.1
  97.8 8.3 %all-to-all-done = bf16[16,16,1024]{2,1,0:T(8,128)(2,1)S(1)} async-done(((bf16[16,16,1024]{2,1,0:T(8,128)(2,1)}), bf16[16,16,1024]{2,1,0:T(8,128)(2,1)S(1)}, u32[]{:S(2)}, u32[]{:S(2)}) %all-to-all-start) | async-done | bytes 524320 | tf_op jit(solution)/shard_map/all_to_all | solution.py:163
  106.1 0.1 convert_reduce_fusion
  106.2 0.1 broadcast_in_dim.10
  106.2 11.6 %all_to_all.15 = bf16[16,16,1024]{2,1,0:T(8,128)(2,1)S(1)} all-to-all(bf16[16,16,1024]{2,1,0:T(8,128)(2,1)S(1)} %broadcast_in_dim.10), channel_id=1, replica_groups={{0,2,4,6,8,10,12,14,16,18,20,22,24,26,28,30},{1,3,5,7,9,11,13,15,17,19,..., dimensions={0} | all-to-all | bytes 1048576 | tf_op jit(solution)/shard_map/all_to_all | solution.py:167
  117.8 8.0 %collective-permute-start.12 = (bf16[256,1024]{1,0:T(8,128)(2,1)S(1)}, bf16[256,1024]{1,0:T(8,128)(2,1)S(1)}, u32[]{:S(2)}, u32[]{:S(2)}) collective-permute-start(bf16[256,1024]{1,0:T(8,128)(2,1)S(1)} %bitcast.13), channel_id=1, source_target_pairs={{0,1},{1,0},{2,3},{3,2},{4,5},{5,4},{6,7},{7,6},{8,9},{9,8},{10,11... | collective-permute-start | bytes 1572872 | tf_op jit(solution)/shard_map/ppermute | solution.py:168
  125.8 1.5 collective-permute-done.12.other_ref
  127.3 1.5 shard_map.41
  128.8 1.3 shard_map.42
  130.1 1.9 collective-permute-start.15
  132.0 6.2 %collective-permute-start.13 = (bf16[128,1024]{1,0:T(8,128)(2,1)S(1)}, bf16[128,1024]{1,0:T(8,128)(2,1)S(1)}, u32[]{:S(2)}, u32[]{:S(2)}) collective-permute-start(bf16[128,1024]{1,0:T(8,128)(2,1)S(1)} %get-tuple-element.16), channel_id=1, source_target_pairs={{0,64},{1,961},{2,66},{3,963},{4,68},{5,965},{6,70},{7,967},{8,72}... | collective-permute-start | bytes 786440 | tf_op jit(solution)/shard_map/ppermute | solution.py:178
  138.3 3.4 %collective-permute-start.14 = (bf16[128,1024]{1,0:T(8,128)(2,1)S(1)}, bf16[128,1024]{1,0:T(8,128)(2,1)S(1)}, u32[]{:S(2)}, u32[]{:S(2)}) collective-permute-start(bf16[128,1024]{1,0:T(8,128)(2,1)S(1)} %get-tuple-element.17), channel_id=1, source_target_pairs={{0,32},{1,993},{2,34},{3,995},{4,36},{5,997},{6,38},{7,999},{8,40}... | collective-permute-start | bytes 786440 | tf_op jit(solution)/shard_map/ppermute | solution.py:178
  141.6 0.0 collective-permute-done.15.refs_2_
  141.6 3.1 %collective-permute-done.13.refs_0_ = bf16[128,1024]{1,0:T(8,128)(2,1)S(1)} collective-permute-done((bf16[128,1024]{1,0:T(8,128)(2,1)S(1)}, bf16[128,1024]{1,0:T(8,128)(2,1)S(1)}, u32[]{:S(2)}, u32[]{:S(2)}) %collective-permute-start.13) | collective-permute-done | bytes 262176 | tf_op jit(solution)/shard_map/ppermute | solution.py:178
  144.7 4.3 %collective-permute-done.14.refs_1_ = bf16[128,1024]{1,0:T(8,128)(2,1)S(1)} collective-permute-done((bf16[128,1024]{1,0:T(8,128)(2,1)S(1)}, bf16[128,1024]{1,0:T(8,128)(2,1)S(1)}, u32[]{:S(2)}, u32[]{:S(2)}) %collective-permute-start.14) | collective-permute-done | bytes 262176 | tf_op jit(solution)/shard_map/ppermute | solution.py:178
  149.0 1.4 shard_map.43
  150.3 15.2 %all-to-all-start.2 = ((bf16[8,16,1024]{2,1,0:T(8,128)(2,1)}), bf16[8,16,1024]{2,1,0:T(8,128)(2,1)S(1)}, u32[]{:S(2)}, u32[]{:S(2)}) async-start(bf16[8,16,1024]{2,1,0:T(8,128)(2,1)} %bitcast.6), calls=%async_computation.2 | async-start | bytes 524288 | tf_op jit(solution)/shard_map/all_to_all | solution.py:184
  165.5 0.1 broadcast_bitcast_fusion
  165.6 38.7 %all-to-all-done.2 = bf16[8,16,1024]{2,1,0:T(8,128)(2,1)S(1)} async-done(((bf16[8,16,1024]{2,1,0:T(8,128)(2,1)}), bf16[8,16,1024]{2,1,0:T(8,128)(2,1)S(1)}, u32[]{:S(2)}, u32[]{:S(2)}) %all-to-all-start.2) | async-done | bytes 262176 | tf_op jit(solution)/shard_map/all_to_all | solution.py:184
  204.3 0.6 multiply_convert_fusion
  (4 shorter events, 0.1 us)
Async XLA Ops:
  0.0 1.4 copy-start.1
  1.4 4.9 %copy-start = (bf16[1024,1024]{1,0:T(8,128)(2,1)S(1)}, bf16[1024,1024]{1,0:T(8,128)(2,1)}, u32[]{:S(2)}) copy-start(bf16[1024,1024]{1,0:T(8,128)(2,1)} %density_ref.1) | copy-start | bytes 6291460
  2.3 1.4 collective-permute-start
  3.0 1.4 collective-permute-start.7
  3.7 1.6 collective-permute-start.1
  4.6 5.4 %collective-permute-start.8 = (bf16[256,1024]{1,0:T(8,128)(2,1)S(1)}, bf16[256,1024]{1,0:T(8,128)(2,1)S(1)}, u32[]{:S(2)}, u32[]{:S(2)}) collective-permute-start(bf16[256,1024]{1,0:T(8,128)(2,1)S(1)} %add.57), channel_id=1, source_target_pairs={{0,768},{1,257},{2,770},{3,259},{4,772},{5,261},{6,774},{7,263},{8... | collective-permute-start | bytes 1572872 | tf_op jit(solution)/shard_map/ppermute | solution.py:159
  5.6 5.4 %collective-permute-start.2 = (bf16[256,1024]{1,0:T(8,128)(2,1)S(1)}, bf16[256,1024]{1,0:T(8,128)(2,1)S(1)}, u32[]{:S(2)}, u32[]{:S(2)}) collective-permute-start(bf16[256,1024]{1,0:T(8,128)(2,1)S(1)} %add.52), channel_id=1, source_target_pairs={{0,768},{1,257},{2,770},{3,259},{4,772},{5,261},{6,774},{7,263},{8... | collective-permute-start | bytes 1572872 | tf_op jit(solution)/shard_map/ppermute | solution.py:159
  7.4 81.0 %collective-permute-start.6 = (bf16[1024,1024]{1,0:T(8,128)(2,1)S(1)}, bf16[1024,1024]{1,0:T(8,128)(2,1)S(1)}, u32[]{:S(2)}, u32[]{:S(2)}) collective-permute-start(bf16[1024,1024]{1,0:T(8,128)(2,1)S(1)} %shard_map.38.sparse_ref), channel_id=1, source_target_pairs={{0,1},{1,0},{2,3},{3,2},{4,5},{5,4},{6,7},{7,6},{8,9},{9,8},{10,11... | collective-permute-start | bytes 6291464 | tf_op jit(solution)/shard_map/ppermute | solution.py:149
  10.2 1.6 collective-permute-start.9
  11.2 1.6 collective-permute-start.3
  12.1 1.6 collective-permute-start.10
  13.0 2.2 %collective-permute-start.4 = (bf16[256,1024]{1,0:T(8,128)(2,1)S(1)}, bf16[256,1024]{1,0:T(8,128)(2,1)S(1)}, u32[]{:S(2)}, u32[]{:S(2)}) collective-permute-start(bf16[256,1024]{1,0:T(8,128)(2,1)S(1)} %add.54), channel_id=1, source_target_pairs={{768,704},{257,321},{770,706},{259,323},{772,708},{261,325},{774,7... | collective-permute-start | bytes 1572872 | tf_op jit(solution)/shard_map/ppermute | solution.py:159
  13.9 66.2 %collective-permute-start.11 = (bf16[256,1024]{1,0:T(8,128)(2,1)S(1)}, bf16[256,1024]{1,0:T(8,128)(2,1)S(1)}, u32[]{:S(2)}, u32[]{:S(2)}) collective-permute-start(bf16[256,1024]{1,0:T(8,128)(2,1)S(1)} %add.60), channel_id=1, source_target_pairs={{704,736},{321,289},{706,738},{323,291},{708,740},{325,293},{710,7... | collective-permute-start | bytes 1572872 | tf_op jit(solution)/shard_map/ppermute | solution.py:159
  15.4 72.9 %collective-permute-start.5 = (bf16[256,1024]{1,0:T(8,128)(2,1)S(1)}, bf16[256,1024]{1,0:T(8,128)(2,1)S(1)}, u32[]{:S(2)}, u32[]{:S(2)}) collective-permute-start(bf16[256,1024]{1,0:T(8,128)(2,1)S(1)} %add.55), channel_id=1, source_target_pairs={{704,736},{321,289},{706,738},{323,291},{708,740},{325,293},{710,7... | collective-permute-start | bytes 1572872 | tf_op jit(solution)/shard_map/ppermute | solution.py:159
  90.0 16.1 %all-to-all-start = ((bf16[16,16,1024]{2,1,0:T(8,128)(2,1)}), bf16[16,16,1024]{2,1,0:T(8,128)(2,1)S(1)}, u32[]{:S(2)}, u32[]{:S(2)}) async-start(bf16[16,16,1024]{2,1,0:T(8,128)(2,1)} %bitcast.2), calls=%async_computation | async-start | bytes 1048576 | tf_op jit(solution)/shard_map/all_to_all | solution.py:163
  117.8 9.5 %collective-permute-start.12 = (bf16[256,1024]{1,0:T(8,128)(2,1)S(1)}, bf16[256,1024]{1,0:T(8,128)(2,1)S(1)}, u32[]{:S(2)}, u32[]{:S(2)}) collective-permute-start(bf16[256,1024]{1,0:T(8,128)(2,1)S(1)} %bitcast.13), channel_id=1, source_target_pairs={{0,1},{1,0},{2,3},{3,2},{4,5},{5,4},{6,7},{7,6},{8,9},{9,8},{10,11... | collective-permute-start | bytes 1572872 | tf_op jit(solution)/shard_map/ppermute | solution.py:168
  130.1 11.5 %collective-permute-start.15 = (bf16[128,1024]{1,0:T(8,128)(2,1)S(1)}, bf16[128,1024]{1,0:T(8,128)(2,1)S(1)}, u32[]{:S(2)}, u32[]{:S(2)}) collective-permute-start(bf16[128,1024]{1,0:T(8,128)(2,1)S(1)} %get-tuple-element.18), channel_id=1, source_target_pairs={{0,992},{1,33},{2,994},{3,35},{4,996},{5,37},{6,998},{7,39},{8,100... | collective-permute-start | bytes 786440 | tf_op jit(solution)/shard_map/ppermute | solution.py:178
  132.0 12.7 %collective-permute-start.13 = (bf16[128,1024]{1,0:T(8,128)(2,1)S(1)}, bf16[128,1024]{1,0:T(8,128)(2,1)S(1)}, u32[]{:S(2)}, u32[]{:S(2)}) collective-permute-start(bf16[128,1024]{1,0:T(8,128)(2,1)S(1)} %get-tuple-element.16), channel_id=1, source_target_pairs={{0,64},{1,961},{2,66},{3,963},{4,68},{5,965},{6,70},{7,967},{8,72}... | collective-permute-start | bytes 786440 | tf_op jit(solution)/shard_map/ppermute | solution.py:178
  138.3 10.7 %collective-permute-start.14 = (bf16[128,1024]{1,0:T(8,128)(2,1)S(1)}, bf16[128,1024]{1,0:T(8,128)(2,1)S(1)}, u32[]{:S(2)}, u32[]{:S(2)}) collective-permute-start(bf16[128,1024]{1,0:T(8,128)(2,1)S(1)} %get-tuple-element.17), channel_id=1, source_target_pairs={{0,32},{1,993},{2,34},{3,995},{4,36},{5,997},{6,38},{7,999},{8,40}... | collective-permute-start | bytes 786440 | tf_op jit(solution)/shard_map/ppermute | solution.py:178
  150.3 54.0 %all-to-all-start.2 = ((bf16[8,16,1024]{2,1,0:T(8,128)(2,1)}), bf16[8,16,1024]{2,1,0:T(8,128)(2,1)S(1)}, u32[]{:S(2)}, u32[]{:S(2)}) async-start(bf16[8,16,1024]{2,1,0:T(8,128)(2,1)} %bitcast.6), calls=%async_computation.2 | async-start | bytes 524288 | tf_op jit(solution)/shard_map/all_to_all | solution.py:184

commit v4 on v3

--- a/solution.py
+++ b/solution.py
@@ -16,30 +16,36 @@
 STEPS = (2, 1, -1, 0)
 
 
-def call(kernel, outs, cost, scratch=()):
+def call(kernel, outs, cost):
     return functools.partial(
         pl.pallas_call,
         kernel,
         out_shape=outs,
         out_specs=jax.tree.map(lambda _: VMEM, outs),
-        scratch_shapes=list(scratch),
         compiler_params=pltpu.CompilerParams(vmem_limit_bytes=24 * 2**20),
         cost_estimate=pl.CostEstimate(flops=cost, bytes_accessed=4 * 2**20, transcendentals=0),
     )
 
 
-def panel_kernel(where_ref, occ_ref, density_ref, mine_ref, sent_ref):
-    first = where_ref[0] == 0
+def panel_kernel(where_ref, occ_ref, window_ref, mine_ref, sent_ref):
     core = where_ref[1] % 2
     blocks = mine_ref.shape[0] // BS
-    for half, out_ref in ((core, mine_ref), (1 - core, sent_ref)):
-        for i in range(blocks):
-            down = half * blocks + i
-            rows = pl.ds(pl.multiple_of(down * BS, BS), BS)
-            for j in range(occ_ref.shape[1]):
-                across = pl.ds(j * BS, BS)
-                kept = density_ref[rows, across] * occ_ref[down, j].astype(F32).astype(BF16)
-                out_ref[pl.ds(i * BS, BS), across] = jnp.where(first, kept, jnp.zeros_like(kept))
+
+    @pl.when(where_ref[0] != 0)
+    def _():
+        mine_ref[...] = jnp.zeros_like(mine_ref)
+        sent_ref[...] = jnp.zeros_like(sent_ref)
+
+    @pl.when(where_ref[0] == 0)
+    def _():
+        for half, out_ref in ((core, mine_ref), (1 - core, sent_ref)):
+            for i in range(blocks):
+                down = half * blocks + i
+                rows = pl.ds(pl.multiple_of(down * BS, BS), BS)
+                for j in range(occ_ref.shape[1]):
+                    across = pl.ds(j * BS, BS)
+                    kept = window_ref[rows, across] * occ_ref[down, j].astype(F32).astype(BF16)
+                    out_ref[pl.ds(i * BS, BS), across] = kept
 
 
 def mask_kernel(occ_ref, density_ref, sparse_ref):
@@ -99,13 +105,17 @@
     cube_part(where_ref, left_ref, sparse_ref, 2 * low_ref.shape[0], low_ref, high_ref)
 
 
+def spread(member, groups):
+    return (member + (1 - member % 2) * (groups // 2)) % groups if groups % 4 == 0 else member
+
+
 def order_kernel(groups, where_ref, kept_ref, *refs):
     *got_refs, out_ref = refs
     row, col = where_ref[0], where_ref[1]
     sign = 1 - 2 * (col % 2)
     piece = out_ref.shape[0] // groups
     for u in range(groups):
-        place = (row // 4 + sign * u + groups) % groups
+        place = spread((row // 4 + sign * u + groups) % groups, groups)
         source = pl.ds(u * piece, piece)
         total = kept_ref[source, :]
         for got_ref in got_refs:
@@ -124,30 +134,32 @@
     tall = jax.ShapeDtypeStruct
     work = window * rows_here * cols_here
 
-    def pairs(moves):
+    def pairs(moves, way=1):
         return [
             (z * sign % rows * cols + c, (z + step) * sign % rows * cols + c)
             for z, step in moves
             for c in range(cols)
-            for sign in [1 - 2 * (c % 2)]
+            for sign in [way * (1 - 2 * (c % 2))]
         ]
 
     same_core = [[2 * i + k for i in range(chips)] for k in range(2)]
     groups = rows // 4
-    strided = [[4 * i + o for i in range(groups)] for o in range(4)]
+    members = sorted(range(groups), key=lambda i: spread(i, groups))
+    strided = [[4 * i + o for i in members] for o in range(4)]
 
     def mask(across, down_first, across_first):
         kept = lax.dynamic_slice(product_keep, (down_first, across_first), (1, across))
         return jnp.repeat(kept, BS, axis=1).astype(F32)
 
     swap = [(c, c ^ 1) for c in range(cols)]
-    mine, sent = call(panel_kernel, [tall((half, cols_here), BF16)] * 2, 10**6)(in_specs=[SMEM, SMEM, VMEM])(
-        where, occupancy, density[:window]
-    )
+    mine, sent = call(
+        panel_kernel,
+        [tall((half, cols_here), BF16)] * 2,
+        10**6,
+    )(in_specs=[SMEM, SMEM, VMEM])(where, occupancy, density[:window])
     halves = [mine, lax.ppermute(sent, BOTH, swap)]
     sparse = call(mask_kernel, tall(density.shape, BF16), 10**6)(in_specs=[SMEM, VMEM])(occupancy, density)
     sibling = lax.ppermute(sparse, "col", swap)
-
     have, gap, stages = [0], rows, []
     while gap > 2:
         gap //= 4
@@ -156,7 +168,7 @@
         have = [z + step * gap for z in have for step in (-1, 0, 1, 2)]
     stages.append([(z, 1) for z in have])
     for moves in stages:
-        halves = [h + lax.ppermute(h, BOTH, pairs(moves)) for h in halves]
+        halves = [h + lax.ppermute(h, BOTH, pairs(moves, way)) for h, way in zip(halves, (1, -1))]
 
     total = call(own_kernel, tall((half, rows_here), F32), work)(in_specs=[VMEM] * 2)(halves[0], sparse)
     kept = call(both_kernel, tall((half, rows_here), BF16), work)(in_specs=[VMEM] * 3)(halves[1], sibling, total)

time: 206 us -> 199 us (0.966)
  the two profiles are of different devices: /device:TPU:33 before, /device:TPU:6 now
where the time goes in v4:
time: 199 us; the launch traced here: 195 us
  starting transfers between devices  95.2 us (48%)
  waiting for transfers between devices  73.1 us (37%)
  blocking collectives  13.1 us (7%)
  Pallas kernels  8.46 us (4%)
  other arithmetic  3.55 us (2%)
    ppermute x10, starting transfers between devices, body(): lax.ppermute(h, BOTH, pairs(moves, way))  37.3 us
    ppermute x10, waiting for transfers between devices, body(): lax.ppermute(h, BOTH, pairs(moves, way))  33.9 us
    all_to_all x1, starting transfers between devices, body(): lax.all_to_all(ready.reshape(groups, piece, cols_here), 'row', 0, 0, axis...  22.7 us
    all_to_all x1, waiting for transfers between devices, body(): lax.all_to_all(ready.reshape(groups, piece, cols_here), 'row', 0, 0, axis...  21.9 us
    all_to_all x1, blocking collectives, body(): lax.all_to_all(square, 'col', 0, 0, axis_index_groups=same_core, tiled=True)  13.1 us
    ppermute x3, starting transfers between devices, body(): lax.ppermute(part, BOTH, pairs([(z, step) for z in range(rows)]))  12.3 us
    ppermute x1, starting transfers between devices, body(): sibling = lax.ppermute(sparse, 'col', swap)  11.6 us
    ppermute x3, waiting for transfers between devices, body(): lax.ppermute(part, BOTH, pairs([(z, step) for z in range(rows)]))  7.85 us
  transfers between devices with their start and end apart: 18, of which 12 were waited for; matrix products, arithmetic and copies ran while one was open for 1% of the time, Pallas kernels for 1%

profile of v4, /device:TPU:6, one launch (start us, length us, event | category | flops | bytes accessed | tf_op | source)
XLA Modules:
  0.0 195.2 jit_solution(1179461950289497355)
XLA Ops:
  0.0 1.3 slice.3.window_ref
  1.3 0.1 pad_add_fusion.where_ref
  1.4 0.0 copy-done.1
  1.4 0.9 shard_map.37
  2.3 1.9 collective-permute-start
  4.2 14.3 %collective-permute-start.7 = (bf16[256,1024]{1,0:T(8,128)(2,1)S(1)}, bf16[256,1024]{1,0:T(8,128)(2,1)S(1)}, u32[]{:S(2)}, u32[]{:S(2)}) collective-permute-start(bf16[256,1024]{1,0:T(8,128)(2,1)S(1)} %get-tuple-element.13), channel_id=1, source_target_pairs={{0,256},{1,769},{2,258},{3,771},{4,260},{5,773},{6,262},{7,775},{8... | collective-permute-start | bytes 1572872 | tf_op jit(solution)/shard_map/ppermute | solution.py:171
  18.5 0.0 collective-permute-done
  18.6 8.0 %collective-permute-start.1 = (bf16[256,1024]{1,0:T(8,128)(2,1)S(1)}, bf16[256,1024]{1,0:T(8,128)(2,1)S(1)}, u32[]{:S(2)}, u32[]{:S(2)}) collective-permute-start(bf16[256,1024]{1,0:T(8,128)(2,1)S(1)} %collective-permute-done), channel_id=1, source_target_pairs={{0,768},{1,257},{2,770},{3,259},{4,772},{5,261},{6,774},{7,263},{8... | collective-permute-start | bytes 1572872 | tf_op jit(solution)/shard_map/ppermute | solution.py:171
  26.5 0.0 collective-permute-done.7
  26.5 0.2 add.57
  26.7 1.3 collective-permute-start.8
  28.1 8.9 %collective-permute-done.1 = bf16[256,1024]{1,0:T(8,128)(2,1)S(1)} collective-permute-done((bf16[256,1024]{1,0:T(8,128)(2,1)S(1)}, bf16[256,1024]{1,0:T(8,128)(2,1)S(1)}, u32[]{:S(2)}, u32[]{:S(2)}) %collective-permute-start.1) | collective-permute-done | bytes 524320 | tf_op jit(solution)/shard_map/ppermute | solution.py:171
  37.0 0.2 add.52
  37.1 2.9 %collective-permute-start.2 = (bf16[256,1024]{1,0:T(8,128)(2,1)S(1)}, bf16[256,1024]{1,0:T(8,128)(2,1)S(1)}, u32[]{:S(2)}, u32[]{:S(2)}) collective-permute-start(bf16[256,1024]{1,0:T(8,128)(2,1)S(1)} %add.52), channel_id=1, source_target_pairs={{0,256},{1,769},{2,258},{3,771},{4,260},{5,773},{6,262},{7,775},{8... | collective-permute-start | bytes 1572872 | tf_op jit(solution)/shard_map/ppermute | solution.py:171
  40.1 0.0 copy-done
  40.1 1.2 shard_map.38.sparse_ref
  41.2 11.6 %collective-permute-start.6 = (bf16[1024,1024]{1,0:T(8,128)(2,1)S(1)}, bf16[1024,1024]{1,0:T(8,128)(2,1)S(1)}, u32[]{:S(2)}, u32[]{:S(2)}) collective-permute-start(bf16[1024,1024]{1,0:T(8,128)(2,1)S(1)} %shard_map.38.sparse_ref), channel_id=1, source_target_pairs={{0,1},{1,0},{2,3},{3,2},{4,5},{5,4},{6,7},{7,6},{8,9},{9,8},{10,11... | collective-permute-start | bytes 6291464 | tf_op jit(solution)/shard_map/ppermute | solution.py:162
  52.8 0.0 collective-permute-done.8
  52.9 0.2 add.58
  53.1 1.3 collective-permute-start.9
  54.4 0.0 collective-permute-done.2
  54.4 0.2 add.53
  54.6 1.3 collective-permute-start.3
  55.9 8.4 %collective-permute-done.9 = bf16[256,1024]{1,0:T(8,128)(2,1)S(1)} collective-permute-done((bf16[256,1024]{1,0:T(8,128)(2,1)S(1)}, bf16[256,1024]{1,0:T(8,128)(2,1)S(1)}, u32[]{:S(2)}, u32[]{:S(2)}) %collective-permute-start.9) | collective-permute-done | bytes 524320 | tf_op jit(solution)/shard_map/ppermute | solution.py:171
  64.3 0.2 add.59
  64.5 1.3 collective-permute-start.10
  65.8 1.1 collective-permute-done.3
  66.9 0.2 add.54
  67.1 4.2 %collective-permute-start.4 = (bf16[256,1024]{1,0:T(8,128)(2,1)S(1)}, bf16[256,1024]{1,0:T(8,128)(2,1)S(1)}, u32[]{:S(2)}, u32[]{:S(2)}) collective-permute-start(bf16[256,1024]{1,0:T(8,128)(2,1)S(1)} %add.54), channel_id=1, source_target_pairs={{256,320},{769,705},{258,322},{771,707},{260,324},{773,709},{262,3... | collective-permute-start | bytes 1572872 | tf_op jit(solution)/shard_map/ppermute | solution.py:171
  71.4 1.2 collective-permute-done.10
  72.6 0.2 add.60
  72.8 1.3 collective-permute-start.11
  74.1 4.8 %collective-permute-done.4 = bf16[256,1024]{1,0:T(8,128)(2,1)S(1)} collective-permute-done((bf16[256,1024]{1,0:T(8,128)(2,1)S(1)}, bf16[256,1024]{1,0:T(8,128)(2,1)S(1)}, u32[]{:S(2)}, u32[]{:S(2)}) %collective-permute-start.4) | collective-permute-done | bytes 524320 | tf_op jit(solution)/shard_map/ppermute | solution.py:171
  78.8 0.2 add.55
  79.0 1.3 collective-permute-start.5
  80.4 6.8 %collective-permute-done.11 = bf16[256,1024]{1,0:T(8,128)(2,1)S(1)} collective-permute-done((bf16[256,1024]{1,0:T(8,128)(2,1)S(1)}, bf16[256,1024]{1,0:T(8,128)(2,1)S(1)}, u32[]{:S(2)}, u32[]{:S(2)}) %collective-permute-start.11) | collective-permute-done | bytes 524320 | tf_op jit(solution)/shard_map/ppermute | solution.py:171
  87.2 0.2 add.61.left_ref
  87.4 0.7 shard_map.39.total_ref
  88.1 2.8 %collective-permute-done.5 = bf16[256,1024]{1,0:T(8,128)(2,1)S(1)} collective-permute-done((bf16[256,1024]{1,0:T(8,128)(2,1)S(1)}, bf16[256,1024]{1,0:T(8,128)(2,1)S(1)}, u32[]{:S(2)}, u32[]{:S(2)}) %collective-permute-start.5) | collective-permute-done | bytes 524320 | tf_op jit(solution)/shard_map/ppermute | solution.py:171
  90.9 0.2 add.56.left_ref
  91.1 0.0 collective-permute-done.6.sparse_ref
  91.1 1.5 shard_map.40
  92.7 7.4 %all-to-all-start = ((bf16[16,16,1024]{2,1,0:T(8,128)(2,1)}), bf16[16,16,1024]{2,1,0:T(8,128)(2,1)S(1)}, u32[]{:S(2)}, u32[]{:S(2)}) async-start(bf16[16,16,1024]{2,1,0:T(8,128)(2,1)} %bitcast.2), calls=%async_computation | async-start | bytes 1048576 | tf_op jit(solution)/shard_map/all_to_all | solution.py:175
  100.1 0.8 convert_bitcast_fusion
  100.9 0.1 broadcast_bitcast_fusion.1
  101.0 7.5 %all-to-all-done = bf16[16,16,1024]{2,1,0:T(8,128)(2,1)S(1)} async-done(((bf16[16,16,1024]{2,1,0:T(8,128)(2,1)}), bf16[16,16,1024]{2,1,0:T(8,128)(2,1)S(1)}, u32[]{:S(2)}, u32[]{:S(2)}) %all-to-all-start) | async-done | bytes 524320 | tf_op jit(solution)/shard_map/all_to_all | solution.py:175
  108.5 0.1 convert_reduce_fusion
  108.6 0.1 broadcast_in_dim.10
  108.6 13.1 %all_to_all.15 = bf16[16,16,1024]{2,1,0:T(8,128)(2,1)S(1)} all-to-all(bf16[16,16,1024]{2,1,0:T(8,128)(2,1)S(1)} %broadcast_in_dim.10), channel_id=1, replica_groups={{0,2,4,6,8,10,12,14,16,18,20,22,24,26,28,30},{1,3,5,7,9,11,13,15,17,19,..., dimensions={0} | all-to-all | bytes 1048576 | tf_op jit(solution)/shard_map/all_to_all | solution.py:179
  121.7 1.9 collective-permute-start.12
  123.6 1.9 collective-permute-done.12.other_ref
  125.5 1.5 shard_map.41
  127.0 1.3 shard_map.42
  128.3 5.6 %collective-permute-start.15 = (bf16[128,1024]{1,0:T(8,128)(2,1)S(1)}, bf16[128,1024]{1,0:T(8,128)(2,1)S(1)}, u32[]{:S(2)}, u32[]{:S(2)}) collective-permute-start(bf16[128,1024]{1,0:T(8,128)(2,1)S(1)} %get-tuple-element.18), channel_id=1, source_target_pairs={{0,992},{1,33},{2,994},{3,35},{4,996},{5,37},{6,998},{7,39},{8,100... | collective-permute-start | bytes 786440 | tf_op jit(solution)/shard_map/ppermute | solution.py:190
  133.9 3.2 %collective-permute-start.13 = (bf16[128,1024]{1,0:T(8,128)(2,1)S(1)}, bf16[128,1024]{1,0:T(8,128)(2,1)S(1)}, u32[]{:S(2)}, u32[]{:S(2)}) collective-permute-start(bf16[128,1024]{1,0:T(8,128)(2,1)S(1)} %get-tuple-element.16), channel_id=1, source_target_pairs={{0,64},{1,961},{2,66},{3,963},{4,68},{5,965},{6,70},{7,967},{8,72}... | collective-permute-start | bytes 786440 | tf_op jit(solution)/shard_map/ppermute | solution.py:190
  137.1 3.4 %collective-permute-start.14 = (bf16[128,1024]{1,0:T(8,128)(2,1)S(1)}, bf16[128,1024]{1,0:T(8,128)(2,1)S(1)}, u32[]{:S(2)}, u32[]{:S(2)}) collective-permute-start(bf16[128,1024]{1,0:T(8,128)(2,1)S(1)} %get-tuple-element.17), channel_id=1, source_target_pairs={{0,32},{1,993},{2,34},{3,995},{4,36},{5,997},{6,38},{7,999},{8,40}... | collective-permute-start | bytes 786440 | tf_op jit(solution)/shard_map/ppermute | solution.py:190
  140.6 0.0 collective-permute-done.15.refs_2_
  140.6 5.1 %collective-permute-done.13.refs_0_ = bf16[128,1024]{1,0:T(8,128)(2,1)S(1)} collective-permute-done((bf16[128,1024]{1,0:T(8,128)(2,1)S(1)}, bf16[128,1024]{1,0:T(8,128)(2,1)S(1)}, u32[]{:S(2)}, u32[]{:S(2)}) %collective-permute-start.13) | collective-permute-done | bytes 262176 | tf_op jit(solution)/shard_map/ppermute | solution.py:190
  145.7 2.7 %collective-permute-done.14.refs_1_ = bf16[128,1024]{1,0:T(8,128)(2,1)S(1)} collective-permute-done((bf16[128,1024]{1,0:T(8,128)(2,1)S(1)}, bf16[128,1024]{1,0:T(8,128)(2,1)S(1)}, u32[]{:S(2)}, u32[]{:S(2)}) %collective-permute-start.14) | collective-permute-done | bytes 262176 | tf_op jit(solution)/shard_map/ppermute | solution.py:190
  148.4 1.4 shard_map.43
  149.8 22.7 %all-to-all-start.2 = ((bf16[8,16,1024]{2,1,0:T(8,128)(2,1)}), bf16[8,16,1024]{2,1,0:T(8,128)(2,1)S(1)}, u32[]{:S(2)}, u32[]{:S(2)}) async-start(bf16[8,16,1024]{2,1,0:T(8,128)(2,1)} %bitcast.6), calls=%async_computation.2 | async-start | bytes 524288 | tf_op jit(solution)/shard_map/all_to_all | solution.py:196
  172.5 0.1 broadcast_bitcast_fusion
  172.6 21.9 %all-to-all-done.2 = bf16[8,16,1024]{2,1,0:T(8,128)(2,1)S(1)} async-done(((bf16[8,16,1024]{2,1,0:T(8,128)(2,1)}), bf16[8,16,1024]{2,1,0:T(8,128)(2,1)S(1)}, u32[]{:S(2)}, u32[]{:S(2)}) %all-to-all-start.2) | async-done | bytes 262176 | tf_op jit(solution)/shard_map/all_to_all | solution.py:196
  194.5 0.6 multiply_convert_fusion
  (4 shorter events, 0.1 us)
Async XLA Ops:
  0.0 1.4 copy-start.1
  1.4 38.7 %copy-start = (bf16[1024,1024]{1,0:T(8,128)(2,1)S(1)}, bf16[1024,1024]{1,0:T(8,128)(2,1)}, u32[]{:S(2)}) copy-start(bf16[1024,1024]{1,0:T(8,128)(2,1)} %density_ref.1) | copy-start | bytes 6291460
  2.3 16.2 %collective-permute-start = (bf16[256,1024]{1,0:T(8,128)(2,1)S(1)}, bf16[256,1024]{1,0:T(8,128)(2,1)S(1)}, u32[]{:S(2)}, u32[]{:S(2)}) collective-permute-start(bf16[256,1024]{1,0:T(8,128)(2,1)S(1)} %get-tuple-element.12), channel_id=1, source_target_pairs={{0,1},{1,0},{2,3},{3,2},{4,5},{5,4},{6,7},{7,6},{8,9},{9,8},{10,11... | collective-permute-start | bytes 1572872 | tf_op jit(solution)/shard_map/ppermute | solution.py:160
  4.2 22.3 %collective-permute-start.7 = (bf16[256,1024]{1,0:T(8,128)(2,1)S(1)}, bf16[256,1024]{1,0:T(8,128)(2,1)S(1)}, u32[]{:S(2)}, u32[]{:S(2)}) collective-permute-start(bf16[256,1024]{1,0:T(8,128)(2,1)S(1)} %get-tuple-element.13), channel_id=1, source_target_pairs={{0,256},{1,769},{2,258},{3,771},{4,260},{5,773},{6,262},{7,775},{8... | collective-permute-start | bytes 1572872 | tf_op jit(solution)/shard_map/ppermute | solution.py:171
  18.6 18.4 %collective-permute-start.1 = (bf16[256,1024]{1,0:T(8,128)(2,1)S(1)}, bf16[256,1024]{1,0:T(8,128)(2,1)S(1)}, u32[]{:S(2)}, u32[]{:S(2)}) collective-permute-start(bf16[256,1024]{1,0:T(8,128)(2,1)S(1)} %collective-permute-done), channel_id=1, source_target_pairs={{0,768},{1,257},{2,770},{3,259},{4,772},{5,261},{6,774},{7,263},{8... | collective-permute-start | bytes 1572872 | tf_op jit(solution)/shard_map/ppermute | solution.py:171
  26.7 26.1 %collective-permute-start.8 = (bf16[256,1024]{1,0:T(8,128)(2,1)S(1)}, bf16[256,1024]{1,0:T(8,128)(2,1)S(1)}, u32[]{:S(2)}, u32[]{:S(2)}) collective-permute-start(bf16[256,1024]{1,0:T(8,128)(2,1)S(1)} %add.57), channel_id=1, source_target_pairs={{0,768},{1,257},{2,770},{3,259},{4,772},{5,261},{6,774},{7,263},{8... | collective-permute-start | bytes 1572872 | tf_op jit(solution)/shard_map/ppermute | solution.py:171
  37.1 17.2 %collective-permute-start.2 = (bf16[256,1024]{1,0:T(8,128)(2,1)S(1)}, bf16[256,1024]{1,0:T(8,128)(2,1)S(1)}, u32[]{:S(2)}, u32[]{:S(2)}) collective-permute-start(bf16[256,1024]{1,0:T(8,128)(2,1)S(1)} %add.52), channel_id=1, source_target_pairs={{0,256},{1,769},{2,258},{3,771},{4,260},{5,773},{6,262},{7,775},{8... | collective-permute-start | bytes 1572872 | tf_op jit(solution)/shard_map/ppermute | solution.py:171
  41.2 49.9 %collective-permute-start.6 = (bf16[1024,1024]{1,0:T(8,128)(2,1)S(1)}, bf16[1024,1024]{1,0:T(8,128)(2,1)S(1)}, u32[]{:S(2)}, u32[]{:S(2)}) collective-permute-start(bf16[1024,1024]{1,0:T(8,128)(2,1)S(1)} %shard_map.38.sparse_ref), channel_id=1, source_target_pairs={{0,1},{1,0},{2,3},{3,2},{4,5},{5,4},{6,7},{7,6},{8,9},{9,8},{10,11... | collective-permute-start | bytes 6291464 | tf_op jit(solution)/shard_map/ppermute | solution.py:162
  53.1 11.2 %collective-permute-start.9 = (bf16[256,1024]{1,0:T(8,128)(2,1)S(1)}, bf16[256,1024]{1,0:T(8,128)(2,1)S(1)}, u32[]{:S(2)}, u32[]{:S(2)}) collective-permute-start(bf16[256,1024]{1,0:T(8,128)(2,1)S(1)} %add.58), channel_id=1, source_target_pairs={{768,832},{257,193},{770,834},{259,195},{772,836},{261,197},{774,8... | collective-permute-start | bytes 1572872 | tf_op jit(solution)/shard_map/ppermute | solution.py:171
  54.6 12.4 %collective-permute-start.3 = (bf16[256,1024]{1,0:T(8,128)(2,1)S(1)}, bf16[256,1024]{1,0:T(8,128)(2,1)S(1)}, u32[]{:S(2)}, u32[]{:S(2)}) collective-permute-start(bf16[256,1024]{1,0:T(8,128)(2,1)S(1)} %add.53), channel_id=1, source_target_pairs={{256,192},{769,833},{258,194},{771,835},{260,196},{773,837},{262,1... | collective-permute-start | bytes 1572872 | tf_op jit(solution)/shard_map/ppermute | solution.py:171
  64.5 8.1 %collective-permute-start.10 = (bf16[256,1024]{1,0:T(8,128)(2,1)S(1)}, bf16[256,1024]{1,0:T(8,128)(2,1)S(1)}, u32[]{:S(2)}, u32[]{:S(2)}) collective-permute-start(bf16[256,1024]{1,0:T(8,128)(2,1)S(1)} %add.59), channel_id=1, source_target_pairs={{768,704},{257,321},{770,706},{259,323},{772,708},{261,325},{774,7... | collective-permute-start | bytes 1572872 | tf_op jit(solution)/shard_map/ppermute | solution.py:171
  67.1 11.7 %collective-permute-start.4 = (bf16[256,1024]{1,0:T(8,128)(2,1)S(1)}, bf16[256,1024]{1,0:T(8,128)(2,1)S(1)}, u32[]{:S(2)}, u32[]{:S(2)}) collective-permute-start(bf16[256,1024]{1,0:T(8,128)(2,1)S(1)} %add.54), channel_id=1, source_target_pairs={{256,320},{769,705},{258,322},{771,707},{260,324},{773,709},{262,3... | collective-permute-start | bytes 1572872 | tf_op jit(solution)/shard_map/ppermute | solution.py:171
  72.8 14.4 %collective-permute-start.11 = (bf16[256,1024]{1,0:T(8,128)(2,1)S(1)}, bf16[256,1024]{1,0:T(8,128)(2,1)S(1)}, u32[]{:S(2)}, u32[]{:S(2)}) collective-permute-start(bf16[256,1024]{1,0:T(8,128)(2,1)S(1)} %add.60), channel_id=1, source_target_pairs={{704,736},{321,289},{706,738},{323,291},{708,740},{325,293},{710,7... | collective-permute-start | bytes 1572872 | tf_op jit(solution)/shard_map/ppermute | solution.py:171
  79.0 11.9 %collective-permute-start.5 = (bf16[256,1024]{1,0:T(8,128)(2,1)S(1)}, bf16[256,1024]{1,0:T(8,128)(2,1)S(1)}, u32[]{:S(2)}, u32[]{:S(2)}) collective-permute-start(bf16[256,1024]{1,0:T(8,128)(2,1)S(1)} %add.55), channel_id=1, source_target_pairs={{320,288},{705,737},{322,290},{707,739},{324,292},{709,741},{326,2... | collective-permute-start | bytes 1572872 | tf_op jit(solution)/shard_map/ppermute | solution.py:171
  92.7 15.8 %all-to-all-start = ((bf16[16,16,1024]{2,1,0:T(8,128)(2,1)}), bf16[16,16,1024]{2,1,0:T(8,128)(2,1)S(1)}, u32[]{:S(2)}, u32[]{:S(2)}) async-start(bf16[16,16,1024]{2,1,0:T(8,128)(2,1)} %bitcast.2), calls=%async_computation | async-start | bytes 1048576 | tf_op jit(solution)/shard_map/all_to_all | solution.py:175
  121.7 3.8 %collective-permute-start.12 = (bf16[256,1024]{1,0:T(8,128)(2,1)S(1)}, bf16[256,1024]{1,0:T(8,128)(2,1)S(1)}, u32[]{:S(2)}, u32[]{:S(2)}) collective-permute-start(bf16[256,1024]{1,0:T(8,128)(2,1)S(1)} %bitcast.13), channel_id=1, source_target_pairs={{0,1},{1,0},{2,3},{3,2},{4,5},{5,4},{6,7},{7,6},{8,9},{9,8},{10,11... | collective-permute-start | bytes 1572872 | tf_op jit(solution)/shard_map/ppermute | solution.py:180
  128.3 12.3 %collective-permute-start.15 = (bf16[128,1024]{1,0:T(8,128)(2,1)S(1)}, bf16[128,1024]{1,0:T(8,128)(2,1)S(1)}, u32[]{:S(2)}, u32[]{:S(2)}) collective-permute-start(bf16[128,1024]{1,0:T(8,128)(2,1)S(1)} %get-tuple-element.18), channel_id=1, source_target_pairs={{0,992},{1,33},{2,994},{3,35},{4,996},{5,37},{6,998},{7,39},{8,100... | collective-permute-start | bytes 786440 | tf_op jit(solution)/shard_map/ppermute | solution.py:190
  133.9 11.8 %collective-permute-start.13 = (bf16[128,1024]{1,0:T(8,128)(2,1)S(1)}, bf16[128,1024]{1,0:T(8,128)(2,1)S(1)}, u32[]{:S(2)}, u32[]{:S(2)}) collective-permute-start(bf16[128,1024]{1,0:T(8,128)(2,1)S(1)} %get-tuple-element.16), channel_id=1, source_target_pairs={{0,64},{1,961},{2,66},{3,963},{4,68},{5,965},{6,70},{7,967},{8,72}... | collective-permute-start | bytes 786440 | tf_op jit(solution)/shard_map/ppermute | solution.py:190
  137.1 11.3 %collective-permute-start.14 = (bf16[128,1024]{1,0:T(8,128)(2,1)S(1)}, bf16[128,1024]{1,0:T(8,128)(2,1)S(1)}, u32[]{:S(2)}, u32[]{:S(2)}) collective-permute-start(bf16[128,1024]{1,0:T(8,128)(2,1)S(1)} %get-tuple-element.17), channel_id=1, source_target_pairs={{0,32},{1,993},{2,34},{3,995},{4,36},{5,997},{6,38},{7,999},{8,40}... | collective-permute-start | bytes 786440 | tf_op jit(solution)/shard_map/ppermute | solution.py:190
  149.8 44.7 %all-to-all-start.2 = ((bf16[8,16,1024]{2,1,0:T(8,128)(2,1)}), bf16[8,16,1024]{2,1,0:T(8,128)(2,1)S(1)}, u32[]{:S(2)}, u32[]{:S(2)}) async-start(bf16[8,16,1024]{2,1,0:T(8,128)(2,1)} %bitcast.6), calls=%async_computation.2 | async-start | bytes 524288 | tf_op jit(solution)/shard_map/all_to_all | solution.py:196

commit v5 on v4

--- a/solution.py
+++ b/solution.py
@@ -167,14 +167,20 @@
         stages.append([(z, -gap) for z in have] + [(z + gap, gap) for z in have])
         have = [z + step * gap for z in have for step in (-1, 0, 1, 2)]
     stages.append([(z, 1) for z in have])
-    for moves in stages:
+    first = (col % 2) * half + (col // 2) * piece
+    masks = (
+        mask(rows_here // BS, first // BS, row * (rows_here // BS)),
+        mask(cols_here // BS, row * piece // BS, col * (cols_here // BS)),
+    )
+    for number, moves in enumerate(stages):
         halves = [h + lax.ppermute(h, BOTH, pairs(moves, way)) for h, way in zip(halves, (1, -1))]
+        if number == len(stages) - 2:
+            halves[1], *masks = lax.optimization_barrier((halves[1], *masks))
 
     total = call(own_kernel, tall((half, rows_here), F32), work)(in_specs=[VMEM] * 2)(halves[0], sparse)
     kept = call(both_kernel, tall((half, rows_here), BF16), work)(in_specs=[VMEM] * 3)(halves[1], sibling, total)
     parts = lax.all_to_all(kept.reshape(chips, piece, rows_here), "col", 0, 0, axis_index_groups=same_core, tiled=True)
-    first = (col % 2) * half + (col // 2) * piece
-    square = parts.astype(F32).sum(0) * mask(rows_here // BS, first // BS, row * (rows_here // BS))
+    square = parts.astype(F32).sum(0) * masks[0]
     square = jnp.broadcast_to(square.astype(BF16), (chips, piece, rows_here))
     mine = lax.all_to_all(square, "col", 0, 0, axis_index_groups=same_core, tiled=True).reshape(half, rows_here)
     other = lax.ppermute(mine, "col", swap)
@@ -195,8 +201,7 @@
     )
     parts = lax.all_to_all(ready.reshape(groups, piece, cols_here), "row", 0, 0, axis_index_groups=strided, tiled=True)
     result = parts.astype(F32).sum(0)
-    result = result * mask(cols_here // BS, row * piece // BS, col * (cols_here // BS))
-    return result.astype(BF16)
+    return (result * masks[1]).astype(BF16)
 
 
 def solution(mesh):

time: 199 us -> 200 us (level)
  blocking collectives: 13.1 us -> 72.8 us
  waiting for transfers between devices: 73.1 us -> 39.4 us
  starting transfers between devices: 95.2 us -> 68 us
  other arithmetic: 3.55 us -> 5.65 us
    all_to_all x0 -> x2, blocking collectives: none -> 59.7 us  [the longest x1 44.5 us: body(): lax.all_to_all(ready.reshape(groups, piece, cols_here), 'row', 0, 0, axis...]
    all_to_all x2 -> x0, starting transfers between devices: 30.1 us -> none  [the longest x1 22.7 us: body(): lax.all_to_all(ready.reshape(groups, piece, cols_here), 'row', 0, 0, axis...]
    all_to_all x2 -> x0, waiting for transfers between devices: 29.4 us -> none  [the longest x1 21.9 us: body(): lax.all_to_all(ready.reshape(groups, piece, cols_here), 'row', 0, 0, axis...]
    ppermute x10, waiting for transfers between devices: 33.9 us -> 29.3 us  [body(): lax.ppermute(h, BOTH, pairs(moves, way))]
    ppermute x10, starting transfers between devices: 37.3 us -> 39.7 us  [body(): lax.ppermute(h, BOTH, pairs(moves, way))]
    add x10, other arithmetic: 1.89 us -> 3.98 us  [body(): h + lax.ppermute(h, BOTH, pairs(moves, way))]
  transfers between devices with their start and end apart: 18 -> 16, of which waited for: 12 -> 9; matrix products, arithmetic and copies ran while one was open for 1% -> 3% of each run, Pallas kernels for 1% -> 1%
where the time goes in v5:
time: 200 us; the launch traced here: 196 us
  blocking collectives  72.8 us (36%)
  starting transfers between devices  68 us (34%)
  waiting for transfers between devices  39.4 us (20%)
  Pallas kernels  8.56 us (4%)
  other arithmetic  5.65 us (3%)
    all_to_all x1, blocking collectives, body(): lax.all_to_all(ready.reshape(groups, piece, cols_here), 'row', 0, 0, axis...  44.5 us
    ppermute x10, starting transfers between devices, body(): lax.ppermute(h, BOTH, pairs(moves, way))  39.7 us
    ppermute x10, waiting for transfers between devices, body(): lax.ppermute(h, BOTH, pairs(moves, way))  29.3 us
    all_to_all x1, blocking collectives, body(): lax.all_to_all(kept.reshape(chips, piece, rows_here), 'col', 0, 0, axis_i...  15.2 us
    all_to_all x1, blocking collectives, body(): lax.all_to_all(square, 'col', 0, 0, axis_index_groups=same_core, tiled=True)  13.1 us
    ppermute x3, starting transfers between devices, body(): lax.ppermute(part, BOTH, pairs([(z, step) for z in range(rows)]))  12.9 us
    ppermute x1, starting transfers between devices, body(): sibling = lax.ppermute(sparse, 'col', swap)  11.6 us
    ppermute x3, waiting for transfers between devices, body(): lax.ppermute(part, BOTH, pairs([(z, step) for z in range(rows)]))  8.23 us
  transfers between devices with their start and end apart: 16, of which 9 were waited for; matrix products, arithmetic and copies ran while one was open for 3% of the time, Pallas kernels for 1%

profile of v5, /device:TPU:6, one launch (start us, length us, event | category | flops | bytes accessed | tf_op | source)
XLA Modules:
  0.0 196.3 jit_solution(2633976489883947010)
XLA Ops:
  0.0 0.0 copy-start.1
  0.0 1.3 slice.3.window_ref
  1.3 0.1 pad_add_fusion.where_ref
  1.4 0.0 copy-done.1
  1.4 0.0 copy-start
  1.4 0.9 shard_map.37
  2.3 1.9 collective-permute-start
  4.2 14.3 %collective-permute-start.7 = (bf16[256,1024]{1,0:T(8,128)(2,1)S(1)}, bf16[256,1024]{1,0:T(8,128)(2,1)S(1)}, u32[]{:S(2)}, u32[]{:S(2)}) collective-permute-start(bf16[256,1024]{1,0:T(8,128)(2,1)S(1)} %get-tuple-element.17), channel_id=1, source_target_pairs={{0,256},{1,769},{2,258},{3,771},{4,260},{5,773},{6,262},{7,775},{8... | collective-permute-start | bytes 1572872 | tf_op jit(solution)/shard_map/ppermute | solution.py:176
  18.5 0.0 collective-permute-done
  18.6 8.0 %collective-permute-start.1 = (bf16[256,1024]{1,0:T(8,128)(2,1)S(1)}, bf16[256,1024]{1,0:T(8,128)(2,1)S(1)}, u32[]{:S(2)}, u32[]{:S(2)}) collective-permute-start(bf16[256,1024]{1,0:T(8,128)(2,1)S(1)} %collective-permute-done), channel_id=1, source_target_pairs={{0,768},{1,257},{2,770},{3,259},{4,772},{5,261},{6,774},{7,263},{8... | collective-permute-start | bytes 1572872 | tf_op jit(solution)/shard_map/ppermute | solution.py:176
  26.5 0.0 collective-permute-done.7
  26.5 0.2 add.63
  26.7 1.3 collective-permute-start.8
  28.1 8.9 %collective-permute-done.1 = bf16[256,1024]{1,0:T(8,128)(2,1)S(1)} collective-permute-done((bf16[256,1024]{1,0:T(8,128)(2,1)S(1)}, bf16[256,1024]{1,0:T(8,128)(2,1)S(1)}, u32[]{:S(2)}, u32[]{:S(2)}) %collective-permute-start.1) | collective-permute-done | bytes 524320 | tf_op jit(solution)/shard_map/ppermute | solution.py:176
  37.0 0.2 add.52
  37.1 2.9 %collective-permute-start.2 = (bf16[256,1024]{1,0:T(8,128)(2,1)S(1)}, bf16[256,1024]{1,0:T(8,128)(2,1)S(1)}, u32[]{:S(2)}, u32[]{:S(2)}) collective-permute-start(bf16[256,1024]{1,0:T(8,128)(2,1)S(1)} %add.52), channel_id=1, source_target_pairs={{0,256},{1,769},{2,258},{3,771},{4,260},{5,773},{6,262},{7,775},{8... | collective-permute-start | bytes 1572872 | tf_op jit(solution)/shard_map/ppermute | solution.py:176
  40.1 0.0 copy-done
  40.1 1.2 shard_map.38.sparse_ref
  41.2 11.6 %collective-permute-start.6 = (bf16[1024,1024]{1,0:T(8,128)(2,1)S(1)}, bf16[1024,1024]{1,0:T(8,128)(2,1)}, u32[]{:S(2)}, u32[]{:S(2)}) collective-permute-start(bf16[1024,1024]{1,0:T(8,128)(2,1)S(1)} %shard_map.38.sparse_ref), channel_id=1, source_target_pairs={{0,1},{1,0},{2,3},{3,2},{4,5},{5,4},{6,7},{7,6},{8,9},{9,8},{10,11... | collective-permute-start | bytes 6291464 | tf_op jit(solution)/shard_map/ppermute | solution.py:162
  52.8 0.0 collective-permute-done.8
  52.9 0.2 add.64
  53.1 1.3 collective-permute-start.9
  54.4 0.0 collective-permute-done.2
  54.4 0.2 add.53
  54.6 1.3 collective-permute-start.3
  55.9 8.4 %collective-permute-done.9 = bf16[256,1024]{1,0:T(8,128)(2,1)S(1)} collective-permute-done((bf16[256,1024]{1,0:T(8,128)(2,1)S(1)}, bf16[256,1024]{1,0:T(8,128)(2,1)S(1)}, u32[]{:S(2)}, u32[]{:S(2)}) %collective-permute-start.9) | collective-permute-done | bytes 524320 | tf_op jit(solution)/shard_map/ppermute | solution.py:176
  64.3 0.2 add.65
  64.5 2.1 %collective-permute-start.10 = (bf16[256,1024]{1,0:T(8,128)(2,1)S(1)}, bf16[256,1024]{1,0:T(8,128)(2,1)}, u32[]{:S(2)}, u32[]{:S(2)}) collective-permute-start(bf16[256,1024]{1,0:T(8,128)(2,1)S(1)} %add.65), channel_id=1, source_target_pairs={{768,704},{257,321},{770,706},{259,323},{772,708},{261,325},{774,7... | collective-permute-start | bytes 1572872 | tf_op jit(solution)/shard_map/ppermute | solution.py:176
  66.6 0.3 collective-permute-done.3
  66.9 0.2 add.54
  67.1 5.8 %collective-permute-start.4 = (bf16[256,1024]{1,0:T(8,128)(2,1)S(1)}, bf16[256,1024]{1,0:T(8,128)(2,1)}, u32[]{:S(2)}, u32[]{:S(2)}) collective-permute-start(bf16[256,1024]{1,0:T(8,128)(2,1)S(1)} %add.54), channel_id=1, source_target_pairs={{256,320},{769,705},{258,322},{771,707},{260,324},{773,709},{262,3... | collective-permute-start | bytes 1572872 | tf_op jit(solution)/shard_map/ppermute | solution.py:176
  72.9 0.0 collective-permute-done.10
  72.9 1.2 add.66
  74.2 1.3 collective-permute-start.11
  75.5 0.8 convert_bitcast_fusion
  76.3 2.5 %collective-permute-done.4 = bf16[256,1024]{1,0:T(8,128)(2,1)} collective-permute-done((bf16[256,1024]{1,0:T(8,128)(2,1)S(1)}, bf16[256,1024]{1,0:T(8,128)(2,1)}, u32[]{:S(2)}, u32[]{:S(2)}) %collective-permute-start.4) | collective-permute-done | bytes 524320 | tf_op jit(solution)/shard_map/ppermute | solution.py:176
  78.9 1.2 add.55
  80.1 0.1 broadcast_in_dim.10
  80.2 0.1 broadcast_in_dim.9
  80.2 1.3 collective-permute-start.5
  81.5 3.7 %collective-permute-done.11 = bf16[256,1024]{1,0:T(8,128)(2,1)S(1)} collective-permute-done((bf16[256,1024]{1,0:T(8,128)(2,1)S(1)}, bf16[256,1024]{1,0:T(8,128)(2,1)S(1)}, u32[]{:S(2)}, u32[]{:S(2)}) %collective-permute-start.11) | collective-permute-done | bytes 524320 | tf_op jit(solution)/shard_map/ppermute | solution.py:176
  85.2 0.2 add.67.left_ref
  85.4 0.7 shard_map.39.total_ref
  86.2 5.5 %collective-permute-done.5 = bf16[256,1024]{1,0:T(8,128)(2,1)S(1)} collective-permute-done((bf16[256,1024]{1,0:T(8,128)(2,1)S(1)}, bf16[256,1024]{1,0:T(8,128)(2,1)S(1)}, u32[]{:S(2)}, u32[]{:S(2)}) %collective-permute-start.5) | collective-permute-done | bytes 524320 | tf_op jit(solution)/shard_map/ppermute | solution.py:176
  91.7 0.2 add.62.left_ref
  91.9 0.0 collective-permute-done.6.sparse_ref
  91.9 2.3 %shard_map.40 = bf16[256,1024]{1,0:T(8,128)(2,1)S(1)} custom-call(bf16[256,1024]{1,0:T(8,128)(2,1)S(1)} %add.62.left_ref, bf16[1024,1024]{1,0:T(8,128)(2,1)} %collective-permute-done.6.sparse_ref, f32[256,1024]{1,0:T(8,128)S(1)} %shard_map.39.total_ref), custom_call_target="tpu_custom_call" | custom-call | flops 536870912 | bytes 4194304 | tf_op jit(solution)/shard_map/pallas_call | solution.py:181
  94.2 15.2 %all_to_all.15 = bf16[16,16,1024]{2,1,0:T(8,128)(2,1)S(1)} all-to-all(bf16[16,16,1024]{2,1,0:T(8,128)(2,1)S(1)} %bitcast.15), channel_id=1, replica_groups={{0,2,4,6,8,10,12,14,16,18,20,22,24,26,28,30},{1,3,5,7,9,11,13,15,17,19,..., dimensions={0} | all-to-all | bytes 1048576 | tf_op jit(solution)/shard_map/all_to_all | solution.py:182
  109.4 0.1 convert_reduce_fusion
  109.5 0.1 broadcast_in_dim.11
  109.6 13.1 %all_to_all.16 = bf16[16,16,1024]{2,1,0:T(8,128)(2,1)S(1)} all-to-all(bf16[16,16,1024]{2,1,0:T(8,128)(2,1)S(1)} %broadcast_in_dim.11), channel_id=1, replica_groups={{0,2,4,6,8,10,12,14,16,18,20,22,24,26,28,30},{1,3,5,7,9,11,13,15,17,19,..., dimensions={0} | all-to-all | bytes 1048576 | tf_op jit(solution)/shard_map/all_to_all | solution.py:185
  122.7 1.9 collective-permute-start.12
  124.6 1.9 collective-permute-done.12.other_ref
  126.5 1.5 shard_map.41
  128.0 1.3 shard_map.42
  129.3 6.2 %collective-permute-start.15 = (bf16[128,1024]{1,0:T(8,128)(2,1)S(1)}, bf16[128,1024]{1,0:T(8,128)(2,1)S(1)}, u32[]{:S(2)}, u32[]{:S(2)}) collective-permute-start(bf16[128,1024]{1,0:T(8,128)(2,1)S(1)} %get-tuple-element.23), channel_id=1, source_target_pairs={{0,992},{1,33},{2,994},{3,35},{4,996},{5,37},{6,998},{7,39},{8,100... | collective-permute-start | bytes 786440 | tf_op jit(solution)/shard_map/ppermute | solution.py:196
  135.5 2.8 %collective-permute-start.13 = (bf16[128,1024]{1,0:T(8,128)(2,1)S(1)}, bf16[128,1024]{1,0:T(8,128)(2,1)S(1)}, u32[]{:S(2)}, u32[]{:S(2)}) collective-permute-start(bf16[128,1024]{1,0:T(8,128)(2,1)S(1)} %get-tuple-element.21), channel_id=1, source_target_pairs={{0,64},{1,961},{2,66},{3,963},{4,68},{5,965},{6,70},{7,967},{8,72}... | collective-permute-start | bytes 786440 | tf_op jit(solution)/shard_map/ppermute | solution.py:196
  138.3 3.9 %collective-permute-start.14 = (bf16[128,1024]{1,0:T(8,128)(2,1)S(1)}, bf16[128,1024]{1,0:T(8,128)(2,1)S(1)}, u32[]{:S(2)}, u32[]{:S(2)}) collective-permute-start(bf16[128,1024]{1,0:T(8,128)(2,1)S(1)} %get-tuple-element.22), channel_id=1, source_target_pairs={{0,32},{1,993},{2,34},{3,995},{4,36},{5,997},{6,38},{7,999},{8,40}... | collective-permute-start | bytes 786440 | tf_op jit(solution)/shard_map/ppermute | solution.py:196
  142.2 0.0 collective-permute-done.15.refs_2_
  142.2 6.4 %collective-permute-done.13.refs_0_ = bf16[128,1024]{1,0:T(8,128)(2,1)S(1)} collective-permute-done((bf16[128,1024]{1,0:T(8,128)(2,1)S(1)}, bf16[128,1024]{1,0:T(8,128)(2,1)S(1)}, u32[]{:S(2)}, u32[]{:S(2)}) %collective-permute-start.13) | collective-permute-done | bytes 262176 | tf_op jit(solution)/shard_map/ppermute | solution.py:196
  148.6 1.8 collective-permute-done.14.refs_1_
  150.4 0.7 shard_map.43
  151.1 44.5 %all_to_all.17 = bf16[8,16,1024]{2,1,0:T(8,128)(2,1)S(1)} all-to-all(bf16[8,16,1024]{2,1,0:T(8,128)(2,1)S(1)} %bitcast.16), channel_id=1, replica_groups={{512,128,768,384,0,640,256,896},{544,160,800,416,32,672,288,928},{576,1..., dimensions={0} | all-to-all | bytes 524288 | tf_op jit(solution)/shard_map/all_to_all | solution.py:202
  195.6 0.6 multiply_convert_fusion
  (2 shorter events, 0.0 us)
Async XLA Ops:
  0.0 1.4 copy-start.1
  1.4 38.7 %copy-start = (bf16[1024,1024]{1,0:T(8,128)(2,1)S(1)}, bf16[1024,1024]{1,0:T(8,128)(2,1)}, u32[]{:S(2)}) copy-start(bf16[1024,1024]{1,0:T(8,128)(2,1)} %density_ref.1) | copy-start | bytes 6291460
  2.3 16.2 %collective-permute-start = (bf16[256,1024]{1,0:T(8,128)(2,1)S(1)}, bf16[256,1024]{1,0:T(8,128)(2,1)S(1)}, u32[]{:S(2)}, u32[]{:S(2)}) collective-permute-start(bf16[256,1024]{1,0:T(8,128)(2,1)S(1)} %get-tuple-element.15), channel_id=1, source_target_pairs={{0,1},{1,0},{2,3},{3,2},{4,5},{5,4},{6,7},{7,6},{8,9},{9,8},{10,11... | collective-permute-start | bytes 1572872 | tf_op jit(solution)/shard_map/ppermute | solution.py:160
  4.2 22.3 %collective-permute-start.7 = (bf16[256,1024]{1,0:T(8,128)(2,1)S(1)}, bf16[256,1024]{1,0:T(8,128)(2,1)S(1)}, u32[]{:S(2)}, u32[]{:S(2)}) collective-permute-start(bf16[256,1024]{1,0:T(8,128)(2,1)S(1)} %get-tuple-element.17), channel_id=1, source_target_pairs={{0,256},{1,769},{2,258},{3,771},{4,260},{5,773},{6,262},{7,775},{8... | collective-permute-start | bytes 1572872 | tf_op jit(solution)/shard_map/ppermute | solution.py:176
  18.6 18.4 %collective-permute-start.1 = (bf16[256,1024]{1,0:T(8,128)(2,1)S(1)}, bf16[256,1024]{1,0:T(8,128)(2,1)S(1)}, u32[]{:S(2)}, u32[]{:S(2)}) collective-permute-start(bf16[256,1024]{1,0:T(8,128)(2,1)S(1)} %collective-permute-done), channel_id=1, source_target_pairs={{0,768},{1,257},{2,770},{3,259},{4,772},{5,261},{6,774},{7,263},{8... | collective-permute-start | bytes 1572872 | tf_op jit(solution)/shard_map/ppermute | solution.py:176
  26.7 26.1 %collective-permute-start.8 = (bf16[256,1024]{1,0:T(8,128)(2,1)S(1)}, bf16[256,1024]{1,0:T(8,128)(2,1)S(1)}, u32[]{:S(2)}, u32[]{:S(2)}) collective-permute-start(bf16[256,1024]{1,0:T(8,128)(2,1)S(1)} %add.63), channel_id=1, source_target_pairs={{0,768},{1,257},{2,770},{3,259},{4,772},{5,261},{6,774},{7,263},{8... | collective-permute-start | bytes 1572872 | tf_op jit(solution)/shard_map/ppermute | solution.py:176
  37.1 17.2 %collective-permute-start.2 = (bf16[256,1024]{1,0:T(8,128)(2,1)S(1)}, bf16[256,1024]{1,0:T(8,128)(2,1)S(1)}, u32[]{:S(2)}, u32[]{:S(2)}) collective-permute-start(bf16[256,1024]{1,0:T(8,128)(2,1)S(1)} %add.52), channel_id=1, source_target_pairs={{0,256},{1,769},{2,258},{3,771},{4,260},{5,773},{6,262},{7,775},{8... | collective-permute-start | bytes 1572872 | tf_op jit(solution)/shard_map/ppermute | solution.py:176
  41.2 50.7 %collective-permute-start.6 = (bf16[1024,1024]{1,0:T(8,128)(2,1)S(1)}, bf16[1024,1024]{1,0:T(8,128)(2,1)}, u32[]{:S(2)}, u32[]{:S(2)}) collective-permute-start(bf16[1024,1024]{1,0:T(8,128)(2,1)S(1)} %shard_map.38.sparse_ref), channel_id=1, source_target_pairs={{0,1},{1,0},{2,3},{3,2},{4,5},{5,4},{6,7},{7,6},{8,9},{9,8},{10,11... | collective-permute-start | bytes 6291464 | tf_op jit(solution)/shard_map/ppermute | solution.py:162
  53.1 11.3 %collective-permute-start.9 = (bf16[256,1024]{1,0:T(8,128)(2,1)S(1)}, bf16[256,1024]{1,0:T(8,128)(2,1)S(1)}, u32[]{:S(2)}, u32[]{:S(2)}) collective-permute-start(bf16[256,1024]{1,0:T(8,128)(2,1)S(1)} %add.64), channel_id=1, source_target_pairs={{768,832},{257,193},{770,834},{259,195},{772,836},{261,197},{774,8... | collective-permute-start | bytes 1572872 | tf_op jit(solution)/shard_map/ppermute | solution.py:176
  54.6 12.3 %collective-permute-start.3 = (bf16[256,1024]{1,0:T(8,128)(2,1)S(1)}, bf16[256,1024]{1,0:T(8,128)(2,1)S(1)}, u32[]{:S(2)}, u32[]{:S(2)}) collective-permute-start(bf16[256,1024]{1,0:T(8,128)(2,1)S(1)} %add.53), channel_id=1, source_target_pairs={{256,192},{769,833},{258,194},{771,835},{260,196},{773,837},{262,1... | collective-permute-start | bytes 1572872 | tf_op jit(solution)/shard_map/ppermute | solution.py:176
  64.5 8.4 %collective-permute-start.10 = (bf16[256,1024]{1,0:T(8,128)(2,1)S(1)}, bf16[256,1024]{1,0:T(8,128)(2,1)}, u32[]{:S(2)}, u32[]{:S(2)}) collective-permute-start(bf16[256,1024]{1,0:T(8,128)(2,1)S(1)} %add.65), channel_id=1, source_target_pairs={{768,704},{257,321},{770,706},{259,323},{772,708},{261,325},{774,7... | collective-permute-start | bytes 1572872 | tf_op jit(solution)/shard_map/ppermute | solution.py:176
  67.1 11.7 %collective-permute-start.4 = (bf16[256,1024]{1,0:T(8,128)(2,1)S(1)}, bf16[256,1024]{1,0:T(8,128)(2,1)}, u32[]{:S(2)}, u32[]{:S(2)}) collective-permute-start(bf16[256,1024]{1,0:T(8,128)(2,1)S(1)} %add.54), channel_id=1, source_target_pairs={{256,320},{769,705},{258,322},{771,707},{260,324},{773,709},{262,3... | collective-permute-start | bytes 1572872 | tf_op jit(solution)/shard_map/ppermute | solution.py:176
  74.2 11.1 %collective-permute-start.11 = (bf16[256,1024]{1,0:T(8,128)(2,1)S(1)}, bf16[256,1024]{1,0:T(8,128)(2,1)S(1)}, u32[]{:S(2)}, u32[]{:S(2)}) collective-permute-start(bf16[256,1024]{1,0:T(8,128)(2,1)S(1)} %add.66), channel_id=1, source_target_pairs={{704,736},{321,289},{706,738},{323,291},{708,740},{325,293},{710,7... | collective-permute-start | bytes 1572872 | tf_op jit(solution)/shard_map/ppermute | solution.py:176
  80.2 11.5 %collective-permute-start.5 = (bf16[256,1024]{1,0:T(8,128)(2,1)S(1)}, bf16[256,1024]{1,0:T(8,128)(2,1)S(1)}, u32[]{:S(2)}, u32[]{:S(2)}) collective-permute-start(bf16[256,1024]{1,0:T(8,128)(2,1)S(1)} %add.55), channel_id=1, source_target_pairs={{320,288},{705,737},{322,290},{707,739},{324,292},{709,741},{326,2... | collective-permute-start | bytes 1572872 | tf_op jit(solution)/shard_map/ppermute | solution.py:176
  122.7 3.8 %collective-permute-start.12 = (bf16[256,1024]{1,0:T(8,128)(2,1)S(1)}, bf16[256,1024]{1,0:T(8,128)(2,1)S(1)}, u32[]{:S(2)}, u32[]{:S(2)}) collective-permute-start(bf16[256,1024]{1,0:T(8,128)(2,1)S(1)} %bitcast.13), channel_id=1, source_target_pairs={{0,1},{1,0},{2,3},{3,2},{4,5},{5,4},{6,7},{7,6},{8,9},{9,8},{10,11... | collective-permute-start | bytes 1572872 | tf_op jit(solution)/shard_map/ppermute | solution.py:186
  129.3 12.9 %collective-permute-start.15 = (bf16[128,1024]{1,0:T(8,128)(2,1)S(1)}, bf16[128,1024]{1,0:T(8,128)(2,1)S(1)}, u32[]{:S(2)}, u32[]{:S(2)}) collective-permute-start(bf16[128,1024]{1,0:T(8,128)(2,1)S(1)} %get-tuple-element.23), channel_id=1, source_target_pairs={{0,992},{1,33},{2,994},{3,35},{4,996},{5,37},{6,998},{7,39},{8,100... | collective-permute-start | bytes 786440 | tf_op jit(solution)/shard_map/ppermute | solution.py:196
  135.5 13.1 %collective-permute-start.13 = (bf16[128,1024]{1,0:T(8,128)(2,1)S(1)}, bf16[128,1024]{1,0:T(8,128)(2,1)S(1)}, u32[]{:S(2)}, u32[]{:S(2)}) collective-permute-start(bf16[128,1024]{1,0:T(8,128)(2,1)S(1)} %get-tuple-element.21), channel_id=1, source_target_pairs={{0,64},{1,961},{2,66},{3,963},{4,68},{5,965},{6,70},{7,967},{8,72}... | collective-permute-start | bytes 786440 | tf_op jit(solution)/shard_map/ppermute | solution.py:196
  138.3 12.2 %collective-permute-start.14 = (bf16[128,1024]{1,0:T(8,128)(2,1)S(1)}, bf16[128,1024]{1,0:T(8,128)(2,1)S(1)}, u32[]{:S(2)}, u32[]{:S(2)}) collective-permute-start(bf16[128,1024]{1,0:T(8,128)(2,1)S(1)} %get-tuple-element.22), channel_id=1, source_target_pairs={{0,32},{1,993},{2,34},{3,995},{4,36},{5,997},{6,38},{7,999},{8,40}... | collective-permute-start | bytes 786440 | tf_op jit(solution)/shard_map/ppermute | solution.py:196

commit v6 on v4

--- a/solution.py
+++ b/solution.py
@@ -134,12 +134,12 @@
     tall = jax.ShapeDtypeStruct
     work = window * rows_here * cols_here
 
-    def pairs(moves, way=1):
+    def pairs(moves, ways):
         return [
             (z * sign % rows * cols + c, (z + step) * sign % rows * cols + c)
             for z, step in moves
             for c in range(cols)
-            for sign in [way * (1 - 2 * (c % 2))]
+            for sign in [ways[c % 2]]
         ]
 
     same_core = [[2 * i + k for i in range(chips)] for k in range(2)]
@@ -168,7 +168,7 @@
         have = [z + step * gap for z in have for step in (-1, 0, 1, 2)]
     stages.append([(z, 1) for z in have])
     for moves in stages:
-        halves = [h + lax.ppermute(h, BOTH, pairs(moves, way)) for h, way in zip(halves, (1, -1))]
+        halves = [h + lax.ppermute(h, BOTH, pairs(moves, (way, way))) for h, way in zip(halves, (1, -1))]
 
     total = call(own_kernel, tall((half, rows_here), F32), work)(in_specs=[VMEM] * 2)(halves[0], sparse)
     kept = call(both_kernel, tall((half, rows_here), BF16), work)(in_specs=[VMEM] * 3)(halves[1], sibling, total)
@@ -187,7 +187,7 @@
         where, left, sparse
     )
     got = [
-        lax.ppermute(part, BOTH, pairs([(z, step) for z in range(rows)]))
+        lax.ppermute(part, BOTH, pairs([(z, step) for z in range(rows)], (1, -1)))
         for part, step in zip((*sent, last), STEPS)
     ]
     ready = call(functools.partial(order_kernel, groups), quarter, 10**6)(in_specs=[SMEM] + [VMEM] * 4)(

time: 199 us -> 203 us (1.020)
  the two profiles are of different devices: /device:TPU:6 before, /device:TPU:34 now
where the time goes in v6:
time: 203 us; the launch traced here: 202 us
  waiting for transfers between devices  117 us (58%)
  starting transfers between devices  58.5 us (29%)
  blocking collectives  13.1 us (6%)
  Pallas kernels  8.25 us (4%)
  other arithmetic  3.56 us (2%)
    ppermute x10, waiting for transfers between devices, body(): lax.ppermute(h, BOTH, pairs(moves, (way, way)))  79.4 us
    all_to_all x1, waiting for transfers between devices, body(): lax.all_to_all(ready.reshape(groups, piece, cols_here), 'row', 0, 0, axis...  23.9 us
    all_to_all x1, starting transfers between devices, body(): lax.all_to_all(ready.reshape(groups, piece, cols_here), 'row', 0, 0, axis...  21.6 us
    ppermute x3, starting transfers between devices, body(): lax.ppermute(part, BOTH, pairs([(z, step) for z in range(rows)], (1, -1)))  16.8 us
    all_to_all x1, blocking collectives, body(): lax.all_to_all(square, 'col', 0, 0, axis_index_groups=same_core, tiled=True)  13.1 us
    ppermute x10, starting transfers between devices, body(): lax.ppermute(h, BOTH, pairs(moves, (way, way)))  8.14 us
    all_to_all x1, waiting for transfers between devices, body(): lax.all_to_all(kept.reshape(chips, piece, rows_here), 'col', 0, 0, axis_i...  7.88 us
    all_to_all x1, starting transfers between devices, body(): lax.all_to_all(kept.reshape(chips, piece, rows_here), 'col', 0, 0, axis_i...  7.48 us
  transfers between devices with their start and end apart: 18, of which 6 were waited for; matrix products, arithmetic and copies ran while one was open for 1% of the time, Pallas kernels for 1%

profile of v6, /device:TPU:34, one launch (start us, length us, event | category | flops | bytes accessed | tf_op | source)
XLA Modules:
  0.0 202.2 jit_solution(4314881910965517585)
XLA Ops:
  0.0 1.3 slice.3.window_ref
  1.3 0.1 pad_add_fusion.where_ref
  1.4 0.0 copy-done.1
  1.4 0.7 shard_map.37
  2.1 0.7 collective-permute-start
  2.8 0.7 collective-permute-start.7
  3.5 0.0 collective-permute-done
  3.5 0.7 collective-permute-start.1
  4.2 0.0 collective-permute-done.7
  4.2 0.2 add.57
  4.4 0.7 collective-permute-start.8
  5.1 0.0 collective-permute-done.1
  5.1 0.2 add.52
  5.3 0.7 collective-permute-start.2
  6.0 0.0 copy-done
  6.0 1.2 shard_map.38.sparse_ref
  7.2 1.9 collective-permute-start.6
  9.1 0.0 collective-permute-done.8
  9.1 0.2 add.58
  9.3 0.7 collective-permute-start.9
  10.0 0.0 collective-permute-done.2
  10.1 0.2 add.53
  10.3 0.7 collective-permute-start.3
  11.0 0.0 collective-permute-done.9
  11.0 0.2 add.59
  11.2 0.7 collective-permute-start.10
  11.9 0.0 collective-permute-done.3
  11.9 0.2 add.54
  12.1 0.7 collective-permute-start.4
  12.8 0.0 collective-permute-done.10
  12.8 0.2 add.60
  13.0 1.3 collective-permute-start.11
  14.3 0.0 collective-permute-done.4
  14.3 0.2 add.55
  14.5 1.3 collective-permute-start.5
  15.8 78.5 %collective-permute-done.11 = bf16[256,1024]{1,0:T(8,128)(2,1)S(1)} collective-permute-done((bf16[256,1024]{1,0:T(8,128)(2,1)S(1)}, bf16[256,1024]{1,0:T(8,128)(2,1)S(1)}, u32[]{:S(2)}, u32[]{:S(2)}) %collective-permute-start.11) | collective-permute-done | bytes 524320 | tf_op jit(solution)/shard_map/ppermute | solution.py:171
  94.2 0.2 add.61.left_ref
  94.4 0.7 shard_map.39.total_ref
  95.2 0.9 collective-permute-done.5
  96.1 0.2 add.56.left_ref
  96.3 0.0 collective-permute-done.6.sparse_ref
  96.3 1.5 shard_map.40
  97.8 7.5 %all-to-all-start = ((bf16[16,16,1024]{2,1,0:T(8,128)(2,1)}), bf16[16,16,1024]{2,1,0:T(8,128)(2,1)S(1)}, u32[]{:S(2)}, u32[]{:S(2)}) async-start(bf16[16,16,1024]{2,1,0:T(8,128)(2,1)} %bitcast.2), calls=%async_computation | async-start | bytes 1048576 | tf_op jit(solution)/shard_map/all_to_all | solution.py:175
  105.3 0.8 convert_bitcast_fusion
  106.1 0.1 broadcast_bitcast_fusion.1
  106.2 7.9 %all-to-all-done = bf16[16,16,1024]{2,1,0:T(8,128)(2,1)S(1)} async-done(((bf16[16,16,1024]{2,1,0:T(8,128)(2,1)}), bf16[16,16,1024]{2,1,0:T(8,128)(2,1)S(1)}, u32[]{:S(2)}, u32[]{:S(2)}) %all-to-all-start) | async-done | bytes 524320 | tf_op jit(solution)/shard_map/all_to_all | solution.py:175
  114.1 0.1 convert_reduce_fusion
  114.2 0.1 broadcast_in_dim.10
  114.3 13.1 %all_to_all.15 = bf16[16,16,1024]{2,1,0:T(8,128)(2,1)S(1)} all-to-all(bf16[16,16,1024]{2,1,0:T(8,128)(2,1)S(1)} %broadcast_in_dim.10), channel_id=1, replica_groups={{0,2,4,6,8,10,12,14,16,18,20,22,24,26,28,30},{1,3,5,7,9,11,13,15,17,19,..., dimensions={0} | all-to-all | bytes 1048576 | tf_op jit(solution)/shard_map/all_to_all | solution.py:179
  127.3 1.9 collective-permute-start.12
  129.3 1.9 collective-permute-done.12.other_ref
  131.1 1.5 shard_map.41
  132.6 1.3 shard_map.42
  133.9 1.9 collective-permute-start.15
  135.8 9.7 %collective-permute-start.13 = (bf16[128,1024]{1,0:T(8,128)(2,1)S(1)}, bf16[128,1024]{1,0:T(8,128)(2,1)S(1)}, u32[]{:S(2)}, u32[]{:S(2)}) collective-permute-start(bf16[128,1024]{1,0:T(8,128)(2,1)S(1)} %get-tuple-element.16), channel_id=1, source_target_pairs={{0,64},{1,961},{2,66},{3,963},{4,68},{5,965},{6,70},{7,967},{8,72}... | collective-permute-start | bytes 786440 | tf_op jit(solution)/shard_map/ppermute | solution.py:190
  145.6 5.1 %collective-permute-start.14 = (bf16[128,1024]{1,0:T(8,128)(2,1)S(1)}, bf16[128,1024]{1,0:T(8,128)(2,1)S(1)}, u32[]{:S(2)}, u32[]{:S(2)}) collective-permute-start(bf16[128,1024]{1,0:T(8,128)(2,1)S(1)} %get-tuple-element.17), channel_id=1, source_target_pairs={{0,32},{1,993},{2,34},{3,995},{4,36},{5,997},{6,38},{7,999},{8,40}... | collective-permute-start | bytes 786440 | tf_op jit(solution)/shard_map/ppermute | solution.py:190
  150.7 0.0 collective-permute-done.15.refs_2_
  150.7 0.0 collective-permute-done.13.refs_0_
  150.7 3.8 %collective-permute-done.14.refs_1_ = bf16[128,1024]{1,0:T(8,128)(2,1)S(1)} collective-permute-done((bf16[128,1024]{1,0:T(8,128)(2,1)S(1)}, bf16[128,1024]{1,0:T(8,128)(2,1)S(1)}, u32[]{:S(2)}, u32[]{:S(2)}) %collective-permute-start.14) | collective-permute-done | bytes 262176 | tf_op jit(solution)/shard_map/ppermute | solution.py:190
  154.6 1.4 shard_map.43
  155.9 21.6 %all-to-all-start.2 = ((bf16[8,16,1024]{2,1,0:T(8,128)(2,1)}), bf16[8,16,1024]{2,1,0:T(8,128)(2,1)S(1)}, u32[]{:S(2)}, u32[]{:S(2)}) async-start(bf16[8,16,1024]{2,1,0:T(8,128)(2,1)} %bitcast.6), calls=%async_computation.2 | async-start | bytes 524288 | tf_op jit(solution)/shard_map/all_to_all | solution.py:196
  177.5 0.1 broadcast_bitcast_fusion
  177.6 23.9 %all-to-all-done.2 = bf16[8,16,1024]{2,1,0:T(8,128)(2,1)S(1)} async-done(((bf16[8,16,1024]{2,1,0:T(8,128)(2,1)}), bf16[8,16,1024]{2,1,0:T(8,128)(2,1)S(1)}, u32[]{:S(2)}, u32[]{:S(2)}) %all-to-all-start.2) | async-done | bytes 262176 | tf_op jit(solution)/shard_map/all_to_all | solution.py:196
  201.6 0.6 multiply_convert_fusion
  (4 shorter events, 0.1 us)
Async XLA Ops:
  0.0 1.4 copy-start.1
  1.4 4.6 %copy-start = (bf16[1024,1024]{1,0:T(8,128)(2,1)S(1)}, bf16[1024,1024]{1,0:T(8,128)(2,1)}, u32[]{:S(2)}) copy-start(bf16[1024,1024]{1,0:T(8,128)(2,1)} %density_ref.1) | copy-start | bytes 6291460
  2.1 1.4 collective-permute-start
  2.8 1.4 collective-permute-start.7
  3.5 1.6 collective-permute-start.1
  4.4 4.7 %collective-permute-start.8 = (bf16[256,1024]{1,0:T(8,128)(2,1)S(1)}, bf16[256,1024]{1,0:T(8,128)(2,1)S(1)}, u32[]{:S(2)}, u32[]{:S(2)}) collective-permute-start(bf16[256,1024]{1,0:T(8,128)(2,1)S(1)} %add.57), channel_id=1, source_target_pairs={{0,768},{1,769},{2,770},{3,771},{4,772},{5,773},{6,774},{7,775},{8... | collective-permute-start | bytes 1572872 | tf_op jit(solution)/shard_map/ppermute | solution.py:171
  5.3 4.7 %collective-permute-start.2 = (bf16[256,1024]{1,0:T(8,128)(2,1)S(1)}, bf16[256,1024]{1,0:T(8,128)(2,1)S(1)}, u32[]{:S(2)}, u32[]{:S(2)}) collective-permute-start(bf16[256,1024]{1,0:T(8,128)(2,1)S(1)} %add.52), channel_id=1, source_target_pairs={{0,256},{1,257},{2,258},{3,259},{4,260},{5,261},{6,262},{7,263},{8... | collective-permute-start | bytes 1572872 | tf_op jit(solution)/shard_map/ppermute | solution.py:171
  7.2 89.1 %collective-permute-start.6 = (bf16[1024,1024]{1,0:T(8,128)(2,1)S(1)}, bf16[1024,1024]{1,0:T(8,128)(2,1)S(1)}, u32[]{:S(2)}, u32[]{:S(2)}) collective-permute-start(bf16[1024,1024]{1,0:T(8,128)(2,1)S(1)} %shard_map.38.sparse_ref), channel_id=1, source_target_pairs={{0,1},{1,0},{2,3},{3,2},{4,5},{5,4},{6,7},{7,6},{8,9},{9,8},{10,11... | collective-permute-start | bytes 6291464 | tf_op jit(solution)/shard_map/ppermute | solution.py:162
  9.3 1.6 collective-permute-start.9
  10.3 1.6 collective-permute-start.3
  11.2 1.6 collective-permute-start.10
  12.1 2.2 %collective-permute-start.4 = (bf16[256,1024]{1,0:T(8,128)(2,1)S(1)}, bf16[256,1024]{1,0:T(8,128)(2,1)S(1)}, u32[]{:S(2)}, u32[]{:S(2)}) collective-permute-start(bf16[256,1024]{1,0:T(8,128)(2,1)S(1)} %add.54), channel_id=1, source_target_pairs={{256,320},{257,321},{258,322},{259,323},{260,324},{261,325},{262,3... | collective-permute-start | bytes 1572872 | tf_op jit(solution)/shard_map/ppermute | solution.py:171
  13.0 81.3 %collective-permute-start.11 = (bf16[256,1024]{1,0:T(8,128)(2,1)S(1)}, bf16[256,1024]{1,0:T(8,128)(2,1)S(1)}, u32[]{:S(2)}, u32[]{:S(2)}) collective-permute-start(bf16[256,1024]{1,0:T(8,128)(2,1)S(1)} %add.60), channel_id=1, source_target_pairs={{704,736},{705,737},{706,738},{707,739},{708,740},{709,741},{710,7... | collective-permute-start | bytes 1572872 | tf_op jit(solution)/shard_map/ppermute | solution.py:171
  14.5 81.6 %collective-permute-start.5 = (bf16[256,1024]{1,0:T(8,128)(2,1)S(1)}, bf16[256,1024]{1,0:T(8,128)(2,1)S(1)}, u32[]{:S(2)}, u32[]{:S(2)}) collective-permute-start(bf16[256,1024]{1,0:T(8,128)(2,1)S(1)} %add.55), channel_id=1, source_target_pairs={{320,288},{321,289},{322,290},{323,291},{324,292},{325,293},{326,2... | collective-permute-start | bytes 1572872 | tf_op jit(solution)/shard_map/ppermute | solution.py:171
  97.8 16.3 %all-to-all-start = ((bf16[16,16,1024]{2,1,0:T(8,128)(2,1)}), bf16[16,16,1024]{2,1,0:T(8,128)(2,1)S(1)}, u32[]{:S(2)}, u32[]{:S(2)}) async-start(bf16[16,16,1024]{2,1,0:T(8,128)(2,1)} %bitcast.2), calls=%async_computation | async-start | bytes 1048576 | tf_op jit(solution)/shard_map/all_to_all | solution.py:175
  127.3 3.8 %collective-permute-start.12 = (bf16[256,1024]{1,0:T(8,128)(2,1)S(1)}, bf16[256,1024]{1,0:T(8,128)(2,1)S(1)}, u32[]{:S(2)}, u32[]{:S(2)}) collective-permute-start(bf16[256,1024]{1,0:T(8,128)(2,1)S(1)} %bitcast.13), channel_id=1, source_target_pairs={{0,1},{1,0},{2,3},{3,2},{4,5},{5,4},{6,7},{7,6},{8,9},{9,8},{10,11... | collective-permute-start | bytes 1572872 | tf_op jit(solution)/shard_map/ppermute | solution.py:180
  133.9 16.8 %collective-permute-start.15 = (bf16[128,1024]{1,0:T(8,128)(2,1)S(1)}, bf16[128,1024]{1,0:T(8,128)(2,1)S(1)}, u32[]{:S(2)}, u32[]{:S(2)}) collective-permute-start(bf16[128,1024]{1,0:T(8,128)(2,1)S(1)} %get-tuple-element.18), channel_id=1, source_target_pairs={{0,992},{1,33},{2,994},{3,35},{4,996},{5,37},{6,998},{7,39},{8,100... | collective-permute-start | bytes 786440 | tf_op jit(solution)/shard_map/ppermute | solution.py:190
  135.8 14.9 %collective-permute-start.13 = (bf16[128,1024]{1,0:T(8,128)(2,1)S(1)}, bf16[128,1024]{1,0:T(8,128)(2,1)S(1)}, u32[]{:S(2)}, u32[]{:S(2)}) collective-permute-start(bf16[128,1024]{1,0:T(8,128)(2,1)S(1)} %get-tuple-element.16), channel_id=1, source_target_pairs={{0,64},{1,961},{2,66},{3,963},{4,68},{5,965},{6,70},{7,967},{8,72}... | collective-permute-start | bytes 786440 | tf_op jit(solution)/shard_map/ppermute | solution.py:190
  145.6 9.0 %collective-permute-start.14 = (bf16[128,1024]{1,0:T(8,128)(2,1)S(1)}, bf16[128,1024]{1,0:T(8,128)(2,1)S(1)}, u32[]{:S(2)}, u32[]{:S(2)}) collective-permute-start(bf16[128,1024]{1,0:T(8,128)(2,1)S(1)} %get-tuple-element.17), channel_id=1, source_target_pairs={{0,32},{1,993},{2,34},{3,995},{4,36},{5,997},{6,38},{7,999},{8,40}... | collective-permute-start | bytes 786440 | tf_op jit(solution)/shard_map/ppermute | solution.py:190
  155.9 45.6 %all-to-all-start.2 = ((bf16[8,16,1024]{2,1,0:T(8,128)(2,1)}), bf16[8,16,1024]{2,1,0:T(8,128)(2,1)S(1)}, u32[]{:S(2)}, u32[]{:S(2)}) async-start(bf16[8,16,1024]{2,1,0:T(8,128)(2,1)} %bitcast.6), calls=%async_computation.2 | async-start | bytes 524288 | tf_op jit(solution)/shard_map/all_to_all | solution.py:196

commit v7 on v4

--- a/solution.py
+++ b/solution.py
@@ -160,13 +160,19 @@
     halves = [mine, lax.ppermute(sent, BOTH, swap)]
     sparse = call(mask_kernel, tall(density.shape, BF16), 10**6)(in_specs=[SMEM, VMEM])(occupancy, density)
     sibling = lax.ppermute(sparse, "col", swap)
-    have, gap, stages = [0], rows, []
+    far = rows // 4
+    have, gap, stages = [-far, 0, far, 2 * far], far, []
     while gap > 2:
         gap //= 4
         stages.append([(z, gap) for z in have])
         stages.append([(z, -gap) for z in have] + [(z + gap, gap) for z in have])
         have = [z + step * gap for z in have for step in (-1, 0, 1, 2)]
     stages.append([(z, 1) for z in have])
+    spread_out = []
+    for h, way in zip(halves, (1, -1)):
+        h = h + lax.ppermute(h, BOTH, pairs([(0, far)], way)) + lax.ppermute(h, BOTH, pairs([(0, -far)], way))
+        spread_out.append(h + lax.ppermute(h, BOTH, pairs([(far, far)], way)))
+    halves = spread_out
     for moves in stages:
         halves = [h + lax.ppermute(h, BOTH, pairs(moves, way)) for h, way in zip(halves, (1, -1))]
 

time: 199 us -> 206 us (1.035)
  waiting for transfers between devices: 73.1 us -> 87.1 us
  starting transfers between devices: 95.2 us -> 87.3 us
    ppermute x0 -> x6, starting transfers between devices: none -> 26.4 us  [the longest x2 15.8 us: body(): lax.ppermute(h, BOTH, pairs([(0, far)], way))]
    ppermute x10 -> x6, starting transfers between devices: 37.3 us -> 11.9 us  [body(): lax.ppermute(h, BOTH, pairs(moves, way))]
    ppermute x0 -> x6, waiting for transfers between devices: none -> 18.2 us  [the longest x2 9.65 us: body(): lax.ppermute(h, BOTH, pairs([(0, -far)], way))]
    ppermute x10 -> x6, waiting for transfers between devices: 33.9 us -> 23.3 us  [body(): lax.ppermute(h, BOTH, pairs(moves, way))]
    ppermute x1, starting transfers between devices: 11.6 us -> 1.92 us  [body(): sibling = lax.ppermute(sparse, 'col', swap)]
    ppermute x3, waiting for transfers between devices: 7.85 us -> 14 us  [body(): lax.ppermute(part, BOTH, pairs([(z, step) for z in range(rows)]))]
  transfers between devices with their start and end apart: 18 -> 20, of which waited for: 12 -> 11; matrix products, arithmetic and copies ran while one was open for 1% -> 1% of each run, Pallas kernels for 1% -> 1%
where the time goes in v7:
time: 206 us; the launch traced here: 202 us
  starting transfers between devices  87.3 us (42%)
  waiting for transfers between devices  87.1 us (42%)
  blocking collectives  13.9 us (7%)
  Pallas kernels  8.47 us (4%)
  other arithmetic  3.34 us (2%)
    ppermute x6, waiting for transfers between devices, body(): lax.ppermute(h, BOTH, pairs(moves, way))  23.3 us
    all_to_all x1, starting transfers between devices, body(): lax.all_to_all(ready.reshape(groups, piece, cols_here), 'row', 0, 0, axis...  22.9 us
    all_to_all x1, waiting for transfers between devices, body(): lax.all_to_all(ready.reshape(groups, piece, cols_here), 'row', 0, 0, axis...  21.6 us
    ppermute x2, starting transfers between devices, body(): lax.ppermute(h, BOTH, pairs([(0, far)], way))  15.8 us
    ppermute x3, waiting for transfers between devices, body(): lax.ppermute(part, BOTH, pairs([(z, step) for z in range(rows)]))  14 us
    all_to_all x1, blocking collectives, body(): lax.all_to_all(square, 'col', 0, 0, axis_index_groups=same_core, tiled=True)  13.9 us
    ppermute x3, starting transfers between devices, body(): lax.ppermute(part, BOTH, pairs([(z, step) for z in range(rows)]))  12.8 us
    ppermute x6, starting transfers between devices, body(): lax.ppermute(h, BOTH, pairs(moves, way))  11.9 us
  transfers between devices with their start and end apart: 20, of which 11 were waited for; matrix products, arithmetic and copies ran while one was open for 1% of the time, Pallas kernels for 1%

profile of v7, /device:TPU:6, one launch (start us, length us, event | category | flops | bytes accessed | tf_op | source)
XLA Modules:
  0.0 202.0 jit_solution(11351654496041603132)
XLA Ops:
  0.0 1.3 slice.3.window_ref
  1.3 0.1 pad_add_fusion.where_ref
  1.4 0.9 shard_map.37
  2.3 1.9 collective-permute-start
  4.2 0.0 copy-start
  4.2 14.4 %collective-permute-start.8 = (bf16[256,1024]{1,0:T(8,128)(2,1)S(1)}, bf16[256,1024]{1,0:T(8,128)(2,1)S(1)}, u32[]{:S(2)}, u32[]{:S(2)}) collective-permute-start(bf16[256,1024]{1,0:T(8,128)(2,1)S(1)} %get-tuple-element.13), channel_id=1, source_target_pairs={{0,256},{1,769},{2,258},{3,771},{4,260},{5,773},{6,262},{7,775},{8... | collective-permute-start | bytes 1572872 | tf_op jit(solution)/shard_map/ppermute | solution.py:173
  18.7 8.0 %collective-permute-start.9 = (bf16[256,1024]{1,0:T(8,128)(2,1)S(1)}, bf16[256,1024]{1,0:T(8,128)(2,1)S(1)}, u32[]{:S(2)}, u32[]{:S(2)}) collective-permute-start(bf16[256,1024]{1,0:T(8,128)(2,1)S(1)} %get-tuple-element.13), channel_id=1, source_target_pairs={{0,768},{1,257},{2,770},{3,259},{4,772},{5,261},{6,774},{7,263},{8... | collective-permute-start | bytes 1572872 | tf_op jit(solution)/shard_map/ppermute | solution.py:173
  26.7 0.0 collective-permute-done
  26.7 1.3 collective-permute-start.1
  28.0 1.3 collective-permute-start.2
  29.3 0.0 collective-permute-done.8
  29.3 9.6 %collective-permute-done.9 = bf16[256,1024]{1,0:T(8,128)(2,1)S(1)} collective-permute-done((bf16[256,1024]{1,0:T(8,128)(2,1)S(1)}, bf16[256,1024]{1,0:T(8,128)(2,1)S(1)}, u32[]{:S(2)}, u32[]{:S(2)}) %collective-permute-start.9) | collective-permute-done | bytes 524320 | tf_op jit(solution)/shard_map/ppermute | solution.py:173
  39.0 0.1 add_add_fusion
  39.1 0.7 collective-permute-start.10
  39.8 8.5 %collective-permute-done.1 = bf16[256,1024]{1,0:T(8,128)(2,1)S(1)} collective-permute-done((bf16[256,1024]{1,0:T(8,128)(2,1)S(1)}, bf16[256,1024]{1,0:T(8,128)(2,1)S(1)}, u32[]{:S(2)}, u32[]{:S(2)}) %collective-permute-start.1) | collective-permute-done | bytes 524320 | tf_op jit(solution)/shard_map/ppermute | solution.py:173
  48.3 0.0 collective-permute-done.2
  48.3 0.1 add_add_fusion.1
  48.4 0.7 collective-permute-start.3
  49.1 1.2 shard_map.38.sparse_ref
  50.3 1.9 collective-permute-start.7
  52.2 0.0 collective-permute-done.10
  52.2 0.2 add.66
  52.4 1.3 collective-permute-start.11
  53.8 0.0 collective-permute-done.3
  53.8 0.2 add.60
  54.0 1.3 collective-permute-start.4
  55.3 9.3 %collective-permute-done.11 = bf16[256,1024]{1,0:T(8,128)(2,1)S(1)} collective-permute-done((bf16[256,1024]{1,0:T(8,128)(2,1)S(1)}, bf16[256,1024]{1,0:T(8,128)(2,1)S(1)}, u32[]{:S(2)}, u32[]{:S(2)}) %collective-permute-start.11) | collective-permute-done | bytes 524320 | tf_op jit(solution)/shard_map/ppermute | solution.py:177
  64.6 0.2 add.67
  64.8 1.3 collective-permute-start.12
  66.2 0.0 collective-permute-done.4
  66.2 0.2 add.61
  66.4 5.3 %collective-permute-start.5 = (bf16[256,1024]{1,0:T(8,128)(2,1)S(1)}, bf16[256,1024]{1,0:T(8,128)(2,1)S(1)}, u32[]{:S(2)}, u32[]{:S(2)}) collective-permute-start(bf16[256,1024]{1,0:T(8,128)(2,1)S(1)} %add.61), channel_id=1, source_target_pairs={{256,320},{769,705},{258,322},{771,707},{260,324},{773,709},{262,3... | collective-permute-start | bytes 1572872 | tf_op jit(solution)/shard_map/ppermute | solution.py:177
  71.7 1.4 collective-permute-done.12
  73.1 0.2 add.68
  73.3 1.3 collective-permute-start.13
  74.6 3.7 %collective-permute-done.5 = bf16[256,1024]{1,0:T(8,128)(2,1)S(1)} collective-permute-done((bf16[256,1024]{1,0:T(8,128)(2,1)S(1)}, bf16[256,1024]{1,0:T(8,128)(2,1)S(1)}, u32[]{:S(2)}, u32[]{:S(2)}) %collective-permute-start.5) | collective-permute-done | bytes 524320 | tf_op jit(solution)/shard_map/ppermute | solution.py:177
  78.3 0.2 add.62
  78.5 1.3 collective-permute-start.6
  79.9 7.6 %collective-permute-done.13 = bf16[256,1024]{1,0:T(8,128)(2,1)S(1)} collective-permute-done((bf16[256,1024]{1,0:T(8,128)(2,1)S(1)}, bf16[256,1024]{1,0:T(8,128)(2,1)S(1)}, u32[]{:S(2)}, u32[]{:S(2)}) %collective-permute-start.13) | collective-permute-done | bytes 524320 | tf_op jit(solution)/shard_map/ppermute | solution.py:177
  87.4 0.2 add.69.left_ref
  87.6 0.7 shard_map.39.total_ref
  88.4 1.3 collective-permute-done.6
  89.7 0.2 add.63.left_ref
  89.9 1.6 shard_map.40
  91.4 7.4 %all-to-all-start = ((bf16[16,16,1024]{2,1,0:T(8,128)(2,1)}), bf16[16,16,1024]{2,1,0:T(8,128)(2,1)S(1)}, u32[]{:S(2)}, u32[]{:S(2)}) async-start(bf16[16,16,1024]{2,1,0:T(8,128)(2,1)} %bitcast.2), calls=%async_computation | async-start | bytes 1048576 | tf_op jit(solution)/shard_map/all_to_all | solution.py:181
  98.8 0.8 convert_bitcast_fusion
  99.7 0.1 broadcast_bitcast_fusion.1
  99.8 8.2 %all-to-all-done = bf16[16,16,1024]{2,1,0:T(8,128)(2,1)S(1)} async-done(((bf16[16,16,1024]{2,1,0:T(8,128)(2,1)}), bf16[16,16,1024]{2,1,0:T(8,128)(2,1)S(1)}, u32[]{:S(2)}, u32[]{:S(2)}) %all-to-all-start) | async-done | bytes 524320 | tf_op jit(solution)/shard_map/all_to_all | solution.py:181
  108.0 0.1 convert_reduce_fusion
  108.1 0.1 broadcast_in_dim.10
  108.1 13.9 %all_to_all.15 = bf16[16,16,1024]{2,1,0:T(8,128)(2,1)S(1)} all-to-all(bf16[16,16,1024]{2,1,0:T(8,128)(2,1)S(1)} %broadcast_in_dim.10), channel_id=1, replica_groups={{0,2,4,6,8,10,12,14,16,18,20,22,24,26,28,30},{1,3,5,7,9,11,13,15,17,19,..., dimensions={0} | all-to-all | bytes 1048576 | tf_op jit(solution)/shard_map/all_to_all | solution.py:185
  122.0 1.9 collective-permute-start.14
  123.9 1.9 collective-permute-done.14.other_ref
  125.8 1.5 shard_map.41
  127.3 1.3 shard_map.42
  128.6 4.0 %collective-permute-start.17 = (bf16[128,1024]{1,0:T(8,128)(2,1)S(1)}, bf16[128,1024]{1,0:T(8,128)(2,1)S(1)}, u32[]{:S(2)}, u32[]{:S(2)}) collective-permute-start(bf16[128,1024]{1,0:T(8,128)(2,1)S(1)} %get-tuple-element.18), channel_id=1, source_target_pairs={{0,992},{1,33},{2,994},{3,35},{4,996},{5,37},{6,998},{7,39},{8,100... | collective-permute-start | bytes 786440 | tf_op jit(solution)/shard_map/ppermute | solution.py:196
  132.6 4.4 %collective-permute-start.15 = (bf16[128,1024]{1,0:T(8,128)(2,1)S(1)}, bf16[128,1024]{1,0:T(8,128)(2,1)S(1)}, u32[]{:S(2)}, u32[]{:S(2)}) collective-permute-start(bf16[128,1024]{1,0:T(8,128)(2,1)S(1)} %get-tuple-element.16), channel_id=1, source_target_pairs={{0,64},{1,961},{2,66},{3,963},{4,68},{5,965},{6,70},{7,967},{8,72}... | collective-permute-start | bytes 786440 | tf_op jit(solution)/shard_map/ppermute | solution.py:196
  137.0 4.4 %collective-permute-start.16 = (bf16[128,1024]{1,0:T(8,128)(2,1)S(1)}, bf16[128,1024]{1,0:T(8,128)(2,1)S(1)}, u32[]{:S(2)}, u32[]{:S(2)}) collective-permute-start(bf16[128,1024]{1,0:T(8,128)(2,1)S(1)} %get-tuple-element.17), channel_id=1, source_target_pairs={{0,32},{1,993},{2,34},{3,995},{4,36},{5,997},{6,38},{7,999},{8,40}... | collective-permute-start | bytes 786440 | tf_op jit(solution)/shard_map/ppermute | solution.py:196
  141.5 14.0 %collective-permute-done.15.refs_0_ = bf16[128,1024]{1,0:T(8,128)(2,1)S(1)} collective-permute-done((bf16[128,1024]{1,0:T(8,128)(2,1)S(1)}, bf16[128,1024]{1,0:T(8,128)(2,1)S(1)}, u32[]{:S(2)}, u32[]{:S(2)}) %collective-permute-start.15) | collective-permute-done | bytes 262176 | tf_op jit(solution)/shard_map/ppermute | solution.py:196
  155.4 1.4 shard_map.43
  156.8 22.9 %all-to-all-start.2 = ((bf16[8,16,1024]{2,1,0:T(8,128)(2,1)}), bf16[8,16,1024]{2,1,0:T(8,128)(2,1)S(1)}, u32[]{:S(2)}, u32[]{:S(2)}) async-start(bf16[8,16,1024]{2,1,0:T(8,128)(2,1)} %bitcast.6), calls=%async_computation.2 | async-start | bytes 524288 | tf_op jit(solution)/shard_map/all_to_all | solution.py:202
  179.6 0.1 broadcast_bitcast_fusion
  179.7 21.6 %all-to-all-done.2 = bf16[8,16,1024]{2,1,0:T(8,128)(2,1)S(1)} async-done(((bf16[8,16,1024]{2,1,0:T(8,128)(2,1)}), bf16[8,16,1024]{2,1,0:T(8,128)(2,1)S(1)}, u32[]{:S(2)}, u32[]{:S(2)}) %all-to-all-start.2) | async-done | bytes 262176 | tf_op jit(solution)/shard_map/all_to_all | solution.py:202
  201.3 0.6 multiply_convert_fusion
  (8 shorter events, 0.1 us)
Async XLA Ops:
  0.0 1.4 copy-start.1
  2.3 24.4 %collective-permute-start = (bf16[256,1024]{1,0:T(8,128)(2,1)S(1)}, bf16[256,1024]{1,0:T(8,128)(2,1)S(1)}, u32[]{:S(2)}, u32[]{:S(2)}) collective-permute-start(bf16[256,1024]{1,0:T(8,128)(2,1)S(1)} %get-tuple-element.12), channel_id=1, source_target_pairs={{0,1},{1,0},{2,3},{3,2},{4,5},{5,4},{6,7},{7,6},{8,9},{9,8},{10,11... | collective-permute-start | bytes 1572872 | tf_op jit(solution)/shard_map/ppermute | solution.py:160
  4.2 44.9 %copy-start = (bf16[1024,1024]{1,0:T(8,128)(2,1)S(1)}, bf16[1024,1024]{1,0:T(8,128)(2,1)}, u32[]{:S(2)}) copy-start(bf16[1024,1024]{1,0:T(8,128)(2,1)} %density_ref.1) | copy-start | bytes 6291460
  4.2 25.1 %collective-permute-start.8 = (bf16[256,1024]{1,0:T(8,128)(2,1)S(1)}, bf16[256,1024]{1,0:T(8,128)(2,1)S(1)}, u32[]{:S(2)}, u32[]{:S(2)}) collective-permute-start(bf16[256,1024]{1,0:T(8,128)(2,1)S(1)} %get-tuple-element.13), channel_id=1, source_target_pairs={{0,256},{1,769},{2,258},{3,771},{4,260},{5,773},{6,262},{7,775},{8... | collective-permute-start | bytes 1572872 | tf_op jit(solution)/shard_map/ppermute | solution.py:173
  18.7 20.3 %collective-permute-start.9 = (bf16[256,1024]{1,0:T(8,128)(2,1)S(1)}, bf16[256,1024]{1,0:T(8,128)(2,1)S(1)}, u32[]{:S(2)}, u32[]{:S(2)}) collective-permute-start(bf16[256,1024]{1,0:T(8,128)(2,1)S(1)} %get-tuple-element.13), channel_id=1, source_target_pairs={{0,768},{1,257},{2,770},{3,259},{4,772},{5,261},{6,774},{7,263},{8... | collective-permute-start | bytes 1572872 | tf_op jit(solution)/shard_map/ppermute | solution.py:173
  26.7 21.7 %collective-permute-start.1 = (bf16[256,1024]{1,0:T(8,128)(2,1)S(1)}, bf16[256,1024]{1,0:T(8,128)(2,1)S(1)}, u32[]{:S(2)}, u32[]{:S(2)}) collective-permute-start(bf16[256,1024]{1,0:T(8,128)(2,1)S(1)} %collective-permute-done), channel_id=1, source_target_pairs={{0,768},{1,257},{2,770},{3,259},{4,772},{5,261},{6,774},{7,263},{8... | collective-permute-start | bytes 1572872 | tf_op jit(solution)/shard_map/ppermute | solution.py:173
  28.0 20.3 %collective-permute-start.2 = (bf16[256,1024]{1,0:T(8,128)(2,1)S(1)}, bf16[256,1024]{1,0:T(8,128)(2,1)S(1)}, u32[]{:S(2)}, u32[]{:S(2)}) collective-permute-start(bf16[256,1024]{1,0:T(8,128)(2,1)S(1)} %collective-permute-done), channel_id=1, source_target_pairs={{0,256},{1,769},{2,258},{3,771},{4,260},{5,773},{6,262},{7,775},{8... | collective-permute-start | bytes 1572872 | tf_op jit(solution)/shard_map/ppermute | solution.py:173
  39.1 13.1 %collective-permute-start.10 = (bf16[256,1024]{1,0:T(8,128)(2,1)S(1)}, bf16[256,1024]{1,0:T(8,128)(2,1)S(1)}, u32[]{:S(2)}, u32[]{:S(2)}) collective-permute-start(bf16[256,1024]{1,0:T(8,128)(2,1)S(1)} %add_add_fusion), channel_id=1, source_target_pairs={{256,512},{769,513},{258,514},{771,515},{260,516},{773,517},{262,5... | collective-permute-start | bytes 1572872 | tf_op jit(solution)/shard_map/ppermute | solution.py:174
  48.4 5.4 %collective-permute-start.3 = (bf16[256,1024]{1,0:T(8,128)(2,1)S(1)}, bf16[256,1024]{1,0:T(8,128)(2,1)S(1)}, u32[]{:S(2)}, u32[]{:S(2)}) collective-permute-start(bf16[256,1024]{1,0:T(8,128)(2,1)S(1)} %add_add_fusion.1), channel_id=1, source_target_pairs={{768,512},{257,513},{770,514},{259,515},{772,516},{261,517},{774,5... | collective-permute-start | bytes 1572872 | tf_op jit(solution)/shard_map/ppermute | solution.py:174
  50.3 39.6 %collective-permute-start.7 = (bf16[1024,1024]{1,0:T(8,128)(2,1)S(1)}, bf16[1024,1024]{1,0:T(8,128)(2,1)S(1)}, u32[]{:S(2)}, u32[]{:S(2)}) collective-permute-start(bf16[1024,1024]{1,0:T(8,128)(2,1)S(1)} %shard_map.38.sparse_ref), channel_id=1, source_target_pairs={{0,1},{1,0},{2,3},{3,2},{4,5},{5,4},{6,7},{7,6},{8,9},{9,8},{10,11... | collective-permute-start | bytes 6291464 | tf_op jit(solution)/shard_map/ppermute | solution.py:162
  52.4 12.2 %collective-permute-start.11 = (bf16[256,1024]{1,0:T(8,128)(2,1)S(1)}, bf16[256,1024]{1,0:T(8,128)(2,1)S(1)}, u32[]{:S(2)}, u32[]{:S(2)}) collective-permute-start(bf16[256,1024]{1,0:T(8,128)(2,1)S(1)} %add.66), channel_id=1, source_target_pairs={{768,832},{257,193},{770,834},{259,195},{772,836},{261,197},{774,8... | collective-permute-start | bytes 1572872 | tf_op jit(solution)/shard_map/ppermute | solution.py:177
  54.0 12.2 %collective-permute-start.4 = (bf16[256,1024]{1,0:T(8,128)(2,1)S(1)}, bf16[256,1024]{1,0:T(8,128)(2,1)S(1)}, u32[]{:S(2)}, u32[]{:S(2)}) collective-permute-start(bf16[256,1024]{1,0:T(8,128)(2,1)S(1)} %add.60), channel_id=1, source_target_pairs={{256,192},{769,833},{258,194},{771,835},{260,196},{773,837},{262,1... | collective-permute-start | bytes 1572872 | tf_op jit(solution)/shard_map/ppermute | solution.py:177
  64.8 8.2 %collective-permute-start.12 = (bf16[256,1024]{1,0:T(8,128)(2,1)S(1)}, bf16[256,1024]{1,0:T(8,128)(2,1)S(1)}, u32[]{:S(2)}, u32[]{:S(2)}) collective-permute-start(bf16[256,1024]{1,0:T(8,128)(2,1)S(1)} %add.67), channel_id=1, source_target_pairs={{768,704},{257,321},{770,706},{259,323},{772,708},{261,325},{774,7... | collective-permute-start | bytes 1572872 | tf_op jit(solution)/shard_map/ppermute | solution.py:177
  66.4 12.0 %collective-permute-start.5 = (bf16[256,1024]{1,0:T(8,128)(2,1)S(1)}, bf16[256,1024]{1,0:T(8,128)(2,1)S(1)}, u32[]{:S(2)}, u32[]{:S(2)}) collective-permute-start(bf16[256,1024]{1,0:T(8,128)(2,1)S(1)} %add.61), channel_id=1, source_target_pairs={{256,320},{769,705},{258,322},{771,707},{260,324},{773,709},{262,3... | collective-permute-start | bytes 1572872 | tf_op jit(solution)/shard_map/ppermute | solution.py:177
  73.3 14.2 %collective-permute-start.13 = (bf16[256,1024]{1,0:T(8,128)(2,1)S(1)}, bf16[256,1024]{1,0:T(8,128)(2,1)S(1)}, u32[]{:S(2)}, u32[]{:S(2)}) collective-permute-start(bf16[256,1024]{1,0:T(8,128)(2,1)S(1)} %add.68), channel_id=1, source_target_pairs={{704,736},{321,289},{706,738},{323,291},{708,740},{325,293},{710,7... | collective-permute-start | bytes 1572872 | tf_op jit(solution)/shard_map/ppermute | solution.py:177
  78.5 11.1 %collective-permute-start.6 = (bf16[256,1024]{1,0:T(8,128)(2,1)S(1)}, bf16[256,1024]{1,0:T(8,128)(2,1)S(1)}, u32[]{:S(2)}, u32[]{:S(2)}) collective-permute-start(bf16[256,1024]{1,0:T(8,128)(2,1)S(1)} %add.62), channel_id=1, source_target_pairs={{320,288},{705,737},{322,290},{707,739},{324,292},{709,741},{326,2... | collective-permute-start | bytes 1572872 | tf_op jit(solution)/shard_map/ppermute | solution.py:177
  91.4 16.5 %all-to-all-start = ((bf16[16,16,1024]{2,1,0:T(8,128)(2,1)}), bf16[16,16,1024]{2,1,0:T(8,128)(2,1)S(1)}, u32[]{:S(2)}, u32[]{:S(2)}) async-start(bf16[16,16,1024]{2,1,0:T(8,128)(2,1)} %bitcast.2), calls=%async_computation | async-start | bytes 1048576 | tf_op jit(solution)/shard_map/all_to_all | solution.py:181
  122.0 3.8 %collective-permute-start.14 = (bf16[256,1024]{1,0:T(8,128)(2,1)S(1)}, bf16[256,1024]{1,0:T(8,128)(2,1)S(1)}, u32[]{:S(2)}, u32[]{:S(2)}) collective-permute-start(bf16[256,1024]{1,0:T(8,128)(2,1)S(1)} %bitcast.13), channel_id=1, source_target_pairs={{0,1},{1,0},{2,3},{3,2},{4,5},{5,4},{6,7},{7,6},{8,9},{9,8},{10,11... | collective-permute-start | bytes 1572872 | tf_op jit(solution)/shard_map/ppermute | solution.py:186
  128.6 12.9 %collective-permute-start.17 = (bf16[128,1024]{1,0:T(8,128)(2,1)S(1)}, bf16[128,1024]{1,0:T(8,128)(2,1)S(1)}, u32[]{:S(2)}, u32[]{:S(2)}) collective-permute-start(bf16[128,1024]{1,0:T(8,128)(2,1)S(1)} %get-tuple-element.18), channel_id=1, source_target_pairs={{0,992},{1,33},{2,994},{3,35},{4,996},{5,37},{6,998},{7,39},{8,100... | collective-permute-start | bytes 786440 | tf_op jit(solution)/shard_map/ppermute | solution.py:196
  132.6 22.8 %collective-permute-start.15 = (bf16[128,1024]{1,0:T(8,128)(2,1)S(1)}, bf16[128,1024]{1,0:T(8,128)(2,1)S(1)}, u32[]{:S(2)}, u32[]{:S(2)}) collective-permute-start(bf16[128,1024]{1,0:T(8,128)(2,1)S(1)} %get-tuple-element.16), channel_id=1, source_target_pairs={{0,64},{1,961},{2,66},{3,963},{4,68},{5,965},{6,70},{7,967},{8,72}... | collective-permute-start | bytes 786440 | tf_op jit(solution)/shard_map/ppermute | solution.py:196
  137.0 18.4 %collective-permute-start.16 = (bf16[128,1024]{1,0:T(8,128)(2,1)S(1)}, bf16[128,1024]{1,0:T(8,128)(2,1)S(1)}, u32[]{:S(2)}, u32[]{:S(2)}) collective-permute-start(bf16[128,1024]{1,0:T(8,128)(2,1)S(1)} %get-tuple-element.17), channel_id=1, source_target_pairs={{0,32},{1,993},{2,34},{3,995},{4,36},{5,997},{6,38},{7,999},{8,40}... | collective-permute-start | bytes 786440 | tf_op jit(solution)/shard_map/ppermute | solution.py:196
  156.8 44.5 %all-to-all-start.2 = ((bf16[8,16,1024]{2,1,0:T(8,128)(2,1)}), bf16[8,16,1024]{2,1,0:T(8,128)(2,1)S(1)}, u32[]{:S(2)}, u32[]{:S(2)}) async-start(bf16[8,16,1024]{2,1,0:T(8,128)(2,1)} %bitcast.6), calls=%async_computation.2 | async-start | bytes 524288 | tf_op jit(solution)/shard_map/all_to_all | solution.py:202

commit v8 on v7

--- a/solution.py
+++ b/solution.py
@@ -170,8 +170,9 @@
     stages.append([(z, 1) for z in have])
     spread_out = []
     for h, way in zip(halves, (1, -1)):
-        h = h + lax.ppermute(h, BOTH, pairs([(0, far)], way)) + lax.ppermute(h, BOTH, pairs([(0, -far)], way))
-        spread_out.append(h + lax.ppermute(h, BOTH, pairs([(far, far)], way)))
+        near = h + lax.ppermute(h, BOTH, pairs([(0, far)], way))
+        back = lax.ppermute(h, BOTH, pairs([(0, -far)], way))
+        spread_out.append(near + back + lax.ppermute(near, BOTH, pairs([(far, far)], way)))
     halves = spread_out
     for moves in stages:
         halves = [h + lax.ppermute(h, BOTH, pairs(moves, way)) for h, way in zip(halves, (1, -1))]

time: 206 us -> 198 us (0.961)
  waiting for transfers between devices: 87.1 us -> 59.1 us
  starting transfers between devices: 87.3 us -> 108 us
    ppermute x6, waiting for transfers between devices: 18.2 us -> 0.02 us  [the longest x2 0.01 us: body(): near = h + lax.ppermute(h, BOTH, pairs([(0, far)], way))]
    ppermute x1, starting transfers between devices: 1.92 us -> 11.6 us  [body(): sibling = lax.ppermute(sparse, 'col', swap)]
    ppermute x6, starting transfers between devices: 26.4 us -> 36.1 us  [the longest x2 22.3 us: body(): near = h + lax.ppermute(h, BOTH, pairs([(0, far)], way))]
    ppermute x3, waiting for transfers between devices: 14 us -> 6.1 us  [body(): lax.ppermute(part, BOTH, pairs([(z, step) for z in range(rows)]))]
  transfers between devices with their start and end apart: 20 -> 20, of which waited for: 11 -> 10; matrix products, arithmetic and copies ran while one was open for 1% -> 1% of each run, Pallas kernels for 1% -> 1%
where the time goes in v8:
time: 198 us; the launch traced here: 195 us
  starting transfers between devices  108 us (55%)
  waiting for transfers between devices  59.1 us (30%)
  blocking collectives  13.9 us (7%)
  Pallas kernels  8.47 us (4%)
  other arithmetic  3.35 us (2%)
    all_to_all x1, starting transfers between devices, body(): lax.all_to_all(ready.reshape(groups, piece, cols_here), 'row', 0, 0, axis...  24.3 us
    ppermute x6, waiting for transfers between devices, body(): lax.ppermute(h, BOTH, pairs(moves, way))  23.4 us
    ppermute x2, starting transfers between devices, body(): near = h + lax.ppermute(h, BOTH, pairs([(0, far)], way))  22.3 us
    all_to_all x1, waiting for transfers between devices, body(): lax.all_to_all(ready.reshape(groups, piece, cols_here), 'row', 0, 0, axis...  19.5 us
    all_to_all x1, blocking collectives, body(): lax.all_to_all(square, 'col', 0, 0, axis_index_groups=same_core, tiled=True)  13.9 us
    ppermute x3, starting transfers between devices, body(): lax.ppermute(part, BOTH, pairs([(z, step) for z in range(rows)]))  12.9 us
    ppermute x2, starting transfers between devices, body(): back = lax.ppermute(h, BOTH, pairs([(0, -far)], way))  12.4 us
    ppermute x6, starting transfers between devices, body(): lax.ppermute(h, BOTH, pairs(moves, way))  11.9 us
  transfers between devices with their start and end apart: 20, of which 10 were waited for; matrix products, arithmetic and copies ran while one was open for 1% of the time, Pallas kernels for 1%

profile of v8, /device:TPU:6, one launch (start us, length us, event | category | flops | bytes accessed | tf_op | source)
XLA Modules:
  0.0 194.7 jit_solution(5900408643389350)
XLA Ops:
  0.0 1.3 slice.3.window_ref
  1.3 0.1 pad_add_fusion.where_ref
  1.4 0.9 shard_map.37
  2.3 1.9 collective-permute-start
  4.2 14.3 %collective-permute-start.8 = (bf16[256,1024]{1,0:T(8,128)(2,1)S(1)}, bf16[256,1024]{1,0:T(8,128)(2,1)S(1)}, u32[]{:S(2)}, u32[]{:S(2)}) collective-permute-start(bf16[256,1024]{1,0:T(8,128)(2,1)S(1)} %get-tuple-element.13), channel_id=1, source_target_pairs={{0,256},{1,769},{2,258},{3,771},{4,260},{5,773},{6,262},{7,775},{8... | collective-permute-start | bytes 1572872 | tf_op jit(solution)/shard_map/ppermute | solution.py:173
  18.5 0.0 collective-permute-done
  18.6 8.0 %collective-permute-start.1 = (bf16[256,1024]{1,0:T(8,128)(2,1)S(1)}, bf16[256,1024]{1,0:T(8,128)(2,1)S(1)}, u32[]{:S(2)}, u32[]{:S(2)}) collective-permute-start(bf16[256,1024]{1,0:T(8,128)(2,1)S(1)} %collective-permute-done), channel_id=1, source_target_pairs={{0,768},{1,257},{2,770},{3,259},{4,772},{5,261},{6,774},{7,263},{8... | collective-permute-start | bytes 1572872 | tf_op jit(solution)/shard_map/ppermute | solution.py:173
  26.5 1.3 collective-permute-start.9
  27.9 0.0 collective-permute-done.8
  27.9 0.2 add.64
  28.1 0.7 collective-permute-start.10
  28.8 11.1 %collective-permute-start.2 = (bf16[256,1024]{1,0:T(8,128)(2,1)S(1)}, bf16[256,1024]{1,0:T(8,128)(2,1)S(1)}, u32[]{:S(2)}, u32[]{:S(2)}) collective-permute-start(bf16[256,1024]{1,0:T(8,128)(2,1)S(1)} %collective-permute-done), channel_id=1, source_target_pairs={{0,256},{1,769},{2,258},{3,771},{4,260},{5,773},{6,262},{7,775},{8... | collective-permute-start | bytes 1572872 | tf_op jit(solution)/shard_map/ppermute | solution.py:174
  39.9 0.0 collective-permute-done.1
  39.9 0.2 add.58
  40.1 0.7 collective-permute-start.3
  40.8 1.2 shard_map.38.sparse_ref
  42.0 11.6 %collective-permute-start.7 = (bf16[1024,1024]{1,0:T(8,128)(2,1)S(1)}, bf16[1024,1024]{1,0:T(8,128)(2,1)S(1)}, u32[]{:S(2)}, u32[]{:S(2)}) collective-permute-start(bf16[1024,1024]{1,0:T(8,128)(2,1)S(1)} %shard_map.38.sparse_ref), channel_id=1, source_target_pairs={{0,1},{1,0},{2,3},{3,2},{4,5},{5,4},{6,7},{7,6},{8,9},{9,8},{10,11... | collective-permute-start | bytes 6291464 | tf_op jit(solution)/shard_map/ppermute | solution.py:162
  53.5 0.0 collective-permute-done.9
  53.6 0.0 collective-permute-done.10
  53.6 0.1 add_add_fusion
  53.7 1.3 collective-permute-start.11
  55.0 0.0 collective-permute-done.2
  55.0 0.0 collective-permute-done.3
  55.0 0.1 add_add_fusion.1
  55.1 1.3 collective-permute-start.4
  56.4 9.4 %collective-permute-done.11 = bf16[256,1024]{1,0:T(8,128)(2,1)S(1)} collective-permute-done((bf16[256,1024]{1,0:T(8,128)(2,1)S(1)}, bf16[256,1024]{1,0:T(8,128)(2,1)S(1)}, u32[]{:S(2)}, u32[]{:S(2)}) %collective-permute-start.11) | collective-permute-done | bytes 524320 | tf_op jit(solution)/shard_map/ppermute | solution.py:178
  65.8 0.2 add.67
  66.0 1.3 collective-permute-start.12
  67.4 0.0 collective-permute-done.4
  67.4 0.2 add.61
  67.6 5.3 %collective-permute-start.5 = (bf16[256,1024]{1,0:T(8,128)(2,1)S(1)}, bf16[256,1024]{1,0:T(8,128)(2,1)S(1)}, u32[]{:S(2)}, u32[]{:S(2)}) collective-permute-start(bf16[256,1024]{1,0:T(8,128)(2,1)S(1)} %add.61), channel_id=1, source_target_pairs={{256,320},{769,705},{258,322},{771,707},{260,324},{773,709},{262,3... | collective-permute-start | bytes 1572872 | tf_op jit(solution)/shard_map/ppermute | solution.py:178
  72.9 1.9 collective-permute-done.12
  74.8 0.2 add.68
  75.0 1.3 collective-permute-start.13
  76.3 3.2 %collective-permute-done.5 = bf16[256,1024]{1,0:T(8,128)(2,1)S(1)} collective-permute-done((bf16[256,1024]{1,0:T(8,128)(2,1)S(1)}, bf16[256,1024]{1,0:T(8,128)(2,1)S(1)}, u32[]{:S(2)}, u32[]{:S(2)}) %collective-permute-start.5) | collective-permute-done | bytes 524320 | tf_op jit(solution)/shard_map/ppermute | solution.py:178
  79.5 0.2 add.62
  79.7 1.3 collective-permute-start.6
  81.1 7.6 %collective-permute-done.13 = bf16[256,1024]{1,0:T(8,128)(2,1)S(1)} collective-permute-done((bf16[256,1024]{1,0:T(8,128)(2,1)S(1)}, bf16[256,1024]{1,0:T(8,128)(2,1)S(1)}, u32[]{:S(2)}, u32[]{:S(2)}) %collective-permute-start.13) | collective-permute-done | bytes 524320 | tf_op jit(solution)/shard_map/ppermute | solution.py:178
  88.6 0.2 add.69.left_ref
  88.8 0.7 shard_map.39.total_ref
  89.6 1.3 collective-permute-done.6
  90.9 0.2 add.63.left_ref
  91.1 1.6 shard_map.40
  92.6 7.4 %all-to-all-start = ((bf16[16,16,1024]{2,1,0:T(8,128)(2,1)}), bf16[16,16,1024]{2,1,0:T(8,128)(2,1)S(1)}, u32[]{:S(2)}, u32[]{:S(2)}) async-start(bf16[16,16,1024]{2,1,0:T(8,128)(2,1)} %bitcast.2), calls=%async_computation | async-start | bytes 1048576 | tf_op jit(solution)/shard_map/all_to_all | solution.py:182
  100.0 0.8 convert_bitcast_fusion
  100.9 0.1 broadcast_bitcast_fusion.1
  100.9 8.2 %all-to-all-done = bf16[16,16,1024]{2,1,0:T(8,128)(2,1)S(1)} async-done(((bf16[16,16,1024]{2,1,0:T(8,128)(2,1)}), bf16[16,16,1024]{2,1,0:T(8,128)(2,1)S(1)}, u32[]{:S(2)}, u32[]{:S(2)}) %all-to-all-start) | async-done | bytes 524320 | tf_op jit(solution)/shard_map/all_to_all | solution.py:182
  109.2 0.1 convert_reduce_fusion
  109.3 0.1 broadcast_in_dim.10
  109.3 13.9 %all_to_all.15 = bf16[16,16,1024]{2,1,0:T(8,128)(2,1)S(1)} all-to-all(bf16[16,16,1024]{2,1,0:T(8,128)(2,1)S(1)} %broadcast_in_dim.10), channel_id=1, replica_groups={{0,2,4,6,8,10,12,14,16,18,20,22,24,26,28,30},{1,3,5,7,9,11,13,15,17,19,..., dimensions={0} | all-to-all | bytes 1048576 | tf_op jit(solution)/shard_map/all_to_all | solution.py:186
  123.2 1.9 collective-permute-start.14
  125.1 1.9 collective-permute-done.14.other_ref
  127.0 1.5 shard_map.41
  128.5 1.3 shard_map.42
  129.8 5.0 %collective-permute-start.17 = (bf16[128,1024]{1,0:T(8,128)(2,1)S(1)}, bf16[128,1024]{1,0:T(8,128)(2,1)S(1)}, u32[]{:S(2)}, u32[]{:S(2)}) collective-permute-start(bf16[128,1024]{1,0:T(8,128)(2,1)S(1)} %get-tuple-element.18), channel_id=1, source_target_pairs={{0,992},{1,33},{2,994},{3,35},{4,996},{5,37},{6,998},{7,39},{8,100... | collective-permute-start | bytes 786440 | tf_op jit(solution)/shard_map/ppermute | solution.py:197
  134.8 3.5 %collective-permute-start.15 = (bf16[128,1024]{1,0:T(8,128)(2,1)S(1)}, bf16[128,1024]{1,0:T(8,128)(2,1)S(1)}, u32[]{:S(2)}, u32[]{:S(2)}) collective-permute-start(bf16[128,1024]{1,0:T(8,128)(2,1)S(1)} %get-tuple-element.16), channel_id=1, source_target_pairs={{0,64},{1,961},{2,66},{3,963},{4,68},{5,965},{6,70},{7,967},{8,72}... | collective-permute-start | bytes 786440 | tf_op jit(solution)/shard_map/ppermute | solution.py:197
  138.3 4.4 %collective-permute-start.16 = (bf16[128,1024]{1,0:T(8,128)(2,1)S(1)}, bf16[128,1024]{1,0:T(8,128)(2,1)S(1)}, u32[]{:S(2)}, u32[]{:S(2)}) collective-permute-start(bf16[128,1024]{1,0:T(8,128)(2,1)S(1)} %get-tuple-element.17), channel_id=1, source_target_pairs={{0,32},{1,993},{2,34},{3,995},{4,36},{5,997},{6,38},{7,999},{8,40}... | collective-permute-start | bytes 786440 | tf_op jit(solution)/shard_map/ppermute | solution.py:197
  142.7 4.5 %collective-permute-done.15.refs_0_ = bf16[128,1024]{1,0:T(8,128)(2,1)S(1)} collective-permute-done((bf16[128,1024]{1,0:T(8,128)(2,1)S(1)}, bf16[128,1024]{1,0:T(8,128)(2,1)S(1)}, u32[]{:S(2)}, u32[]{:S(2)}) %collective-permute-start.15) | collective-permute-done | bytes 262176 | tf_op jit(solution)/shard_map/ppermute | solution.py:197
  147.2 1.6 collective-permute-done.16.refs_1_
  148.8 1.4 shard_map.43
  150.1 24.3 %all-to-all-start.2 = ((bf16[8,16,1024]{2,1,0:T(8,128)(2,1)}), bf16[8,16,1024]{2,1,0:T(8,128)(2,1)S(1)}, u32[]{:S(2)}, u32[]{:S(2)}) async-start(bf16[8,16,1024]{2,1,0:T(8,128)(2,1)} %bitcast.6), calls=%async_computation.2 | async-start | bytes 524288 | tf_op jit(solution)/shard_map/all_to_all | solution.py:203
  174.4 0.1 broadcast_bitcast_fusion
  174.5 19.5 %all-to-all-done.2 = bf16[8,16,1024]{2,1,0:T(8,128)(2,1)S(1)} async-done(((bf16[8,16,1024]{2,1,0:T(8,128)(2,1)}), bf16[8,16,1024]{2,1,0:T(8,128)(2,1)S(1)}, u32[]{:S(2)}, u32[]{:S(2)}) %all-to-all-start.2) | async-done | bytes 262176 | tf_op jit(solution)/shard_map/all_to_all | solution.py:203
  194.1 0.6 multiply_convert_fusion
  (8 shorter events, 0.1 us)
Async XLA Ops:
  0.0 1.4 copy-start.1
  1.4 39.4 %copy-start = (bf16[1024,1024]{1,0:T(8,128)(2,1)S(1)}, bf16[1024,1024]{1,0:T(8,128)(2,1)}, u32[]{:S(2)}) copy-start(bf16[1024,1024]{1,0:T(8,128)(2,1)} %density_ref.1) | copy-start | bytes 6291460
  2.3 16.2 %collective-permute-start = (bf16[256,1024]{1,0:T(8,128)(2,1)S(1)}, bf16[256,1024]{1,0:T(8,128)(2,1)S(1)}, u32[]{:S(2)}, u32[]{:S(2)}) collective-permute-start(bf16[256,1024]{1,0:T(8,128)(2,1)S(1)} %get-tuple-element.12), channel_id=1, source_target_pairs={{0,1},{1,0},{2,3},{3,2},{4,5},{5,4},{6,7},{7,6},{8,9},{9,8},{10,11... | collective-permute-start | bytes 1572872 | tf_op jit(solution)/shard_map/ppermute | solution.py:160
  4.2 23.6 %collective-permute-start.8 = (bf16[256,1024]{1,0:T(8,128)(2,1)S(1)}, bf16[256,1024]{1,0:T(8,128)(2,1)S(1)}, u32[]{:S(2)}, u32[]{:S(2)}) collective-permute-start(bf16[256,1024]{1,0:T(8,128)(2,1)S(1)} %get-tuple-element.13), channel_id=1, source_target_pairs={{0,256},{1,769},{2,258},{3,771},{4,260},{5,773},{6,262},{7,775},{8... | collective-permute-start | bytes 1572872 | tf_op jit(solution)/shard_map/ppermute | solution.py:173
  18.6 21.3 %collective-permute-start.1 = (bf16[256,1024]{1,0:T(8,128)(2,1)S(1)}, bf16[256,1024]{1,0:T(8,128)(2,1)S(1)}, u32[]{:S(2)}, u32[]{:S(2)}) collective-permute-start(bf16[256,1024]{1,0:T(8,128)(2,1)S(1)} %collective-permute-done), channel_id=1, source_target_pairs={{0,768},{1,257},{2,770},{3,259},{4,772},{5,261},{6,774},{7,263},{8... | collective-permute-start | bytes 1572872 | tf_op jit(solution)/shard_map/ppermute | solution.py:173
  26.5 27.0 %collective-permute-start.9 = (bf16[256,1024]{1,0:T(8,128)(2,1)S(1)}, bf16[256,1024]{1,0:T(8,128)(2,1)S(1)}, u32[]{:S(2)}, u32[]{:S(2)}) collective-permute-start(bf16[256,1024]{1,0:T(8,128)(2,1)S(1)} %get-tuple-element.13), channel_id=1, source_target_pairs={{0,768},{1,257},{2,770},{3,259},{4,772},{5,261},{6,774},{7,263},{8... | collective-permute-start | bytes 1572872 | tf_op jit(solution)/shard_map/ppermute | solution.py:174
  28.1 25.5 %collective-permute-start.10 = (bf16[256,1024]{1,0:T(8,128)(2,1)S(1)}, bf16[256,1024]{1,0:T(8,128)(2,1)S(1)}, u32[]{:S(2)}, u32[]{:S(2)}) collective-permute-start(bf16[256,1024]{1,0:T(8,128)(2,1)S(1)} %add.64), channel_id=1, source_target_pairs={{256,512},{769,513},{258,514},{771,515},{260,516},{773,517},{262,5... | collective-permute-start | bytes 1572872 | tf_op jit(solution)/shard_map/ppermute | solution.py:175
  28.8 26.2 %collective-permute-start.2 = (bf16[256,1024]{1,0:T(8,128)(2,1)S(1)}, bf16[256,1024]{1,0:T(8,128)(2,1)S(1)}, u32[]{:S(2)}, u32[]{:S(2)}) collective-permute-start(bf16[256,1024]{1,0:T(8,128)(2,1)S(1)} %collective-permute-done), channel_id=1, source_target_pairs={{0,256},{1,769},{2,258},{3,771},{4,260},{5,773},{6,262},{7,775},{8... | collective-permute-start | bytes 1572872 | tf_op jit(solution)/shard_map/ppermute | solution.py:174
  40.1 14.9 %collective-permute-start.3 = (bf16[256,1024]{1,0:T(8,128)(2,1)S(1)}, bf16[256,1024]{1,0:T(8,128)(2,1)S(1)}, u32[]{:S(2)}, u32[]{:S(2)}) collective-permute-start(bf16[256,1024]{1,0:T(8,128)(2,1)S(1)} %add.58), channel_id=1, source_target_pairs={{768,512},{257,513},{770,514},{259,515},{772,516},{261,517},{774,5... | collective-permute-start | bytes 1572872 | tf_op jit(solution)/shard_map/ppermute | solution.py:175
  42.0 49.1 %collective-permute-start.7 = (bf16[1024,1024]{1,0:T(8,128)(2,1)S(1)}, bf16[1024,1024]{1,0:T(8,128)(2,1)S(1)}, u32[]{:S(2)}, u32[]{:S(2)}) collective-permute-start(bf16[1024,1024]{1,0:T(8,128)(2,1)S(1)} %shard_map.38.sparse_ref), channel_id=1, source_target_pairs={{0,1},{1,0},{2,3},{3,2},{4,5},{5,4},{6,7},{7,6},{8,9},{9,8},{10,11... | collective-permute-start | bytes 6291464 | tf_op jit(solution)/shard_map/ppermute | solution.py:162
  53.7 12.2 %collective-permute-start.11 = (bf16[256,1024]{1,0:T(8,128)(2,1)S(1)}, bf16[256,1024]{1,0:T(8,128)(2,1)S(1)}, u32[]{:S(2)}, u32[]{:S(2)}) collective-permute-start(bf16[256,1024]{1,0:T(8,128)(2,1)S(1)} %add_add_fusion), channel_id=1, source_target_pairs={{768,832},{257,193},{770,834},{259,195},{772,836},{261,197},{774,8... | collective-permute-start | bytes 1572872 | tf_op jit(solution)/shard_map/ppermute | solution.py:178
  55.1 12.3 %collective-permute-start.4 = (bf16[256,1024]{1,0:T(8,128)(2,1)S(1)}, bf16[256,1024]{1,0:T(8,128)(2,1)S(1)}, u32[]{:S(2)}, u32[]{:S(2)}) collective-permute-start(bf16[256,1024]{1,0:T(8,128)(2,1)S(1)} %add_add_fusion.1), channel_id=1, source_target_pairs={{256,192},{769,833},{258,194},{771,835},{260,196},{773,837},{262,1... | collective-permute-start | bytes 1572872 | tf_op jit(solution)/shard_map/ppermute | solution.py:178
  66.0 8.8 %collective-permute-start.12 = (bf16[256,1024]{1,0:T(8,128)(2,1)S(1)}, bf16[256,1024]{1,0:T(8,128)(2,1)S(1)}, u32[]{:S(2)}, u32[]{:S(2)}) collective-permute-start(bf16[256,1024]{1,0:T(8,128)(2,1)S(1)} %add.67), channel_id=1, source_target_pairs={{768,704},{257,321},{770,706},{259,323},{772,708},{261,325},{774,7... | collective-permute-start | bytes 1572872 | tf_op jit(solution)/shard_map/ppermute | solution.py:178
  67.6 12.0 %collective-permute-start.5 = (bf16[256,1024]{1,0:T(8,128)(2,1)S(1)}, bf16[256,1024]{1,0:T(8,128)(2,1)S(1)}, u32[]{:S(2)}, u32[]{:S(2)}) collective-permute-start(bf16[256,1024]{1,0:T(8,128)(2,1)S(1)} %add.61), channel_id=1, source_target_pairs={{256,320},{769,705},{258,322},{771,707},{260,324},{773,709},{262,3... | collective-permute-start | bytes 1572872 | tf_op jit(solution)/shard_map/ppermute | solution.py:178
  75.0 13.6 %collective-permute-start.13 = (bf16[256,1024]{1,0:T(8,128)(2,1)S(1)}, bf16[256,1024]{1,0:T(8,128)(2,1)S(1)}, u32[]{:S(2)}, u32[]{:S(2)}) collective-permute-start(bf16[256,1024]{1,0:T(8,128)(2,1)S(1)} %add.68), channel_id=1, source_target_pairs={{704,736},{321,289},{706,738},{323,291},{708,740},{325,293},{710,7... | collective-permute-start | bytes 1572872 | tf_op jit(solution)/shard_map/ppermute | solution.py:178
  79.7 11.1 %collective-permute-start.6 = (bf16[256,1024]{1,0:T(8,128)(2,1)S(1)}, bf16[256,1024]{1,0:T(8,128)(2,1)S(1)}, u32[]{:S(2)}, u32[]{:S(2)}) collective-permute-start(bf16[256,1024]{1,0:T(8,128)(2,1)S(1)} %add.62), channel_id=1, source_target_pairs={{320,288},{705,737},{322,290},{707,739},{324,292},{709,741},{326,2... | collective-permute-start | bytes 1572872 | tf_op jit(solution)/shard_map/ppermute | solution.py:178
  92.6 16.5 %all-to-all-start = ((bf16[16,16,1024]{2,1,0:T(8,128)(2,1)}), bf16[16,16,1024]{2,1,0:T(8,128)(2,1)S(1)}, u32[]{:S(2)}, u32[]{:S(2)}) async-start(bf16[16,16,1024]{2,1,0:T(8,128)(2,1)} %bitcast.2), calls=%async_computation | async-start | bytes 1048576 | tf_op jit(solution)/shard_map/all_to_all | solution.py:182
  123.2 3.8 %collective-permute-start.14 = (bf16[256,1024]{1,0:T(8,128)(2,1)S(1)}, bf16[256,1024]{1,0:T(8,128)(2,1)S(1)}, u32[]{:S(2)}, u32[]{:S(2)}) collective-permute-start(bf16[256,1024]{1,0:T(8,128)(2,1)S(1)} %bitcast.13), channel_id=1, source_target_pairs={{0,1},{1,0},{2,3},{3,2},{4,5},{5,4},{6,7},{7,6},{8,9},{9,8},{10,11... | collective-permute-start | bytes 1572872 | tf_op jit(solution)/shard_map/ppermute | solution.py:187
  129.8 12.9 %collective-permute-start.17 = (bf16[128,1024]{1,0:T(8,128)(2,1)S(1)}, bf16[128,1024]{1,0:T(8,128)(2,1)S(1)}, u32[]{:S(2)}, u32[]{:S(2)}) collective-permute-start(bf16[128,1024]{1,0:T(8,128)(2,1)S(1)} %get-tuple-element.18), channel_id=1, source_target_pairs={{0,992},{1,33},{2,994},{3,35},{4,996},{5,37},{6,998},{7,39},{8,100... | collective-permute-start | bytes 786440 | tf_op jit(solution)/shard_map/ppermute | solution.py:197
  134.8 12.4 %collective-permute-start.15 = (bf16[128,1024]{1,0:T(8,128)(2,1)S(1)}, bf16[128,1024]{1,0:T(8,128)(2,1)S(1)}, u32[]{:S(2)}, u32[]{:S(2)}) collective-permute-start(bf16[128,1024]{1,0:T(8,128)(2,1)S(1)} %get-tuple-element.16), channel_id=1, source_target_pairs={{0,64},{1,961},{2,66},{3,963},{4,68},{5,965},{6,70},{7,967},{8,72}... | collective-permute-start | bytes 786440 | tf_op jit(solution)/shard_map/ppermute | solution.py:197
  138.3 10.5 %collective-permute-start.16 = (bf16[128,1024]{1,0:T(8,128)(2,1)S(1)}, bf16[128,1024]{1,0:T(8,128)(2,1)S(1)}, u32[]{:S(2)}, u32[]{:S(2)}) collective-permute-start(bf16[128,1024]{1,0:T(8,128)(2,1)S(1)} %get-tuple-element.17), channel_id=1, source_target_pairs={{0,32},{1,993},{2,34},{3,995},{4,36},{5,997},{6,38},{7,999},{8,40}... | collective-permute-start | bytes 786440 | tf_op jit(solution)/shard_map/ppermute | solution.py:197
  150.1 43.9 %all-to-all-start.2 = ((bf16[8,16,1024]{2,1,0:T(8,128)(2,1)}), bf16[8,16,1024]{2,1,0:T(8,128)(2,1)S(1)}, u32[]{:S(2)}, u32[]{:S(2)}) async-start(bf16[8,16,1024]{2,1,0:T(8,128)(2,1)} %bitcast.6), calls=%async_computation.2 | async-start | bytes 524288 | tf_op jit(solution)/shard_map/all_to_all | solution.py:203

commit v9 on v8

--- a/solution.py
+++ b/solution.py
@@ -106,7 +106,10 @@
 
 
 def spread(member, groups):
-    return (member + (1 - member % 2) * (groups // 2)) % groups if groups % 4 == 0 else member
+    if groups % 4:
+        return member
+    away = (member + groups // 2) % groups
+    return away + member % 2 * ((groups - away) % groups - away)
 
 
 def order_kernel(groups, where_ref, kept_ref, *refs):

time: 198 us -> 198 us (level)
  the two profiles are of different devices: /device:TPU:6 before, /device:TPU:32 now
where the time goes in v9:
time: 198 us
  waiting for transfers between devices  112 us (57%)
  starting transfers between devices  58.2 us (29%)
  blocking collectives  14 us (7%)
  Pallas kernels  8.27 us (4%)
  other arithmetic  3.36 us (2%)
    ppermute x6, waiting for transfers between devices, body(): lax.ppermute(h, BOTH, pairs(moves, way))  73.4 us
    all_to_all x1, starting transfers between devices, body(): lax.all_to_all(ready.reshape(groups, piece, cols_here), 'row', 0, 0, axis...  23.7 us
    all_to_all x1, waiting for transfers between devices, body(): lax.all_to_all(ready.reshape(groups, piece, cols_here), 'row', 0, 0, axis...  21.2 us
    all_to_all x1, blocking collectives, body(): lax.all_to_all(square, 'col', 0, 0, axis_index_groups=same_core, tiled=True)  14 us
    ppermute x3, starting transfers between devices, body(): lax.ppermute(part, BOTH, pairs([(z, step) for z in range(rows)]))  13.4 us
    all_to_all x1, waiting for transfers between devices, body(): lax.all_to_all(kept.reshape(chips, piece, rows_here), 'col', 0, 0, axis_i...  10.8 us
    all_to_all x1, starting transfers between devices, body(): lax.all_to_all(kept.reshape(chips, piece, rows_here), 'col', 0, 0, axis_i...  7.03 us
    ppermute x6, starting transfers between devices, body(): lax.ppermute(h, BOTH, pairs(moves, way))  5.36 us
  transfers between devices with their start and end apart: 20, of which 7 were waited for; matrix products, arithmetic and copies ran while one was open for 1% of the time, Pallas kernels for 1%

profile of v9, /device:TPU:32, one launch (start us, length us, event | category | flops | bytes accessed | tf_op | source)
XLA Modules:
  0.0 197.5 jit_solution(12574709572163910236)
XLA Ops:
  0.0 1.3 slice.3.window_ref
  1.3 0.1 pad_add_fusion.where_ref
  1.4 0.7 shard_map.37
  2.1 0.7 collective-permute-start
  2.8 0.7 collective-permute-start.8
  3.5 0.0 collective-permute-done
  3.5 0.7 collective-permute-start.1
  4.2 0.7 collective-permute-start.9
  4.9 0.0 collective-permute-done.8
  4.9 0.2 add.64
  5.1 0.7 collective-permute-start.10
  5.8 0.7 collective-permute-start.2
  6.5 0.0 collective-permute-done.1
  6.5 0.2 add.58
  6.7 0.7 collective-permute-start.3
  7.4 1.2 shard_map.38.sparse_ref
  8.6 1.9 collective-permute-start.7
  10.5 0.0 collective-permute-done.9
  10.6 0.1 add_add_fusion
  10.6 0.7 collective-permute-start.11
  11.4 0.0 collective-permute-done.3
  11.4 0.1 add_add_fusion.1
  11.5 0.7 collective-permute-start.4
  12.2 0.0 collective-permute-done.11
  12.2 0.2 add.67
  12.4 0.7 collective-permute-start.12
  13.1 0.0 collective-permute-done.4
  13.1 0.2 add.61
  13.3 0.7 collective-permute-start.5
  14.0 0.0 collective-permute-done.12
  14.0 0.2 add.68
  14.2 1.3 collective-permute-start.13
  15.5 0.0 collective-permute-done.5
  15.5 0.2 add.62
  15.7 1.3 collective-permute-start.6
  17.0 72.2 %collective-permute-done.13 = bf16[256,1024]{1,0:T(8,128)(2,1)S(1)} collective-permute-done((bf16[256,1024]{1,0:T(8,128)(2,1)S(1)}, bf16[256,1024]{1,0:T(8,128)(2,1)S(1)}, u32[]{:S(2)}, u32[]{:S(2)}) %collective-permute-start.13) | collective-permute-done | bytes 524320 | tf_op jit(solution)/shard_map/ppermute | solution.py:181
  89.2 0.2 add.69.left_ref
  89.4 0.7 shard_map.39.total_ref
  90.1 1.2 collective-permute-done.6
  91.3 0.2 add.63.left_ref
  91.5 0.0 collective-permute-done.7.sparse_ref
  91.5 1.6 shard_map.40
  93.1 7.0 %all-to-all-start = ((bf16[16,16,1024]{2,1,0:T(8,128)(2,1)}), bf16[16,16,1024]{2,1,0:T(8,128)(2,1)S(1)}, u32[]{:S(2)}, u32[]{:S(2)}) async-start(bf16[16,16,1024]{2,1,0:T(8,128)(2,1)} %bitcast.2), calls=%async_computation | async-start | bytes 1048576 | tf_op jit(solution)/shard_map/all_to_all | solution.py:185
  100.2 0.8 convert_bitcast_fusion
  101.0 0.1 broadcast_bitcast_fusion.1
  101.1 10.8 %all-to-all-done = bf16[16,16,1024]{2,1,0:T(8,128)(2,1)S(1)} async-done(((bf16[16,16,1024]{2,1,0:T(8,128)(2,1)}), bf16[16,16,1024]{2,1,0:T(8,128)(2,1)S(1)}, u32[]{:S(2)}, u32[]{:S(2)}) %all-to-all-start) | async-done | bytes 524320 | tf_op jit(solution)/shard_map/all_to_all | solution.py:185
  111.9 0.1 convert_reduce_fusion
  112.0 0.1 broadcast_in_dim.10
  112.1 14.0 %all_to_all.15 = bf16[16,16,1024]{2,1,0:T(8,128)(2,1)S(1)} all-to-all(bf16[16,16,1024]{2,1,0:T(8,128)(2,1)S(1)} %broadcast_in_dim.10), channel_id=1, replica_groups={{0,2,4,6,8,10,12,14,16,18,20,22,24,26,28,30},{1,3,5,7,9,11,13,15,17,19,..., dimensions={0} | all-to-all | bytes 1048576 | tf_op jit(solution)/shard_map/all_to_all | solution.py:189
  126.1 1.9 collective-permute-start.14
  128.0 1.9 collective-permute-done.14.other_ref
  129.9 1.5 shard_map.41
  131.4 1.3 shard_map.42
  132.7 1.9 collective-permute-start.17
  134.6 6.3 %collective-permute-start.15 = (bf16[128,1024]{1,0:T(8,128)(2,1)S(1)}, bf16[128,1024]{1,0:T(8,128)(2,1)S(1)}, u32[]{:S(2)}, u32[]{:S(2)}) collective-permute-start(bf16[128,1024]{1,0:T(8,128)(2,1)S(1)} %get-tuple-element.16), channel_id=1, source_target_pairs={{0,64},{1,961},{2,66},{3,963},{4,68},{5,965},{6,70},{7,967},{8,72}... | collective-permute-start | bytes 786440 | tf_op jit(solution)/shard_map/ppermute | solution.py:200
  140.9 5.1 %collective-permute-start.16 = (bf16[128,1024]{1,0:T(8,128)(2,1)S(1)}, bf16[128,1024]{1,0:T(8,128)(2,1)S(1)}, u32[]{:S(2)}, u32[]{:S(2)}) collective-permute-start(bf16[128,1024]{1,0:T(8,128)(2,1)S(1)} %get-tuple-element.17), channel_id=1, source_target_pairs={{0,32},{1,993},{2,34},{3,995},{4,36},{5,997},{6,38},{7,999},{8,40}... | collective-permute-start | bytes 786440 | tf_op jit(solution)/shard_map/ppermute | solution.py:200
  146.1 0.0 collective-permute-done.17.refs_2_
  146.1 1.3 collective-permute-done.15.refs_0_
  147.4 3.1 %collective-permute-done.16.refs_1_ = bf16[128,1024]{1,0:T(8,128)(2,1)S(1)} collective-permute-done((bf16[128,1024]{1,0:T(8,128)(2,1)S(1)}, bf16[128,1024]{1,0:T(8,128)(2,1)S(1)}, u32[]{:S(2)}, u32[]{:S(2)}) %collective-permute-start.16) | collective-permute-done | bytes 262176 | tf_op jit(solution)/shard_map/ppermute | solution.py:200
  150.5 1.4 shard_map.43
  151.8 23.7 %all-to-all-start.2 = ((bf16[8,16,1024]{2,1,0:T(8,128)(2,1)}), bf16[8,16,1024]{2,1,0:T(8,128)(2,1)S(1)}, u32[]{:S(2)}, u32[]{:S(2)}) async-start(bf16[8,16,1024]{2,1,0:T(8,128)(2,1)} %bitcast.6), calls=%async_computation.2 | async-start | bytes 524288 | tf_op jit(solution)/shard_map/all_to_all | solution.py:206
  175.6 0.1 broadcast_bitcast_fusion
  175.6 21.2 %all-to-all-done.2 = bf16[8,16,1024]{2,1,0:T(8,128)(2,1)S(1)} async-done(((bf16[8,16,1024]{2,1,0:T(8,128)(2,1)}), bf16[8,16,1024]{2,1,0:T(8,128)(2,1)S(1)}, u32[]{:S(2)}, u32[]{:S(2)}) %all-to-all-start.2) | async-done | bytes 262176 | tf_op jit(solution)/shard_map/all_to_all | solution.py:206
  196.9 0.6 multiply_convert_fusion
  (8 shorter events, 0.1 us)
Async XLA Ops:
  0.0 1.4 copy-start.1
  1.4 6.0 %copy-start = (bf16[1024,1024]{1,0:T(8,128)(2,1)S(1)}, bf16[1024,1024]{1,0:T(8,128)(2,1)}, u32[]{:S(2)}) copy-start(bf16[1024,1024]{1,0:T(8,128)(2,1)} %density_ref.1) | copy-start | bytes 6291460
  2.1 1.4 collective-permute-start
  2.8 2.1 %collective-permute-start.8 = (bf16[256,1024]{1,0:T(8,128)(2,1)S(1)}, bf16[256,1024]{1,0:T(8,128)(2,1)S(1)}, u32[]{:S(2)}, u32[]{:S(2)}) collective-permute-start(bf16[256,1024]{1,0:T(8,128)(2,1)S(1)} %get-tuple-element.13), channel_id=1, source_target_pairs={{0,256},{1,769},{2,258},{3,771},{4,260},{5,773},{6,262},{7,775},{8... | collective-permute-start | bytes 1572872 | tf_op jit(solution)/shard_map/ppermute | solution.py:176
  3.5 3.0 %collective-permute-start.1 = (bf16[256,1024]{1,0:T(8,128)(2,1)S(1)}, bf16[256,1024]{1,0:T(8,128)(2,1)S(1)}, u32[]{:S(2)}, u32[]{:S(2)}) collective-permute-start(bf16[256,1024]{1,0:T(8,128)(2,1)S(1)} %collective-permute-done), channel_id=1, source_target_pairs={{0,768},{1,257},{2,770},{3,259},{4,772},{5,261},{6,774},{7,263},{8... | collective-permute-start | bytes 1572872 | tf_op jit(solution)/shard_map/ppermute | solution.py:176
  4.2 6.3 %collective-permute-start.9 = (bf16[256,1024]{1,0:T(8,128)(2,1)S(1)}, bf16[256,1024]{1,0:T(8,128)(2,1)S(1)}, u32[]{:S(2)}, u32[]{:S(2)}) collective-permute-start(bf16[256,1024]{1,0:T(8,128)(2,1)S(1)} %get-tuple-element.13), channel_id=1, source_target_pairs={{0,768},{1,257},{2,770},{3,259},{4,772},{5,261},{6,774},{7,263},{8... | collective-permute-start | bytes 1572872 | tf_op jit(solution)/shard_map/ppermute | solution.py:177
  5.1 5.4 %collective-permute-start.10 = (bf16[256,1024]{1,0:T(8,128)(2,1)S(1)}, bf16[256,1024]{1,0:T(8,128)(2,1)S(1)}, u32[]{:S(2)}, u32[]{:S(2)}) collective-permute-start(bf16[256,1024]{1,0:T(8,128)(2,1)S(1)} %add.64), channel_id=1, source_target_pairs={{256,512},{769,513},{258,514},{771,515},{260,516},{773,517},{262,5... | collective-permute-start | bytes 1572872 | tf_op jit(solution)/shard_map/ppermute | solution.py:178
  5.8 5.5 %collective-permute-start.2 = (bf16[256,1024]{1,0:T(8,128)(2,1)S(1)}, bf16[256,1024]{1,0:T(8,128)(2,1)S(1)}, u32[]{:S(2)}, u32[]{:S(2)}) collective-permute-start(bf16[256,1024]{1,0:T(8,128)(2,1)S(1)} %collective-permute-done), channel_id=1, source_target_pairs={{0,256},{1,769},{2,258},{3,771},{4,260},{5,773},{6,262},{7,775},{8... | collective-permute-start | bytes 1572872 | tf_op jit(solution)/shard_map/ppermute | solution.py:177
  6.7 4.6 %collective-permute-start.3 = (bf16[256,1024]{1,0:T(8,128)(2,1)S(1)}, bf16[256,1024]{1,0:T(8,128)(2,1)S(1)}, u32[]{:S(2)}, u32[]{:S(2)}) collective-permute-start(bf16[256,1024]{1,0:T(8,128)(2,1)S(1)} %add.58), channel_id=1, source_target_pairs={{768,512},{257,513},{770,514},{259,515},{772,516},{261,517},{774,5... | collective-permute-start | bytes 1572872 | tf_op jit(solution)/shard_map/ppermute | solution.py:178
  8.6 82.9 %collective-permute-start.7 = (bf16[1024,1024]{1,0:T(8,128)(2,1)S(1)}, bf16[1024,1024]{1,0:T(8,128)(2,1)S(1)}, u32[]{:S(2)}, u32[]{:S(2)}) collective-permute-start(bf16[1024,1024]{1,0:T(8,128)(2,1)S(1)} %shard_map.38.sparse_ref), channel_id=1, source_target_pairs={{0,1},{1,0},{2,3},{3,2},{4,5},{5,4},{6,7},{7,6},{8,9},{9,8},{10,11... | collective-permute-start | bytes 6291464 | tf_op jit(solution)/shard_map/ppermute | solution.py:165
  10.6 1.5 collective-permute-start.11
  11.5 1.6 collective-permute-start.4
  12.4 1.6 collective-permute-start.12
  13.3 2.2 %collective-permute-start.5 = (bf16[256,1024]{1,0:T(8,128)(2,1)S(1)}, bf16[256,1024]{1,0:T(8,128)(2,1)S(1)}, u32[]{:S(2)}, u32[]{:S(2)}) collective-permute-start(bf16[256,1024]{1,0:T(8,128)(2,1)S(1)} %add.61), channel_id=1, source_target_pairs={{256,320},{769,705},{258,322},{771,707},{260,324},{773,709},{262,3... | collective-permute-start | bytes 1572872 | tf_op jit(solution)/shard_map/ppermute | solution.py:181
  14.2 75.0 %collective-permute-start.13 = (bf16[256,1024]{1,0:T(8,128)(2,1)S(1)}, bf16[256,1024]{1,0:T(8,128)(2,1)S(1)}, u32[]{:S(2)}, u32[]{:S(2)}) collective-permute-start(bf16[256,1024]{1,0:T(8,128)(2,1)S(1)} %add.68), channel_id=1, source_target_pairs={{704,736},{321,289},{706,738},{323,291},{708,740},{325,293},{710,7... | collective-permute-start | bytes 1572872 | tf_op jit(solution)/shard_map/ppermute | solution.py:181
  15.7 75.6 %collective-permute-start.6 = (bf16[256,1024]{1,0:T(8,128)(2,1)S(1)}, bf16[256,1024]{1,0:T(8,128)(2,1)S(1)}, u32[]{:S(2)}, u32[]{:S(2)}) collective-permute-start(bf16[256,1024]{1,0:T(8,128)(2,1)S(1)} %add.62), channel_id=1, source_target_pairs={{320,288},{705,737},{322,290},{707,739},{324,292},{709,741},{326,2... | collective-permute-start | bytes 1572872 | tf_op jit(solution)/shard_map/ppermute | solution.py:181
  93.1 18.9 %all-to-all-start = ((bf16[16,16,1024]{2,1,0:T(8,128)(2,1)}), bf16[16,16,1024]{2,1,0:T(8,128)(2,1)S(1)}, u32[]{:S(2)}, u32[]{:S(2)}) async-start(bf16[16,16,1024]{2,1,0:T(8,128)(2,1)} %bitcast.2), calls=%async_computation | async-start | bytes 1048576 | tf_op jit(solution)/shard_map/all_to_all | solution.py:185
  126.1 3.8 %collective-permute-start.14 = (bf16[256,1024]{1,0:T(8,128)(2,1)S(1)}, bf16[256,1024]{1,0:T(8,128)(2,1)S(1)}, u32[]{:S(2)}, u32[]{:S(2)}) collective-permute-start(bf16[256,1024]{1,0:T(8,128)(2,1)S(1)} %bitcast.13), channel_id=1, source_target_pairs={{0,1},{1,0},{2,3},{3,2},{4,5},{5,4},{6,7},{7,6},{8,9},{9,8},{10,11... | collective-permute-start | bytes 1572872 | tf_op jit(solution)/shard_map/ppermute | solution.py:190
  132.7 13.4 %collective-permute-start.17 = (bf16[128,1024]{1,0:T(8,128)(2,1)S(1)}, bf16[128,1024]{1,0:T(8,128)(2,1)S(1)}, u32[]{:S(2)}, u32[]{:S(2)}) collective-permute-start(bf16[128,1024]{1,0:T(8,128)(2,1)S(1)} %get-tuple-element.18), channel_id=1, source_target_pairs={{0,992},{1,33},{2,994},{3,35},{4,996},{5,37},{6,998},{7,39},{8,100... | collective-permute-start | bytes 786440 | tf_op jit(solution)/shard_map/ppermute | solution.py:200
  134.6 12.8 %collective-permute-start.15 = (bf16[128,1024]{1,0:T(8,128)(2,1)S(1)}, bf16[128,1024]{1,0:T(8,128)(2,1)S(1)}, u32[]{:S(2)}, u32[]{:S(2)}) collective-permute-start(bf16[128,1024]{1,0:T(8,128)(2,1)S(1)} %get-tuple-element.16), channel_id=1, source_target_pairs={{0,64},{1,961},{2,66},{3,963},{4,68},{5,965},{6,70},{7,967},{8,72}... | collective-permute-start | bytes 786440 | tf_op jit(solution)/shard_map/ppermute | solution.py:200
  140.9 9.5 %collective-permute-start.16 = (bf16[128,1024]{1,0:T(8,128)(2,1)S(1)}, bf16[128,1024]{1,0:T(8,128)(2,1)S(1)}, u32[]{:S(2)}, u32[]{:S(2)}) collective-permute-start(bf16[128,1024]{1,0:T(8,128)(2,1)S(1)} %get-tuple-element.17), channel_id=1, source_target_pairs={{0,32},{1,993},{2,34},{3,995},{4,36},{5,997},{6,38},{7,999},{8,40}... | collective-permute-start | bytes 786440 | tf_op jit(solution)/shard_map/ppermute | solution.py:200
  151.8 45.0 %all-to-all-start.2 = ((bf16[8,16,1024]{2,1,0:T(8,128)(2,1)}), bf16[8,16,1024]{2,1,0:T(8,128)(2,1)S(1)}, u32[]{:S(2)}, u32[]{:S(2)}) async-start(bf16[8,16,1024]{2,1,0:T(8,128)(2,1)} %bitcast.6), calls=%async_computation.2 | async-start | bytes 524288 | tf_op jit(solution)/shard_map/all_to_all | solution.py:206

commit v10 on v8

--- a/solution.py
+++ b/solution.py
@@ -76,18 +76,18 @@
         out_ref[:, n] = (total_ref[:, n] + square_part(left_ref, sparse_ref, n)).astype(BF16)
 
 
-def cube_part(where_ref, left_ref, sparse_ref, first, low_ref, high_ref):
+def cube_part(where_ref, left_ref, sparse_ref, first, *out_refs):
     three = jnp.where(where_ref[0] == where_ref[1], 3.0, 0.0).astype(F32)
-    size = low_ref.shape[0]
-    rows = pl.ds(first, 2 * size)
-    for n in tiles(low_ref.shape[1]):
+    size = out_refs[0].shape[0]
+    rows = pl.ds(first, len(out_refs) * size)
+    for n in tiles(out_refs[0].shape[1]):
         product = jnp.dot(left_ref[rows, :], sparse_ref[:, n], preferred_element_type=F32)
         total = three * left_ref[rows, n].astype(F32) - 2.0 * product
-        low_ref[:, n] = total[:size].astype(low_ref.dtype)
-        high_ref[:, n] = total[size:].astype(high_ref.dtype)
-
-
-def first_kernel(rows, where_ref, mine_ref, other_ref, sparse_ref, left_ref, low_ref, high_ref):
+        for i, out_ref in enumerate(out_refs):
+            out_ref[:, n] = total[i * size : (i + 1) * size].astype(out_ref.dtype)
+
+
+def first_kernel(rows, where_ref, mine_ref, other_ref, sparse_ref, left_ref, *sent_refs):
     row, core = where_ref[0], where_ref[1] % 2
     sign = 1 - 2 * core
     piece = left_ref.shape[0] // rows
@@ -98,11 +98,11 @@
         source = pl.ds(pl.multiple_of((target % half) * piece, piece), piece)
         spot = pl.ds(place * piece, piece)
         left_ref[spot, :] = jnp.where(target // half == core, mine_ref[source, :], other_ref[source, :])
-    cube_part(where_ref, left_ref, sparse_ref, 0, low_ref, high_ref)
-
-
-def second_kernel(where_ref, left_ref, sparse_ref, low_ref, high_ref):
-    cube_part(where_ref, left_ref, sparse_ref, 2 * low_ref.shape[0], low_ref, high_ref)
+    cube_part(where_ref, left_ref, sparse_ref, 0, *sent_refs)
+
+
+def second_kernel(where_ref, left_ref, sparse_ref, kept_ref):
+    cube_part(where_ref, left_ref, sparse_ref, left_ref.shape[0] - kept_ref.shape[0], kept_ref)
 
 
 def spread(member, groups):
@@ -188,14 +188,12 @@
 
     quarter = tall((window // 4, cols_here), BF16)
     left, *sent = call(
-        functools.partial(first_kernel, rows), (tall((window, rows_here), BF16), quarter, quarter), work
+        functools.partial(first_kernel, rows), (tall((window, rows_here), BF16), *[quarter] * 3), work
     )(in_specs=[SMEM, VMEM, VMEM, VMEM])(where, mine, other, sparse)
-    last, kept = call(second_kernel, (quarter, tall(quarter.shape, F32)), work)(in_specs=[SMEM, VMEM, VMEM])(
-        where, left, sparse
-    )
+    kept = call(second_kernel, tall(quarter.shape, F32), work)(in_specs=[SMEM, VMEM, VMEM])(where, left, sparse)
     got = [
         lax.ppermute(part, BOTH, pairs([(z, step) for z in range(rows)]))
-        for part, step in zip((*sent, last), STEPS)
+        for part, step in zip(sent, STEPS)
     ]
     ready = call(functools.partial(order_kernel, groups), quarter, 10**6)(in_specs=[SMEM] + [VMEM] * 4)(
         where, kept, *got

time: 198 us -> 199 us (level)
  transfers between devices with their start and end apart: 20 -> 20, of which waited for: 10 -> 11; matrix products, arithmetic and copies ran while one was open for 1% -> 1% of each run, Pallas kernels for 1% -> 1%
where the time goes in v10:
time: 199 us; the launch traced here: 196 us
  starting transfers between devices  109 us (55%)
  waiting for transfers between devices  58.7 us (29%)
  blocking collectives  13.9 us (7%)
  Pallas kernels  8.48 us (4%)
  other arithmetic  3.35 us (2%)
    all_to_all x1, starting transfers between devices, body(): lax.all_to_all(ready.reshape(groups, piece, cols_here), 'row', 0, 0, axis...  24.8 us
    ppermute x6, waiting for transfers between devices, body(): lax.ppermute(h, BOTH, pairs(moves, way))  23.4 us
    ppermute x2, starting transfers between devices, body(): near = h + lax.ppermute(h, BOTH, pairs([(0, far)], way))  22.3 us
    all_to_all x1, waiting for transfers between devices, body(): lax.all_to_all(ready.reshape(groups, piece, cols_here), 'row', 0, 0, axis...  20.6 us
    all_to_all x1, blocking collectives, body(): lax.all_to_all(square, 'col', 0, 0, axis_index_groups=same_core, tiled=True)  13.9 us
    ppermute x3, starting transfers between devices, body(): lax.ppermute(part, BOTH, pairs([(z, step) for z in range(rows)]))  13.6 us
    ppermute x2, starting transfers between devices, body(): back = lax.ppermute(h, BOTH, pairs([(0, -far)], way))  12.4 us
    ppermute x6, starting transfers between devices, body(): lax.ppermute(h, BOTH, pairs(moves, way))  11.9 us
  transfers between devices with their start and end apart: 20, of which 11 were waited for; matrix products, arithmetic and copies ran while one was open for 1% of the time, Pallas kernels for 1%

profile of v10, /device:TPU:6, one launch (start us, length us, event | category | flops | bytes accessed | tf_op | source)
XLA Modules:
  0.0 195.5 jit_solution(18433509590751291647)
XLA Ops:
  0.0 1.3 slice.3.window_ref
  1.3 0.1 pad_add_fusion.where_ref
  1.4 0.9 shard_map.37
  2.3 1.9 collective-permute-start
  4.2 14.3 %collective-permute-start.8 = (bf16[256,1024]{1,0:T(8,128)(2,1)S(1)}, bf16[256,1024]{1,0:T(8,128)(2,1)S(1)}, u32[]{:S(2)}, u32[]{:S(2)}) collective-permute-start(bf16[256,1024]{1,0:T(8,128)(2,1)S(1)} %get-tuple-element.12), channel_id=1, source_target_pairs={{0,256},{1,769},{2,258},{3,771},{4,260},{5,773},{6,262},{7,775},{8... | collective-permute-start | bytes 1572872 | tf_op jit(solution)/shard_map/ppermute | solution.py:173
  18.5 0.0 collective-permute-done
  18.6 8.0 %collective-permute-start.1 = (bf16[256,1024]{1,0:T(8,128)(2,1)S(1)}, bf16[256,1024]{1,0:T(8,128)(2,1)S(1)}, u32[]{:S(2)}, u32[]{:S(2)}) collective-permute-start(bf16[256,1024]{1,0:T(8,128)(2,1)S(1)} %collective-permute-done), channel_id=1, source_target_pairs={{0,768},{1,257},{2,770},{3,259},{4,772},{5,261},{6,774},{7,263},{8... | collective-permute-start | bytes 1572872 | tf_op jit(solution)/shard_map/ppermute | solution.py:173
  26.5 1.3 collective-permute-start.9
  27.9 0.0 collective-permute-done.8
  27.9 0.2 add.64
  28.1 0.7 collective-permute-start.10
  28.8 11.1 %collective-permute-start.2 = (bf16[256,1024]{1,0:T(8,128)(2,1)S(1)}, bf16[256,1024]{1,0:T(8,128)(2,1)S(1)}, u32[]{:S(2)}, u32[]{:S(2)}) collective-permute-start(bf16[256,1024]{1,0:T(8,128)(2,1)S(1)} %collective-permute-done), channel_id=1, source_target_pairs={{0,256},{1,769},{2,258},{3,771},{4,260},{5,773},{6,262},{7,775},{8... | collective-permute-start | bytes 1572872 | tf_op jit(solution)/shard_map/ppermute | solution.py:174
  39.9 0.2 add.58
  40.1 0.7 collective-permute-start.3
  40.8 1.2 shard_map.38.sparse_ref
  42.0 11.6 %collective-permute-start.7 = (bf16[1024,1024]{1,0:T(8,128)(2,1)S(1)}, bf16[1024,1024]{1,0:T(8,128)(2,1)S(1)}, u32[]{:S(2)}, u32[]{:S(2)}) collective-permute-start(bf16[1024,1024]{1,0:T(8,128)(2,1)S(1)} %shard_map.38.sparse_ref), channel_id=1, source_target_pairs={{0,1},{1,0},{2,3},{3,2},{4,5},{5,4},{6,7},{7,6},{8,9},{9,8},{10,11... | collective-permute-start | bytes 6291464 | tf_op jit(solution)/shard_map/ppermute | solution.py:162
  53.5 0.0 collective-permute-done.9
  53.6 0.0 collective-permute-done.10
  53.6 0.1 add_add_fusion
  53.7 1.3 collective-permute-start.11
  55.0 0.0 collective-permute-done.2
  55.0 0.1 add_add_fusion.1
  55.1 1.3 collective-permute-start.4
  56.4 9.4 %collective-permute-done.11 = bf16[256,1024]{1,0:T(8,128)(2,1)S(1)} collective-permute-done((bf16[256,1024]{1,0:T(8,128)(2,1)S(1)}, bf16[256,1024]{1,0:T(8,128)(2,1)S(1)}, u32[]{:S(2)}, u32[]{:S(2)}) %collective-permute-start.11) | collective-permute-done | bytes 524320 | tf_op jit(solution)/shard_map/ppermute | solution.py:178
  65.8 0.2 add.67
  66.0 1.3 collective-permute-start.12
  67.4 0.0 collective-permute-done.4
  67.4 0.2 add.61
  67.6 5.3 %collective-permute-start.5 = (bf16[256,1024]{1,0:T(8,128)(2,1)S(1)}, bf16[256,1024]{1,0:T(8,128)(2,1)S(1)}, u32[]{:S(2)}, u32[]{:S(2)}) collective-permute-start(bf16[256,1024]{1,0:T(8,128)(2,1)S(1)} %add.61), channel_id=1, source_target_pairs={{256,320},{769,705},{258,322},{771,707},{260,324},{773,709},{262,3... | collective-permute-start | bytes 1572872 | tf_op jit(solution)/shard_map/ppermute | solution.py:178
  72.9 1.9 collective-permute-done.12
  74.8 0.2 add.68
  75.0 1.3 collective-permute-start.13
  76.3 3.2 %collective-permute-done.5 = bf16[256,1024]{1,0:T(8,128)(2,1)S(1)} collective-permute-done((bf16[256,1024]{1,0:T(8,128)(2,1)S(1)}, bf16[256,1024]{1,0:T(8,128)(2,1)S(1)}, u32[]{:S(2)}, u32[]{:S(2)}) %collective-permute-start.5) | collective-permute-done | bytes 524320 | tf_op jit(solution)/shard_map/ppermute | solution.py:178
  79.5 0.2 add.62
  79.7 1.3 collective-permute-start.6
  81.1 7.6 %collective-permute-done.13 = bf16[256,1024]{1,0:T(8,128)(2,1)S(1)} collective-permute-done((bf16[256,1024]{1,0:T(8,128)(2,1)S(1)}, bf16[256,1024]{1,0:T(8,128)(2,1)S(1)}, u32[]{:S(2)}, u32[]{:S(2)}) %collective-permute-start.13) | collective-permute-done | bytes 524320 | tf_op jit(solution)/shard_map/ppermute | solution.py:178
  88.6 0.2 add.69.left_ref
  88.8 0.7 shard_map.39.total_ref
  89.6 1.3 collective-permute-done.6
  90.9 0.2 add.63.left_ref
  91.1 0.0 collective-permute-done.7.sparse_ref
  91.1 1.5 shard_map.40
  92.6 7.4 %all-to-all-start = ((bf16[16,16,1024]{2,1,0:T(8,128)(2,1)}), bf16[16,16,1024]{2,1,0:T(8,128)(2,1)S(1)}, u32[]{:S(2)}, u32[]{:S(2)}) async-start(bf16[16,16,1024]{2,1,0:T(8,128)(2,1)} %bitcast.2), calls=%async_computation | async-start | bytes 1048576 | tf_op jit(solution)/shard_map/all_to_all | solution.py:182
  100.0 0.8 convert_bitcast_fusion
  100.9 0.1 broadcast_bitcast_fusion.1
  100.9 8.2 %all-to-all-done = bf16[16,16,1024]{2,1,0:T(8,128)(2,1)S(1)} async-done(((bf16[16,16,1024]{2,1,0:T(8,128)(2,1)}), bf16[16,16,1024]{2,1,0:T(8,128)(2,1)S(1)}, u32[]{:S(2)}, u32[]{:S(2)}) %all-to-all-start) | async-done | bytes 524320 | tf_op jit(solution)/shard_map/all_to_all | solution.py:182
  109.2 0.1 convert_reduce_fusion
  109.3 0.1 broadcast_in_dim.10
  109.3 13.9 %all_to_all.15 = bf16[16,16,1024]{2,1,0:T(8,128)(2,1)S(1)} all-to-all(bf16[16,16,1024]{2,1,0:T(8,128)(2,1)S(1)} %broadcast_in_dim.10), channel_id=1, replica_groups={{0,2,4,6,8,10,12,14,16,18,20,22,24,26,28,30},{1,3,5,7,9,11,13,15,17,19,..., dimensions={0} | all-to-all | bytes 1048576 | tf_op jit(solution)/shard_map/all_to_all | solution.py:186
  123.2 1.9 collective-permute-start.14
  125.1 1.9 collective-permute-done.14.other_ref
  127.0 1.8 shard_map.41
  128.8 6.6 %collective-permute-start.15 = (bf16[128,1024]{1,0:T(8,128)(2,1)S(1)}, bf16[128,1024]{1,0:T(8,128)(2,1)S(1)}, u32[]{:S(2)}, u32[]{:S(2)}) collective-permute-start(bf16[128,1024]{1,0:T(8,128)(2,1)S(1)} %get-tuple-element.14), channel_id=1, source_target_pairs={{0,64},{1,961},{2,66},{3,963},{4,68},{5,965},{6,70},{7,967},{8,72}... | collective-permute-start | bytes 786440 | tf_op jit(solution)/shard_map/ppermute | solution.py:195
  135.3 4.4 %collective-permute-start.16 = (bf16[128,1024]{1,0:T(8,128)(2,1)S(1)}, bf16[128,1024]{1,0:T(8,128)(2,1)S(1)}, u32[]{:S(2)}, u32[]{:S(2)}) collective-permute-start(bf16[128,1024]{1,0:T(8,128)(2,1)S(1)} %get-tuple-element.15), channel_id=1, source_target_pairs={{0,32},{1,993},{2,34},{3,995},{4,36},{5,997},{6,38},{7,999},{8,40}... | collective-permute-start | bytes 786440 | tf_op jit(solution)/shard_map/ppermute | solution.py:195
  139.7 2.7 %collective-permute-start.17 = (bf16[128,1024]{1,0:T(8,128)(2,1)S(1)}, bf16[128,1024]{1,0:T(8,128)(2,1)S(1)}, u32[]{:S(2)}, u32[]{:S(2)}) collective-permute-start(bf16[128,1024]{1,0:T(8,128)(2,1)S(1)} %get-tuple-element.16), channel_id=1, source_target_pairs={{0,992},{1,33},{2,994},{3,35},{4,996},{5,37},{6,998},{7,39},{8,100... | collective-permute-start | bytes 786440 | tf_op jit(solution)/shard_map/ppermute | solution.py:195
  142.4 1.0 shard_map.42.kept_ref
  143.4 0.1 collective-permute-done.15.refs_0_
  143.5 4.1 %collective-permute-done.16.refs_1_ = bf16[128,1024]{1,0:T(8,128)(2,1)S(1)} collective-permute-done((bf16[128,1024]{1,0:T(8,128)(2,1)S(1)}, bf16[128,1024]{1,0:T(8,128)(2,1)S(1)}, u32[]{:S(2)}, u32[]{:S(2)}) %collective-permute-start.16) | collective-permute-done | bytes 262176 | tf_op jit(solution)/shard_map/ppermute | solution.py:195
  147.6 0.5 collective-permute-done.17.refs_2_
  148.1 1.4 shard_map.43
  149.4 24.8 %all-to-all-start.2 = ((bf16[8,16,1024]{2,1,0:T(8,128)(2,1)}), bf16[8,16,1024]{2,1,0:T(8,128)(2,1)S(1)}, u32[]{:S(2)}, u32[]{:S(2)}) async-start(bf16[8,16,1024]{2,1,0:T(8,128)(2,1)} %bitcast.6), calls=%async_computation.2 | async-start | bytes 524288 | tf_op jit(solution)/shard_map/all_to_all | solution.py:201
  174.2 0.1 broadcast_bitcast_fusion
  174.3 20.6 %all-to-all-done.2 = bf16[8,16,1024]{2,1,0:T(8,128)(2,1)S(1)} async-done(((bf16[8,16,1024]{2,1,0:T(8,128)(2,1)}), bf16[8,16,1024]{2,1,0:T(8,128)(2,1)S(1)}, u32[]{:S(2)}, u32[]{:S(2)}) %all-to-all-start.2) | async-done | bytes 262176 | tf_op jit(solution)/shard_map/all_to_all | solution.py:201
  194.9 0.6 multiply_convert_fusion
  (8 shorter events, 0.1 us)
Async XLA Ops:
  0.0 1.4 copy-start.1
  1.4 39.4 %copy-start = (bf16[1024,1024]{1,0:T(8,128)(2,1)S(1)}, bf16[1024,1024]{1,0:T(8,128)(2,1)}, u32[]{:S(2)}) copy-start(bf16[1024,1024]{1,0:T(8,128)(2,1)} %density_ref.1) | copy-start | bytes 6291460
  2.3 16.2 %collective-permute-start = (bf16[256,1024]{1,0:T(8,128)(2,1)S(1)}, bf16[256,1024]{1,0:T(8,128)(2,1)S(1)}, u32[]{:S(2)}, u32[]{:S(2)}) collective-permute-start(bf16[256,1024]{1,0:T(8,128)(2,1)S(1)} %get-tuple-element.11), channel_id=1, source_target_pairs={{0,1},{1,0},{2,3},{3,2},{4,5},{5,4},{6,7},{7,6},{8,9},{9,8},{10,11... | collective-permute-start | bytes 1572872 | tf_op jit(solution)/shard_map/ppermute | solution.py:160
  4.2 23.6 %collective-permute-start.8 = (bf16[256,1024]{1,0:T(8,128)(2,1)S(1)}, bf16[256,1024]{1,0:T(8,128)(2,1)S(1)}, u32[]{:S(2)}, u32[]{:S(2)}) collective-permute-start(bf16[256,1024]{1,0:T(8,128)(2,1)S(1)} %get-tuple-element.12), channel_id=1, source_target_pairs={{0,256},{1,769},{2,258},{3,771},{4,260},{5,773},{6,262},{7,775},{8... | collective-permute-start | bytes 1572872 | tf_op jit(solution)/shard_map/ppermute | solution.py:173
  18.6 21.3 %collective-permute-start.1 = (bf16[256,1024]{1,0:T(8,128)(2,1)S(1)}, bf16[256,1024]{1,0:T(8,128)(2,1)S(1)}, u32[]{:S(2)}, u32[]{:S(2)}) collective-permute-start(bf16[256,1024]{1,0:T(8,128)(2,1)S(1)} %collective-permute-done), channel_id=1, source_target_pairs={{0,768},{1,257},{2,770},{3,259},{4,772},{5,261},{6,774},{7,263},{8... | collective-permute-start | bytes 1572872 | tf_op jit(solution)/shard_map/ppermute | solution.py:173
  26.5 27.0 %collective-permute-start.9 = (bf16[256,1024]{1,0:T(8,128)(2,1)S(1)}, bf16[256,1024]{1,0:T(8,128)(2,1)S(1)}, u32[]{:S(2)}, u32[]{:S(2)}) collective-permute-start(bf16[256,1024]{1,0:T(8,128)(2,1)S(1)} %get-tuple-element.12), channel_id=1, source_target_pairs={{0,768},{1,257},{2,770},{3,259},{4,772},{5,261},{6,774},{7,263},{8... | collective-permute-start | bytes 1572872 | tf_op jit(solution)/shard_map/ppermute | solution.py:174
  28.1 25.5 %collective-permute-start.10 = (bf16[256,1024]{1,0:T(8,128)(2,1)S(1)}, bf16[256,1024]{1,0:T(8,128)(2,1)S(1)}, u32[]{:S(2)}, u32[]{:S(2)}) collective-permute-start(bf16[256,1024]{1,0:T(8,128)(2,1)S(1)} %add.64), channel_id=1, source_target_pairs={{256,512},{769,513},{258,514},{771,515},{260,516},{773,517},{262,5... | collective-permute-start | bytes 1572872 | tf_op jit(solution)/shard_map/ppermute | solution.py:175
  28.8 26.2 %collective-permute-start.2 = (bf16[256,1024]{1,0:T(8,128)(2,1)S(1)}, bf16[256,1024]{1,0:T(8,128)(2,1)S(1)}, u32[]{:S(2)}, u32[]{:S(2)}) collective-permute-start(bf16[256,1024]{1,0:T(8,128)(2,1)S(1)} %collective-permute-done), channel_id=1, source_target_pairs={{0,256},{1,769},{2,258},{3,771},{4,260},{5,773},{6,262},{7,775},{8... | collective-permute-start | bytes 1572872 | tf_op jit(solution)/shard_map/ppermute | solution.py:174
  40.1 14.9 %collective-permute-start.3 = (bf16[256,1024]{1,0:T(8,128)(2,1)S(1)}, bf16[256,1024]{1,0:T(8,128)(2,1)S(1)}, u32[]{:S(2)}, u32[]{:S(2)}) collective-permute-start(bf16[256,1024]{1,0:T(8,128)(2,1)S(1)} %add.58), channel_id=1, source_target_pairs={{768,512},{257,513},{770,514},{259,515},{772,516},{261,517},{774,5... | collective-permute-start | bytes 1572872 | tf_op jit(solution)/shard_map/ppermute | solution.py:175
  42.0 49.1 %collective-permute-start.7 = (bf16[1024,1024]{1,0:T(8,128)(2,1)S(1)}, bf16[1024,1024]{1,0:T(8,128)(2,1)S(1)}, u32[]{:S(2)}, u32[]{:S(2)}) collective-permute-start(bf16[1024,1024]{1,0:T(8,128)(2,1)S(1)} %shard_map.38.sparse_ref), channel_id=1, source_target_pairs={{0,1},{1,0},{2,3},{3,2},{4,5},{5,4},{6,7},{7,6},{8,9},{9,8},{10,11... | collective-permute-start | bytes 6291464 | tf_op jit(solution)/shard_map/ppermute | solution.py:162
  53.7 12.2 %collective-permute-start.11 = (bf16[256,1024]{1,0:T(8,128)(2,1)S(1)}, bf16[256,1024]{1,0:T(8,128)(2,1)S(1)}, u32[]{:S(2)}, u32[]{:S(2)}) collective-permute-start(bf16[256,1024]{1,0:T(8,128)(2,1)S(1)} %add_add_fusion), channel_id=1, source_target_pairs={{768,832},{257,193},{770,834},{259,195},{772,836},{261,197},{774,8... | collective-permute-start | bytes 1572872 | tf_op jit(solution)/shard_map/ppermute | solution.py:178
  55.1 12.3 %collective-permute-start.4 = (bf16[256,1024]{1,0:T(8,128)(2,1)S(1)}, bf16[256,1024]{1,0:T(8,128)(2,1)S(1)}, u32[]{:S(2)}, u32[]{:S(2)}) collective-permute-start(bf16[256,1024]{1,0:T(8,128)(2,1)S(1)} %add_add_fusion.1), channel_id=1, source_target_pairs={{256,192},{769,833},{258,194},{771,835},{260,196},{773,837},{262,1... | collective-permute-start | bytes 1572872 | tf_op jit(solution)/shard_map/ppermute | solution.py:178
  66.0 8.8 %collective-permute-start.12 = (bf16[256,1024]{1,0:T(8,128)(2,1)S(1)}, bf16[256,1024]{1,0:T(8,128)(2,1)S(1)}, u32[]{:S(2)}, u32[]{:S(2)}) collective-permute-start(bf16[256,1024]{1,0:T(8,128)(2,1)S(1)} %add.67), channel_id=1, source_target_pairs={{768,704},{257,321},{770,706},{259,323},{772,708},{261,325},{774,7... | collective-permute-start | bytes 1572872 | tf_op jit(solution)/shard_map/ppermute | solution.py:178
  67.6 12.0 %collective-permute-start.5 = (bf16[256,1024]{1,0:T(8,128)(2,1)S(1)}, bf16[256,1024]{1,0:T(8,128)(2,1)S(1)}, u32[]{:S(2)}, u32[]{:S(2)}) collective-permute-start(bf16[256,1024]{1,0:T(8,128)(2,1)S(1)} %add.61), channel_id=1, source_target_pairs={{256,320},{769,705},{258,322},{771,707},{260,324},{773,709},{262,3... | collective-permute-start | bytes 1572872 | tf_op jit(solution)/shard_map/ppermute | solution.py:178
  75.0 13.6 %collective-permute-start.13 = (bf16[256,1024]{1,0:T(8,128)(2,1)S(1)}, bf16[256,1024]{1,0:T(8,128)(2,1)S(1)}, u32[]{:S(2)}, u32[]{:S(2)}) collective-permute-start(bf16[256,1024]{1,0:T(8,128)(2,1)S(1)} %add.68), channel_id=1, source_target_pairs={{704,736},{321,289},{706,738},{323,291},{708,740},{325,293},{710,7... | collective-permute-start | bytes 1572872 | tf_op jit(solution)/shard_map/ppermute | solution.py:178
  79.7 11.1 %collective-permute-start.6 = (bf16[256,1024]{1,0:T(8,128)(2,1)S(1)}, bf16[256,1024]{1,0:T(8,128)(2,1)S(1)}, u32[]{:S(2)}, u32[]{:S(2)}) collective-permute-start(bf16[256,1024]{1,0:T(8,128)(2,1)S(1)} %add.62), channel_id=1, source_target_pairs={{320,288},{705,737},{322,290},{707,739},{324,292},{709,741},{326,2... | collective-permute-start | bytes 1572872 | tf_op jit(solution)/shard_map/ppermute | solution.py:178
  92.6 16.5 %all-to-all-start = ((bf16[16,16,1024]{2,1,0:T(8,128)(2,1)}), bf16[16,16,1024]{2,1,0:T(8,128)(2,1)S(1)}, u32[]{:S(2)}, u32[]{:S(2)}) async-start(bf16[16,16,1024]{2,1,0:T(8,128)(2,1)} %bitcast.2), calls=%async_computation | async-start | bytes 1048576 | tf_op jit(solution)/shard_map/all_to_all | solution.py:182
  123.2 3.8 %collective-permute-start.14 = (bf16[256,1024]{1,0:T(8,128)(2,1)S(1)}, bf16[256,1024]{1,0:T(8,128)(2,1)S(1)}, u32[]{:S(2)}, u32[]{:S(2)}) collective-permute-start(bf16[256,1024]{1,0:T(8,128)(2,1)S(1)} %bitcast.13), channel_id=1, source_target_pairs={{0,1},{1,0},{2,3},{3,2},{4,5},{5,4},{6,7},{7,6},{8,9},{9,8},{10,11... | collective-permute-start | bytes 1572872 | tf_op jit(solution)/shard_map/ppermute | solution.py:187
  128.8 14.7 %collective-permute-start.15 = (bf16[128,1024]{1,0:T(8,128)(2,1)S(1)}, bf16[128,1024]{1,0:T(8,128)(2,1)S(1)}, u32[]{:S(2)}, u32[]{:S(2)}) collective-permute-start(bf16[128,1024]{1,0:T(8,128)(2,1)S(1)} %get-tuple-element.14), channel_id=1, source_target_pairs={{0,64},{1,961},{2,66},{3,963},{4,68},{5,965},{6,70},{7,967},{8,72}... | collective-permute-start | bytes 786440 | tf_op jit(solution)/shard_map/ppermute | solution.py:195
  135.3 12.3 %collective-permute-start.16 = (bf16[128,1024]{1,0:T(8,128)(2,1)S(1)}, bf16[128,1024]{1,0:T(8,128)(2,1)S(1)}, u32[]{:S(2)}, u32[]{:S(2)}) collective-permute-start(bf16[128,1024]{1,0:T(8,128)(2,1)S(1)} %get-tuple-element.15), channel_id=1, source_target_pairs={{0,32},{1,993},{2,34},{3,995},{4,36},{5,997},{6,38},{7,999},{8,40}... | collective-permute-start | bytes 786440 | tf_op jit(solution)/shard_map/ppermute | solution.py:195
  139.7 8.4 %collective-permute-start.17 = (bf16[128,1024]{1,0:T(8,128)(2,1)S(1)}, bf16[128,1024]{1,0:T(8,128)(2,1)S(1)}, u32[]{:S(2)}, u32[]{:S(2)}) collective-permute-start(bf16[128,1024]{1,0:T(8,128)(2,1)S(1)} %get-tuple-element.16), channel_id=1, source_target_pairs={{0,992},{1,33},{2,994},{3,35},{4,996},{5,37},{6,998},{7,39},{8,100... | collective-permute-start | bytes 786440 | tf_op jit(solution)/shard_map/ppermute | solution.py:195
  149.4 45.4 %all-to-all-start.2 = ((bf16[8,16,1024]{2,1,0:T(8,128)(2,1)}), bf16[8,16,1024]{2,1,0:T(8,128)(2,1)S(1)}, u32[]{:S(2)}, u32[]{:S(2)}) async-start(bf16[8,16,1024]{2,1,0:T(8,128)(2,1)} %bitcast.6), calls=%async_computation.2 | async-start | bytes 524288 | tf_op jit(solution)/shard_map/all_to_all | solution.py:201
